TPU v7x, 32 devices: a whole 2x2x4 slice. The times are simulated.
32 devices in a mesh: cen: 16 (over z, y, core), out: 2 (over x).
Axes of the slice: x: 2, y: 2, z: 4, core: 2. Of those that a mesh axis runs over, the one named last changes fastest.
Arguments:
- features: float32 [32768, 1024], P('cen', 'out'), may hold values from -6 to 6
- centres: float32 [32768, 1024], P('cen', 'out'), may hold values from -6 to 6
- coefs: float32 [32768, 1000], P('cen', 'out'), may hold values from -0.0625 to 0.0625
- batch_index: int32 [2, 256], P(None, 'cen'), may hold values from 0 to 2047
- targets: float32 [2, 256, 1000], P(None, 'cen', 'out'), may hold values from -6 to 6
Outputs:
- residuals: float32 [2, 256, 1000], P(None, 'cen', 'out')
- new_coefs: float32 [32768, 1000], P('cen', 'out')
All inputs are finite; a program needn't handle non-finite values.
Results may differ from a plain program's by a relative error of at most 0.0001.
Values sent between devices are 32-bit elements; how exact they have to be, the bound alone decides.
No kernel may reach another device: no remote copies, remote signals or barrier semaphores. Data moves between devices by JAX's collectives and lax.ppermute only.
A program may use at most 64 MiB of HBM per device.

v0:
```python
import math

import jax
import jax.numpy as jnp
from jax import lax
from jax.sharding import PartitionSpec as P

W = 1024


def inner_rows(left, right):
    return lax.dot_general(
        left,
        right,
        (((1,), (1,)), ((), ())),
        precision=lax.Precision.HIGHEST,
        preferred_element_type=jnp.float32,
    )


def partial_squares(batch, centres, centre_sq):
    batch_sq = jnp.sum(batch * batch, axis=1)
    return batch_sq[:, None] + centre_sq[None, :] - 2.0 * inner_rows(batch, centres)


def laplace(squared):
    return jnp.exp(-jnp.sqrt(jnp.maximum(squared, 0.0)) / (0.5 * math.sqrt(W)))


def body(features, centres, coefs, batch_index, targets):
    local_rows = batch_index.shape[1]
    batch_total = local_rows * lax.axis_size("cen")
    entries = centres.shape[0] * lax.axis_size("cen") * coefs.shape[1] * lax.axis_size("out")
    centre_sq = jnp.sum(centres * centres, axis=1)
    results = []
    grads = []
    sums = []
    for step in range(2):
        picked = jnp.take(features, batch_index[step], axis=0)
        batch = lax.all_gather(picked, "cen", axis=0, tiled=True)
        share = lax.psum_scatter(
            partial_squares(batch, centres, centre_sq), "out", scatter_dimension=1, tiled=True
        )
        kern = lax.all_gather(laplace(share), "out", axis=1, tiled=True)
        predicted = lax.psum_scatter(
            jnp.dot(
                kern, coefs, precision=lax.Precision.HIGHEST, preferred_element_type=jnp.float32
            ),
            "cen",
            scatter_dimension=0,
            tiled=True,
        )
        resid = predicted - targets[step]
        results.append(resid)
        all_resid = lax.all_gather(resid, "cen", axis=0, tiled=True)
        grad = (
            lax.dot_general(
                kern,
                all_resid,
                (((0,), (0,)), ((), ())),
                precision=lax.Precision.HIGHEST,
                preferred_element_type=jnp.float32,
            )
            / batch_total
        )
        grads.append(grad)
        sums.append(lax.psum(jnp.sum(grad * grad), ("cen", "out")))
    new_coefs = coefs
    for step in range(2):
        scale = jnp.sqrt(sums[step] / entries + 1e-06)
        new_coefs = new_coefs - 0.1 * grads[step] / scale
    return (jnp.stack(results), new_coefs)


def solution(mesh):
    placed = (
        P("cen", "out"),
        P("cen", "out"),
        P("cen", "out"),
        P(None, "cen"),
        P(None, "cen", "out"),
    )
    return jax.shard_map(
        body,
        mesh=mesh,
        in_specs=placed,
        out_specs=(P(None, "cen", "out"), P("cen", "out")),
        check_vma=False,
    )
```

profile of v0, /device:TPU:0, one launch (start us, length us, event | category | flops | bytes accessed | tf_op | source)
XLA Modules:
  0.0 406.2 jit_solution(436184824486440202)
XLA Ops:
  7.2 0.0 reduce-scatter.9.cloned.1.call-start
  7.2 0.8 compare_and_fusion.1
  8.0 2.5 multiply_reduce_fusion
  10.5 2.8 gather_fusion.1
  13.3 0.1 broadcast_select_fusion
  13.4 24.6 %all_gather.20 = f32[256,512]{1,0:T(8,128)S(1)} all-gather(f32[16,512]{1,0:T(8,128)S(1)} %broadcast_select_fusion), channel_id=1, replica_groups=mesh['cen'=16,'out'=2] {'cen'}, dimensions={0}, use_global_device_ids=true | all-gather | bytes 557056 | tf_op jit(solution)/shard_map/all_gather | solution.py:40
  37.9 0.1 multiply_reduce_fusion.3
  38.1 7.2 %fusion = f32[256,2048]{1,0:T(8,128)} fusion(f32[256,512]{1,0:T(8,128)S(1)} %all_gather.20, f32[2048,512]{1,0:T(8,128)} %param.8, f32[256]{0:T(256)S(1)} %multiply_reduce_fusion.3, f32[2048]{0:T(1024)S(1)} %multiply_reduce_fusion), kind=kOutput, calls=%fused_computation.7 | convolution fusion | flops 3222798336 | bytes 6824960 | tf_op jit(solution)/shard_map/dot_general | solution.py:12
  45.3 0.0 reduce-scatter.9.cloned.1.call-update
  45.3 0.0 reduce-scatter.5.cloned.1.call-start
  45.4 2.8 gather_fusion
  48.1 0.1 broadcast_select_fusion.1
  48.2 18.9 %all_gather.18 = f32[256,512]{1,0:T(8,128)S(1)} all-gather(f32[16,512]{1,0:T(8,128)S(1)} %broadcast_select_fusion.1), channel_id=1, replica_groups=mesh['cen'=16,'out'=2] {'cen'}, dimensions={0}, use_global_device_ids=true | all-gather | bytes 557056 | tf_op jit(solution)/shard_map/all_gather | solution.py:40
  67.1 0.1 multiply_reduce_fusion.4
  67.2 7.2 %fusion.1 = f32[256,2048]{1,0:T(8,128)} fusion(f32[256,512]{1,0:T(8,128)S(1)} %all_gather.18, f32[2048,512]{1,0:T(8,128)} %param.8, f32[2048]{0:T(1024)S(1)} %multiply_reduce_fusion, f32[256]{0:T(256)S(1)} %multiply_reduce_fusion.4), kind=kOutput, calls=%fused_computation.9 | convolution fusion | flops 3222798336 | bytes 6824960 | tf_op jit(solution)/shard_map/dot_general | solution.py:12
  74.4 0.0 reduce-scatter.5.cloned.1.call-update
  74.4 0.0 all-gather.5.cloned.1.call-start
  74.5 0.1 reduce-scatter.9.cloned.1.call-done
  74.5 2.6 multiply_exponential_fusion
  77.1 0.0 all-gather.5.cloned.1.call-update
  77.2 0.0 all-gather.3.cloned.1.call-start
  77.2 32.1 %reduce-scatter.5.cloned.1.call-done = f32[256,1024]{1,0:T(8,128)} async-done(((f32[256,2048]{1,0:T(8,128)}), f32[256,1024]{1,0:T(8,128)}) %reduce-scatter.5.cloned.1.call-update) | async-done | bytes 1048592 | tf_op jit(solution)/shard_map/reduce_scatter | solution.py:41
  109.3 2.6 multiply_exponential_fusion.1
  111.9 0.0 all-gather.3.cloned.1.call-update
  111.9 0.2 reduce-scatter.11.cloned.1.call-start
  112.2 31.9 %all-gather.5.cloned.1.call-done = f32[256,2048]{1,0:T(8,128)} async-done(((f32[256,1024]{1,0:T(8,128)}), f32[256,2048]{1,0:T(8,128)}) %all-gather.5.cloned.1.call-update) | async-done | bytes 2097168 | tf_op jit(solution)/shard_map/all_gather | solution.py:44
  144.0 7.3 %fusion.3 = f32[256,500]{1,0:T(8,128)} fusion(f32[256,2048]{1,0:T(8,128)} %all-gather.5.cloned.1.call-done, f32[2048,500]{0,1:T(8,128)} %param.9), kind=kOutput, calls=%fused_computation.26 | convolution fusion | flops 3145728000 | bytes 6705152 | tf_op jit(solution)/shard_map/dot_general | solution.py:46
  151.3 0.0 copy-start.2
  151.3 0.0 reduce-scatter.11.cloned.1.call-update
  151.3 0.0 copy-start
  151.4 0.0 reduce-scatter.7.cloned.1.call-start
  151.4 27.8 %all-gather.3.cloned.1.call-done = f32[256,2048]{1,0:T(8,128)} async-done(((f32[256,1024]{1,0:T(8,128)}), f32[256,2048]{1,0:T(8,128)}) %all-gather.3.cloned.1.call-update) | async-done | bytes 2097168 | tf_op jit(solution)/shard_map/all_gather | solution.py:44
  179.2 7.3 %fusion.2 = f32[256,500]{1,0:T(8,128)} fusion(f32[256,2048]{1,0:T(8,128)} %all-gather.3.cloned.1.call-done, f32[2048,500]{0,1:T(8,128)} %param.9), kind=kOutput, calls=%fused_computation.25 | convolution fusion | flops 3145728000 | bytes 6705152 | tf_op jit(solution)/shard_map/dot_general | solution.py:46
  186.4 0.0 reduce-scatter.7.cloned.1.call-update
  186.5 51.9 %reduce-scatter.11.cloned.1.call-done = f32[16,500]{1,0:T(8,128)} async-done(((f32[256,500]{1,0:T(8,128)}), f32[16,500]{1,0:T(8,128)}) %reduce-scatter.11.cloned.1.call-update) | async-done | bytes 32016 | tf_op jit(solution)/shard_map/reduce_scatter | solution.py:45
  238.4 59.2 %reduce-scatter.7.cloned.1.call-done = f32[16,500]{1,0:T(8,128)} async-done(((f32[256,500]{1,0:T(8,128)}), f32[16,500]{1,0:T(8,128)}) %reduce-scatter.7.cloned.1.call-update) | async-done | bytes 32016 | tf_op jit(solution)/shard_map/reduce_scatter | solution.py:45
  297.6 0.0 copy-done.2
  297.6 0.0 copy-start.1
  297.6 0.9 bitcast_subtract_fusion.1
  298.6 20.9 %all_gather.22 = f32[256,500]{1,0:T(8,128)S(1)} all-gather(f32[16,500]{1,0:T(8,128)S(1)} %get-tuple-element.9), channel_id=1, replica_groups=mesh['cen'=16,'out'=2] {'cen'}, dimensions={0}, use_global_device_ids=true | all-gather | bytes 544000 | tf_op jit(solution)/shard_map/all_gather | solution.py:55
  319.4 19.1 %all_gather.23 = f32[256,500]{1,0:T(8,128)S(1)} all-gather(f32[16,500]{1,0:T(8,128)S(1)} %get-tuple-element.10), channel_id=1, replica_groups=mesh['cen'=16,'out'=2] {'cen'}, dimensions={0}, use_global_device_ids=true | all-gather | bytes 544000 | tf_op jit(solution)/shard_map/all_gather | solution.py:55
  338.5 0.0 copy-done
  338.5 6.0 %multiply_reduce_fusion.1 = (f32[]{:T(128)}, f32[2048,500]{0,1:T(8,128)}) fusion(f32[256,2048]{1,0:T(8,128)S(1)} %copy-done, f32[256,500]{1,0:T(8,128)S(1)} %all_gather.23), kind=kOutput, calls=%fused_computation.4 | convolution fusion | flops 3148800000 | bytes 6705156 | tf_op jit(solution)/shard_map/dot_general | solution.py:57
  344.5 0.0 copy-done.1
  344.5 6.1 %multiply_reduce_fusion.2 = (f32[]{:T(128)}, f32[2048,500]{0,1:T(8,128)}) fusion(f32[256,2048]{1,0:T(8,128)S(1)} %copy-done.1, f32[256,500]{1,0:T(8,128)S(1)} %all_gather.22), kind=kOutput, calls=%fused_computation.5 | convolution fusion | flops 3148800000 | bytes 6705156 | tf_op jit(solution)/shard_map/dot_general | solution.py:57
  350.6 38.2 %all-reduce = (f32[]{:T(128)}, f32[]{:T(128)}) all-reduce(f32[]{:T(128)} %get-tuple-element.13, f32[]{:T(128)} %get-tuple-element.15), channel_id=1, replica_groups=mesh['cen'=16,'out'=2] {'cen','out'}, use_global_device_ids=true, to_apply=%region_10.12 | all-reduce | flops 2 | bytes 16 | tf_op jit(solution)/shard_map/psum | solution.py:67
  390.2 0.6 pad_maximum_fusion
  390.9 8.4 %divide_subtract_fusion = f32[2048,500]{0,1:T(8,128)} fusion(f32[2048,500]{0,1:T(8,128)} %get-tuple-element.14, f32[2048,500]{0,1:T(8,128)} %param.9, f32[2048,500]{0,1:T(8,128)} %get-tuple-element.16, f32[]{:T(128)S(6)} %sqrt.15, f32[]{:T(128)S(6)} %sqrt.14), kind=kLoop, calls=%fused_computation.3 | loop fusion | flops 6144000 | bytes 16384008 | tf_op jit(solution)/shard_map/sub | solution.py:71
  (2 shorter events, 0.0 us)
Async XLA Ops:
  7.2 67.4 %reduce-scatter.9.cloned.1.call-start = ((), (), s32[]{:S(2)}) async-start(), calls=%async_computation.7 | async-start | bytes 3145728 | tf_op jit(solution)/shard_map/reduce_scatter | solution.py:41
  45.3 64.0 %reduce-scatter.5.cloned.1.call-start = ((), (), s32[]{:S(2)}) async-start(), calls=%async_computation.4 | async-start | bytes 3145728 | tf_op jit(solution)/shard_map/reduce_scatter | solution.py:41
  74.4 69.6 %all-gather.5.cloned.1.call-start = ((), (), s32[]{:S(2)}) async-start(), calls=%async_computation.8 | async-start | bytes 3145728 | tf_op jit(solution)/shard_map/all_gather | solution.py:44
  77.2 102.0 %all-gather.3.cloned.1.call-start = ((), (), s32[]{:S(2)}) async-start(), calls=%async_computation.5 | async-start | bytes 3145728 | tf_op jit(solution)/shard_map/all_gather | solution.py:44
  111.9 126.4 %reduce-scatter.11.cloned.1.call-start = ((), (), s32[]{:S(2)}) async-start(), calls=%async_computation.9 | async-start | bytes 557056 | tf_op jit(solution)/shard_map/reduce_scatter | solution.py:45
  151.3 146.3 %copy-start.2 = (f32[2,16,500]{2,1,0:T(8,128)S(1)}, f32[2,16,500]{2,1,0:T(8,128)}, u32[]{:S(2)}) copy-start(f32[2,16,500]{2,1,0:T(8,128)} %param.11) | copy-start | bytes 192004
  151.3 187.2 %copy-start = (f32[256,2048]{1,0:T(8,128)S(1)}, f32[256,2048]{1,0:T(8,128)}, u32[]{:S(2)}) copy-start(f32[256,2048]{1,0:T(8,128)} %all-gather.5.cloned.1.call-done) | copy-start | bytes 6291460
  151.4 146.3 %reduce-scatter.7.cloned.1.call-start = ((), (), s32[]{:S(2)}) async-start(), calls=%async_computation.6 | async-start | bytes 557056 | tf_op jit(solution)/shard_map/reduce_scatter | solution.py:45
  297.6 46.9 %copy-start.1 = (f32[256,2048]{1,0:T(8,128)S(1)}, f32[256,2048]{1,0:T(8,128)}, u32[]{:S(2)}) copy-start(f32[256,2048]{1,0:T(8,128)} %all-gather.3.cloned.1.call-done) | copy-start | bytes 6291460
Sparse Core Ops, SparseCore 0:
  45.4 29.0 reduce-scatter.8
  77.5 31.8 reduce-scatter.4
  110.9 33.1 all-gather.4
  146.0 33.1 all-gather.2
  182.6 55.7 reduce-scatter.10
  242.8 54.8 reduce-scatter.6
where the time goes:
time: 408 us; the launch traced here: 406 us
  waiting for transfers between devices  203 us (50%)
  blocking collectives  122 us (30%)
  matrix products  41 us (10%)
  other arithmetic  18.9 us (5%)
  between operations  15.6 us (4%)
  local copies, waits for them, and re-layouts  5.57 us (1%)
    reduce_scatter x2, waiting for transfers between devices, body(): lax.psum_scatter(jnp.dot(kern, coefs, precision=lax.Precision.HIGHEST, pr...  111 us
    all_gather x2, waiting for transfers between devices, body(): kern = lax.all_gather(laplace(share), 'out', axis=1, tiled=True)  59.6 us
    all_gather x2, blocking collectives, body(): batch = lax.all_gather(picked, 'cen', axis=0, tiled=True)  43.4 us
    all_gather x2, blocking collectives, body(): all_resid = lax.all_gather(resid, 'cen', axis=0, tiled=True)  39.9 us
    psum x1, blocking collectives, body(): sums.append(lax.psum(jnp.sum(grad * grad), ('cen', 'out')))  38.2 us
    reduce_scatter x2, waiting for transfers between devices, body(): lax.psum_scatter(partial_squares(batch, centres, centre_sq), 'out', scatt...  32.2 us
    dot_general x2, matrix products, body(): jnp.dot(kern, coefs, precision=lax.Precision.HIGHEST, preferred_element_t...  14.6 us
    dot_general x2, matrix products, inner_rows(): lax.dot_general(left, right, (((1,), (1,)), ((), ())), precision=lax.Prec...  14.4 us
  transfers between devices with their start and end apart: 6, of which 6 were waited for; matrix products, arithmetic and copies ran while one was open for 7% of the time, Pallas kernels for 0%

commit v1 on v0

v1 whole, which is shorter than its diff:
```python
import math

import jax
import jax.numpy as jnp
from jax import lax
from jax.sharding import PartitionSpec as P

SHARE = 4


def product(left, right, dims, precision):
    return lax.dot_general(
        left,
        right,
        (dims, ((), ())),
        precision=precision,
        preferred_element_type=jnp.float32,
    )


def partial_squares(batch, centres):
    batch_sq = jnp.sum(batch * batch, axis=1)
    centre_sq = jnp.sum(centres * centres, axis=1)
    inner = product(batch, centres, ((1,), (1,)), lax.Precision.HIGHEST)
    return batch_sq[:, None] + centre_sq[None, :] - 2.0 * inner


def laplace(squared, width):
    return jnp.exp(-jnp.sqrt(jnp.maximum(squared, 0.0)) / (0.5 * math.sqrt(width)))


def swap(x, bit):
    n = lax.axis_size("cen")
    return lax.ppermute(x, "cen", [(i, i ^ bit) for i in range(n)])


def others(x):
    n = lax.axis_size("out")
    return [lax.ppermute(x, "out", [(i, (i + s) % n) for i in range(n)]) for s in range(1, n)]


def sum_out(x):
    if lax.axis_size("out") > 2:
        return lax.psum(x, "out")
    for part in others(x):
        x = x + part
    return x


def bits():
    n = lax.axis_size("cen")
    return [1 << b for b in range(n.bit_length() - 1)]


def gather(x):
    rest = x.shape
    for bit in reversed(bits()):
        x = jnp.stack([x, swap(x, bit)])
    return x.reshape((-1,) + rest[1:])


def scatter_sum(x):
    n = lax.axis_size("cen")
    x = x.reshape((n, -1) + x.shape[1:])
    for bit in bits():
        half = x.shape[0] // 2
        halves = x.reshape((2, half) + x.shape[1:])
        x = halves[0] + swap(halves[1], bit)
    return x[0]


def total(x):
    for part in others(x):
        x = x + part
    for bit in bits():
        x = x + swap(x, bit)
    return x


def body(features, centres, coefs, batch_index, targets):
    local_rows = batch_index.shape[1]
    batch_total = local_rows * lax.axis_size("cen")
    width = features.shape[1] * lax.axis_size("out")
    entries = centres.shape[0] * lax.axis_size("cen") * coefs.shape[1] * lax.axis_size("out")
    pair = lax.axis_size("out") <= 2
    sent = centres.shape[0] // SHARE if pair else 0
    early, late = centres[:sent], centres[sent:]

    picked = [jnp.take(features, batch_index[step], axis=0) for step in range(2)]
    own = [gather(picked[step]) for step in range(2)]
    if pair:
        far_centres = others(early)
        far_rows = [gather(rows) for rows in others(jnp.concatenate(picked))]

    kerns = []
    for step in range(2):
        late_sq = sum_out(partial_squares(own[step], late))
        if not pair:
            kerns.append(laplace(late_sq, width))
            continue
        early_sq = partial_squares(own[step], early)
        for rows, far in zip(far_rows, far_centres):
            rows = rows.reshape((-1, 2, local_rows, rows.shape[1]))[:, step]
            early_sq = early_sq + partial_squares(rows.reshape((-1, rows.shape[-1])), far)
        kerns.append(jnp.concatenate([laplace(early_sq, width), laplace(late_sq, width)], axis=1))

    results = []
    new_coefs = coefs
    for step in range(2):
        predicted = product(kerns[step], coefs, ((1,), (0,)), lax.Precision.HIGH)
        resid = scatter_sum(predicted) - targets[step]
        results.append(resid)
        grad = product(kerns[step], gather(resid), ((0,), (0,)), lax.Precision.HIGH) / batch_total
        scale = jnp.sqrt(total(jnp.sum(grad * grad)) / entries + 1e-06)
        new_coefs = new_coefs - 0.1 * grad / scale
    return (jnp.stack(results), new_coefs)


def solution(mesh):
    placed = (
        P("cen", "out"),
        P("cen", "out"),
        P("cen", "out"),
        P(None, "cen"),
        P(None, "cen", "out"),
    )
    return jax.shard_map(
        body,
        mesh=mesh,
        in_specs=placed,
        out_specs=(P(None, "cen", "out"), P("cen", "out")),
        check_vma=False,
    )
```

time: 408 us -> 216 us (0.53)
  waiting for transfers between devices: 203 us -> 75.8 us
  blocking collectives: 122 us -> 0 us
  starting transfers between devices: 0.43 us -> 58.5 us
  local copies, waits for them, and re-layouts: 5.57 us -> 13.4 us
  matrix products: 41 us -> 33.9 us
  between operations: 15.6 us -> 8.92 us
  other arithmetic: 18.9 us -> 24.3 us
    reduce_scatter x4 -> x0, waiting for transfers between devices: 143 us -> none  [the longest x2 111 us: body(): lax.psum_scatter(jnp.dot(kern, coefs, precision=lax.Precision.HIGHEST, pr...]
    all_gather x4 -> x0, blocking collectives: 83.4 us -> none  [the longest x2 43.4 us: body(): batch = lax.all_gather(picked, 'cen', axis=0, tiled=True)]
    ppermute x0 -> x42, waiting for transfers between devices: none -> 75.8 us  [the longest x6 47.7 us: others(): lax.ppermute(x, 'out', [(i, (i + s) % n) for i in range(n)])]
    all_gather x2 -> x0, waiting for transfers between devices: 59.6 us -> none  [body(): kern = lax.all_gather(laplace(share), 'out', axis=1, tiled=True)]
    ppermute x0 -> x42, starting transfers between devices: none -> 58.5 us  [the longest x36 52.4 us: swap(): return lax.ppermute(x, 'cen', [(i, i ^ bit) for i in range(n)])]
    psum x1 -> x0, blocking collectives: 38.2 us -> none  [body(): sums.append(lax.psum(jnp.sum(grad * grad), ('cen', 'out')))]
    dot_general x6 -> x10, matrix products: 41 us -> 33.9 us  [product(): lax.dot_general(left, right, (dims, ((), ())), precision=precision, prefe...]
    slice x0 -> x12, local copies, waits for them, and re-layouts: none -> 6.8 us  [scatter_sum(): x = halves[0] + swap(halves[1], bit)]
  transfers between devices with their start and end apart: 6 -> 42, of which waited for: 6 -> 19; matrix products, arithmetic and copies ran while one was open for 7% -> 27% of each run, Pallas kernels for 0% -> 0%
where the time goes in v1:
time: 216 us; the launch traced here: 215 us
  waiting for transfers between devices  75.8 us (35%)
  starting transfers between devices  58.5 us (27%)
  matrix products  33.9 us (16%)
  other arithmetic  24.3 us (11%)
  local copies, waits for them, and re-layouts  13.4 us (6%)
  between operations  8.92 us (4%)
    ppermute x36, starting transfers between devices, swap(): return lax.ppermute(x, 'cen', [(i, i ^ bit) for i in range(n)])  52.4 us
    ppermute x6, waiting for transfers between devices, others(): lax.ppermute(x, 'out', [(i, (i + s) % n) for i in range(n)])  47.7 us
    dot_general x10, matrix products, product(): lax.dot_general(left, right, (dims, ((), ())), precision=precision, prefe...  33.9 us
    ppermute x36, waiting for transfers between devices, swap(): return lax.ppermute(x, 'cen', [(i, i ^ bit) for i in range(n)])  28.1 us
    sub x1, other arithmetic, body(): new_coefs = new_coefs - 0.1 * grad / scale  8.45 us
    slice x12, local copies, waits for them, and re-layouts, scatter_sum(): x = halves[0] + swap(halves[1], bit)  6.8 us
    ppermute x6, starting transfers between devices, others(): lax.ppermute(x, 'out', [(i, (i + s) % n) for i in range(n)])  6.14 us
    gather x2, local copies, waits for them, and re-layouts, body(): jnp.take(features, batch_index[step], axis=0)  5.55 us
  transfers between devices with their start and end apart: 42, of which 19 were waited for; matrix products, arithmetic and copies ran while one was open for 27% of the time, Pallas kernels for 0%

profile of v1, /device:TPU:0, one launch (start us, length us, event | category | flops | bytes accessed | tf_op | source)
XLA Modules:
  0.0 214.9 jit_solution(11432020761424161220)
XLA Ops:
  1.4 2.8 %gather_fusion = f32[16,512]{1,0:T(8,128)S(1)} fusion(f32[2048,512]{1,0:T(8,128)} %param.7, s32[1024]{0:T(1024)S(1)} %pad_clamp_fusion.1), kind=kCustom, calls=%fused_computation.clone | custom fusion | bytes 65600 | tf_op jit(solution)/shard_map/jit(_take)/gather | solution.py:89
  4.3 4.0 %collective-permute-start = (f32[16,512]{1,0:T(8,128)S(1)}, f32[16,512]{1,0:T(8,128)S(1)}, u32[]{:S(2)}, u32[]{:S(2)}) collective-permute-start(f32[16,512]{1,0:T(8,128)S(1)} %broadcast_select_fusion.1), channel_id=1, source_target_pairs={{0,16},{2,18},{4,20},{6,22},{8,24},{10,26},{12,28},{14,30},{16,0},... | collective-permute-start | bytes 98312 | tf_op jit(solution)/shard_map/ppermute | solution.py:34
  8.3 2.8 %gather_fusion.1 = f32[16,512]{1,0:T(8,128)S(1)} fusion(f32[2048,512]{1,0:T(8,128)} %param.7, s32[1024]{0:T(1024)S(1)} %pad_clamp_fusion), kind=kCustom, calls=%fused_computation.1.clone | custom fusion | bytes 65600 | tf_op jit(solution)/shard_map/jit(_take)/gather | solution.py:89
  11.2 1.8 collective-permute-start.4
  13.0 2.5 %multiply_reduce_fusion.4 = (f32[512]{0:T(512)S(1)}, f32[512,512]{1,0:T(8,128)}) fusion(f32[2048,512]{1,0:T(8,128)} %param.8), kind=kLoop, calls=%fused_computation.40 | loop fusion | flops 523776 | bytes 2099200 | tf_op jit(solution)/shard_map/reduce_sum | solution.py:23
  16.0 1.8 collective-permute-start.16
  18.2 2.8 %collective-permute-start.5 = (f32[32,512]{1,0:T(8,128)S(1)}, f32[32,512]{1,0:T(8,128)S(1)}, u32[]{:S(2)}, u32[]{:S(2)}) collective-permute-start(f32[32,512]{1,0:T(8,128)S(1)} %collective-permute-done.4), channel_id=1, source_target_pairs={{0,16},{2,18},{4,20},{6,22},{8,24},{10,26},{12,28},{14,30},{16,0},... | collective-permute-start | bytes 196616 | tf_op jit(solution)/shard_map/ppermute | solution.py:34
  21.1 1.7 collective-permute-start.17
  23.5 2.0 collective-permute-start.6
  25.6 1.6 collective-permute-start.2
  27.3 1.2 collective-permute-done.6
  28.6 1.7 collective-permute-start.7
  31.0 5.2 %collective-permute-done.7 = f32[2,2,32,512]{3,2,1,0:T(8,128)S(1)} collective-permute-done((f32[2,2,32,512]{3,2,1,0:T(8,128)S(1)}, f32[2,2,32,512]{3,2,1,0:T(8,128)S(1)}, u32[]{:S(2)}, u32[]{:S(2)}) %collective-permute-start.7) | collective-permute-done | bytes 262176 | tf_op jit(solution)/shard_map/ppermute | solution.py:34
  36.9 1.1 fusion.42
  38.1 5.8 %fusion.1 = f32[256,1536]{1,0:T(8,128)} fusion(f32[256,512]{1,0:T(8,128)S(1)} %bitcast.86, f32[2048,512]{1,0:T(8,128)} %param.8, f32[256]{0:T(256)S(1)} %add.172, f32[1536]{0:T(1024)S(1)} %multiply_reduce_fusion.2), kind=kOutput, calls=%fused_computation.9 | convolution fusion | flops 2417098752 | bytes 5250048 | tf_op jit(solution)/shard_map/dot_general | solution.py:12
  43.9 1.1 multiply_reduce_fusion.8
  45.1 1.5 collective-permute-start.19
  46.6 5.9 %fusion = f32[256,1536]{1,0:T(8,128)} fusion(f32[256,512]{1,0:T(8,128)S(1)} %bitcast.88, f32[2048,512]{1,0:T(8,128)} %param.8, f32[1536]{0:T(1024)S(1)} %multiply_reduce_fusion.2, f32[256]{0:T(256)S(1)} %add.155), kind=kOutput, calls=%fused_computation.8 | convolution fusion | flops 2417098752 | bytes 5250048 | tf_op jit(solution)/shard_map/dot_general | solution.py:12
  53.0 1.1 pad_maximum_fusion.6
  54.5 1.1 convolution_multiply_fusion.2
  55.6 3.3 %fusion.15 = f32[256,512]{1,0:T(8,128)} fusion(f32[256,512]{1,0:T(8,128)S(1)} %bitcast.87, f32[256,512]{1,0:T(8,128)S(1)} %convolution_multiply_fusion.2, f32[256]{0:T(256)S(1)} %add.175, f32[256]{0:T(256)S(1)} %add.172, f32[512]{0:T(512)S(1)} %multiply_reduce_fusion.3, f32[512]{0:T(512)S(1)} %get-tuple-element.9, f32[2048,512]{1,0:T(8,128)} %param.8), kind=kOutput, calls=%fused_computation.31 | convolution fusion | flops 806486016 | bytes 2627584 | tf_op jit(solution)/shard_map/dot_general | solution.py:12
  58.9 1.1 convolution_multiply_fusion.4
  60.1 3.5 %fusion.21 = f32[256,512]{1,0:T(8,128)} fusion(f32[256,512]{1,0:T(8,128)S(1)} %bitcast.89, f32[256,512]{1,0:T(8,128)S(1)} %convolution_multiply_fusion.4, f32[512]{0:T(512)S(1)} %multiply_reduce_fusion.3, f32[256]{0:T(256)S(1)} %add.159, f32[512]{0:T(512)S(1)} %get-tuple-element.9, f32[256]{0:T(256)S(1)} %add.155, f32[2048,512]{1,0:T(8,128)} %param.8), kind=kOutput, calls=%fused_computation.37 | convolution fusion | flops 806486016 | bytes 2627584 | tf_op jit(solution)/shard_map/dot_general | solution.py:12
  63.6 19.0 %collective-permute-done.19 = f32[256,1536]{1,0:T(8,128)} collective-permute-done((f32[256,1536]{1,0:T(8,128)}, f32[256,1536]{1,0:T(8,128)}, u32[]{:S(2)}, u32[]{:S(2)}) %collective-permute-start.19) | collective-permute-done | bytes 1572896 | tf_op jit(solution)/shard_map/ppermute | solution.py:39
  82.6 2.5 %multiply_exponential_fusion = f32[256,1536]{1,0:T(8,128)S(1)} fusion(f32[256,1536]{1,0:T(8,128)} %fusion.1, f32[256,1536]{1,0:T(8,128)} %collective-permute-done.19), kind=kLoop, calls=%fused_computation.18 | loop fusion | flops 1572864 | bytes 4718592 | tf_op jit(solution)/shard_map/exp | solution.py:29
  85.1 1.9 fusion.5
  87.1 0.8 copy.14
  88.0 28.0 %collective-permute-done.10 = f32[256,1536]{1,0:T(8,128)} collective-permute-done((f32[256,1536]{1,0:T(8,128)}, f32[256,1536]{1,0:T(8,128)}, u32[]{:S(2)}, u32[]{:S(2)}) %collective-permute-start.10) | collective-permute-done | bytes 1572896 | tf_op jit(solution)/shard_map/ppermute | solution.py:39
  115.9 2.5 %multiply_exponential_fusion.1 = f32[256,1536]{1,0:T(8,128)S(1)} fusion(f32[256,1536]{1,0:T(8,128)} %fusion, f32[256,1536]{1,0:T(8,128)} %collective-permute-done.10), kind=kLoop, calls=%fused_computation.19 | loop fusion | flops 1572864 | bytes 4718592 | tf_op jit(solution)/shard_map/exp | solution.py:29
  118.4 1.9 fusion.7
  121.2 1.8 copy.12
  123.0 0.8 copy.13
  123.8 1.1 add.182
  125.6 1.5 collective-permute-start.21
  127.1 1.8 copy.11
  128.9 1.1 add.168
  130.6 1.1 collective-permute-done.21
  131.7 1.7 collective-permute-start.22
  133.4 2.3 %collective-permute-done.12 = f32[4,16,500]{2,1,0:T(8,128)S(1)} collective-permute-done((f32[4,16,500]{2,1,0:T(8,128)S(1)}, f32[4,16,500]{2,1,0:T(8,128)S(1)}, u32[]{:S(2)}, u32[]{:S(2)}) %collective-permute-start.12) | collective-permute-done | bytes 128032 | tf_op jit(solution)/shard_map/ppermute | solution.py:34
  135.7 1.7 collective-permute-start.13
  137.4 2.3 %collective-permute-start.23 = (f32[1,16,500]{2,1,0:T(8,128)S(1)}, f32[1,16,500]{2,1,0:T(8,128)S(1)}, u32[]{:S(2)}, u32[]{:S(2)}) collective-permute-start(f32[1,16,500]{2,1,0:T(8,128)S(1)} %slice.133), channel_id=1, source_target_pairs={{0,16},{2,18},{4,20},{6,22},{8,24},{10,26},{12,28},{14,30},{16,0},... | collective-permute-start | bytes 96008 | tf_op jit(solution)/shard_map/ppermute | solution.py:34
  140.1 2.9 %collective-permute-start.14 = (f32[1,16,500]{2,1,0:T(8,128)S(1)}, f32[1,16,500]{2,1,0:T(8,128)S(1)}, u32[]{:S(2)}, u32[]{:S(2)}) collective-permute-start(f32[1,16,500]{2,1,0:T(8,128)S(1)} %slice.124), channel_id=1, source_target_pairs={{0,16},{2,18},{4,20},{6,22},{8,24},{10,26},{12,28},{14,30},{16,0},... | collective-permute-start | bytes 96008 | tf_op jit(solution)/shard_map/ppermute | solution.py:34
  143.0 2.0 collective-permute-done.14
  145.0 3.0 %collective-permute-start.24 = (f32[16,500]{1,0:T(8,128)S(1)}, f32[16,500]{1,0:T(8,128)S(1)}, u32[]{:S(2)}, u32[]{:S(2)}) collective-permute-start(f32[16,500]{1,0:T(8,128)S(1)} %bitcast.103), channel_id=1, source_target_pairs={{0,16},{2,18},{4,20},{6,22},{8,24},{10,26},{12,28},{14,30},{16,0},... | collective-permute-start | bytes 96008 | tf_op jit(solution)/shard_map/ppermute | solution.py:34
  148.0 1.9 collective-permute-done.24
  150.0 2.8 %collective-permute-done.33 = f32[16,500]{1,0:T(8,128)S(1)} collective-permute-done((f32[16,500]{1,0:T(8,128)S(1)}, f32[16,500]{1,0:T(8,128)S(1)}, u32[]{:S(2)}, u32[]{:S(2)}) %collective-permute-start.33) | collective-permute-done | bytes 32032 | tf_op jit(solution)/shard_map/ppermute | solution.py:34
  153.4 1.7 collective-permute-start.34
  155.1 2.6 %collective-permute-done.34 = f32[2,16,500]{2,1,0:T(8,128)S(1)} collective-permute-done((f32[2,16,500]{2,1,0:T(8,128)S(1)}, f32[2,16,500]{2,1,0:T(8,128)S(1)}, u32[]{:S(2)}, u32[]{:S(2)}) %collective-permute-start.34) | collective-permute-done | bytes 64032 | tf_op jit(solution)/shard_map/ppermute | solution.py:34
  158.4 1.7 collective-permute-start.25
  160.0 2.7 %collective-permute-done.35 = f32[2,2,16,500]{3,2,1,0:T(8,128)S(1)} collective-permute-done((f32[2,2,16,500]{3,2,1,0:T(8,128)S(1)}, f32[2,2,16,500]{3,2,1,0:T(8,128)S(1)}, u32[]{:S(2)}, u32[]{:S(2)}) %collective-permute-start.35) | collective-permute-done | bytes 128032 | tf_op jit(solution)/shard_map/ppermute | solution.py:34
  162.9 1.3 collective-permute-start.26
  164.2 4.7 %collective-permute-done.26 = f32[2,2,16,500]{3,2,1,0:T(8,128)S(1)} collective-permute-done((f32[2,2,16,500]{3,2,1,0:T(8,128)S(1)}, f32[2,2,16,500]{3,2,1,0:T(8,128)S(1)}, u32[]{:S(2)}, u32[]{:S(2)}) %collective-permute-start.26) | collective-permute-done | bytes 128032 | tf_op jit(solution)/shard_map/ppermute | solution.py:34
  169.1 4.6 %multiply_reduce_fusion = (f32[]{:T(128)}, f32[2048,500]{0,1:T(8,128)}) fusion(f32[256,500]{1,0:T(8,128)S(1)} %bitcast.93, f32[256,1536]{1,0:T(8,128)S(1)} %multiply_exponential_fusion, f32[256,512]{1,0:T(8,128)S(1)} %copy-done.6), kind=kOutput, calls=%fused_computation.3 | convolution fusion | flops 1576460288 | bytes 6705156 | tf_op jit(solution)/shard_map/dot_general | solution.py:12
  173.7 1.5 collective-permute-start.37
  175.3 4.8 %multiply_reduce_fusion.1 = (f32[]{:T(128)}, f32[2048,500]{0,1:T(8,128)}) fusion(f32[256,500]{1,0:T(8,128)S(1)} %bitcast.94, f32[256,1536]{1,0:T(8,128)S(1)} %multiply_exponential_fusion.1, f32[256,512]{1,0:T(8,128)S(1)} %copy-done.4), kind=kOutput, calls=%fused_computation.4 | convolution fusion | flops 1576460288 | bytes 6705156 | tf_op jit(solution)/shard_map/dot_general | solution.py:12
  181.8 1.0 collective-permute-start.38
  184.9 0.9 collective-permute-start.29
  186.4 1.9 collective-permute-start.39
  189.0 2.8 %collective-permute-start.30 = (f32[]{:T(128)}, f32[]{:T(128)}, u32[]{:S(2)}, u32[]{:S(2)}) collective-permute-start(f32[]{:T(128)} %add.187), channel_id=1, source_target_pairs={{0,4},{2,6},{4,0},{6,2},{8,12},{10,14},{12,8},{14,10},{16,20},{18,... | collective-permute-start | bytes 20 | tf_op jit(solution)/shard_map/ppermute | solution.py:34
  192.5 3.0 %collective-permute-start.40 = (f32[]{:T(128)}, f32[]{:T(128)}, u32[]{:S(2)}, u32[]{:S(2)}) collective-permute-start(f32[]{:T(128)} %add.194), channel_id=1, source_target_pairs={{0,8},{2,10},{4,12},{6,14},{8,0},{10,2},{12,4},{14,6},{16,24},{18,... | collective-permute-start | bytes 20 | tf_op jit(solution)/shard_map/ppermute | solution.py:34
  196.2 1.7 collective-permute-start.31
  198.6 2.0 collective-permute-start.41
  201.2 3.7 %collective-permute-start.32 = (f32[]{:T(128)}, f32[]{:T(128)}, u32[]{:S(2)}, u32[]{:S(2)}) collective-permute-start(f32[]{:T(128)} %add.189), channel_id=1, source_target_pairs={{0,16},{2,18},{4,20},{6,22},{8,24},{10,26},{12,28},{14,30},{16,0},... | collective-permute-start | bytes 20 | tf_op jit(solution)/shard_map/ppermute | solution.py:34
  206.5 8.5 %divide_subtract_fusion = f32[2048,500]{0,1:T(8,128)} fusion(f32[2048,500]{0,1:T(8,128)} %get-tuple-element.59, f32[2048,500]{0,1:T(8,128)} %param.9, f32[2048,500]{0,1:T(8,128)} %get-tuple-element.61, f32[]{:T(128)S(6)} %sqrt.23, f32[]{:T(128)S(6)} %sqrt.22), kind=kLoop, calls=%fused_computation.2 | loop fusion | flops 6144000 | bytes 16384008 | tf_op jit(solution)/shard_map/sub | solution.py:115
  (107 shorter events, 11.2 us)
Async XLA Ops:
  4.3 13.6 %collective-permute-start = (f32[16,512]{1,0:T(8,128)S(1)}, f32[16,512]{1,0:T(8,128)S(1)}, u32[]{:S(2)}, u32[]{:S(2)}) collective-permute-start(f32[16,512]{1,0:T(8,128)S(1)} %broadcast_select_fusion.1), channel_id=1, source_target_pairs={{0,16},{2,18},{4,20},{6,22},{8,24},{10,26},{12,28},{14,30},{16,0},... | collective-permute-start | bytes 98312 | tf_op jit(solution)/shard_map/ppermute | solution.py:34
  11.2 4.8 %collective-permute-start.15 = (f32[16,512]{1,0:T(8,128)S(1)}, f32[16,512]{1,0:T(8,128)S(1)}, u32[]{:S(2)}, u32[]{:S(2)}) collective-permute-start(f32[16,512]{1,0:T(8,128)S(1)} %broadcast_select_fusion), channel_id=1, source_target_pairs={{0,16},{2,18},{4,20},{6,22},{8,24},{10,26},{12,28},{14,30},{16,0},... | collective-permute-start | bytes 98312 | tf_op jit(solution)/shard_map/ppermute | solution.py:34
  11.2 7.0 %collective-permute-start.4 = (f32[32,512]{1,0:T(8,128)S(1)}, f32[32,512]{1,0:T(8,128)S(1)}, u32[]{:S(2)}, u32[]{:S(2)}) collective-permute-start(f32[32,512]{1,0:T(8,128)S(1)} %pad_maximum_fusion.25), channel_id=1, source_target_pairs={{0,1},{1,0},{2,3},{3,2},{4,5},{5,4},{6,7},{7,6},{8,9},{9,8},{10,11... | collective-permute-start | bytes 196616 | tf_op jit(solution)/shard_map/ppermute | solution.py:39
  13.0 17.3 %copy-start = (f32[2048,512]{1,0:T(8,128)S(1)}, f32[2048,512]{1,0:T(8,128)}, u32[]{:S(2)}) copy-start(f32[2048,512]{1,0:T(8,128)} %param.8) | copy-start | bytes 12582916
  15.5 38.9 %collective-permute-start.9 = (f32[512,512]{1,0:T(8,128)}, f32[512,512]{1,0:T(8,128)S(1)}, u32[]{:S(2)}, u32[]{:S(2)}) collective-permute-start(f32[512,512]{1,0:T(8,128)} %get-tuple-element.10), channel_id=1, source_target_pairs={{0,1},{1,0},{2,3},{3,2},{4,5},{5,4},{6,7},{7,6},{8,9},{9,8},{10,11... | collective-permute-start | bytes 3145736 | tf_op jit(solution)/shard_map/ppermute | solution.py:39
  16.0 5.1 %collective-permute-start.16 = (f32[2,16,512]{2,1,0:T(8,128)S(1)}, f32[2,16,512]{2,1,0:T(8,128)S(1)}, u32[]{:S(2)}, u32[]{:S(2)}) collective-permute-start(f32[2,16,512]{2,1,0:T(8,128)S(1)} %get-tuple-element.50), channel_id=1, source_target_pairs={{0,8},{2,10},{4,12},{6,14},{8,0},{10,2},{12,4},{14,6},{16,24},{18,... | collective-permute-start | bytes 196616 | tf_op jit(solution)/shard_map/ppermute | solution.py:34
  17.8 7.7 %collective-permute-start.1 = (f32[2,16,512]{2,1,0:T(8,128)S(1)}, f32[2,16,512]{2,1,0:T(8,128)S(1)}, u32[]{:S(2)}, u32[]{:S(2)}) collective-permute-start(f32[2,16,512]{2,1,0:T(8,128)S(1)} %get-tuple-element.52), channel_id=1, source_target_pairs={{0,8},{2,10},{4,12},{6,14},{8,0},{10,2},{12,4},{14,6},{16,24},{18,... | collective-permute-start | bytes 196616 | tf_op jit(solution)/shard_map/ppermute | solution.py:34
  18.2 5.3 %collective-permute-start.5 = (f32[32,512]{1,0:T(8,128)S(1)}, f32[32,512]{1,0:T(8,128)S(1)}, u32[]{:S(2)}, u32[]{:S(2)}) collective-permute-start(f32[32,512]{1,0:T(8,128)S(1)} %collective-permute-done.4), channel_id=1, source_target_pairs={{0,16},{2,18},{4,20},{6,22},{8,24},{10,26},{12,28},{14,30},{16,0},... | collective-permute-start | bytes 196616 | tf_op jit(solution)/shard_map/ppermute | solution.py:34
  21.1 6.1 %collective-permute-start.17 = (f32[2,2,16,512]{3,2,1,0:T(8,128)S(1)}, f32[2,2,16,512]{3,2,1,0:T(8,128)S(1)}, u32[]{:S(2)}, u32[]{:S(2)}) collective-permute-start(f32[2,2,16,512]{3,2,1,0:T(8,128)S(1)} %get-tuple-element.38), channel_id=1, source_target_pairs={{0,4},{2,6},{4,0},{6,2},{8,12},{10,14},{12,8},{14,10},{16,20},{18,... | collective-permute-start | bytes 393224 | tf_op jit(solution)/shard_map/ppermute | solution.py:34
  23.5 5.0 %collective-permute-start.6 = (f32[2,32,512]{2,1,0:T(8,128)S(1)}, f32[2,32,512]{2,1,0:T(8,128)S(1)}, u32[]{:S(2)}, u32[]{:S(2)}) collective-permute-start(f32[2,32,512]{2,1,0:T(8,128)S(1)} %get-tuple-element.40), channel_id=1, source_target_pairs={{0,8},{2,10},{4,12},{6,14},{8,0},{10,2},{12,4},{14,6},{16,24},{18,... | collective-permute-start | bytes 393224 | tf_op jit(solution)/shard_map/ppermute | solution.py:34
  25.6 5.1 %collective-permute-start.2 = (f32[2,2,16,512]{3,2,1,0:T(8,128)S(1)}, f32[2,2,16,512]{3,2,1,0:T(8,128)S(1)}, u32[]{:S(2)}, u32[]{:S(2)}) collective-permute-start(f32[2,2,16,512]{3,2,1,0:T(8,128)S(1)} %get-tuple-element.42), channel_id=1, source_target_pairs={{0,4},{2,6},{4,0},{6,2},{8,12},{10,14},{12,8},{14,10},{16,20},{18,... | collective-permute-start | bytes 393224 | tf_op jit(solution)/shard_map/ppermute | solution.py:34
  27.2 3.6 %collective-permute-start.18 = (f32[2,2,2,16,512]{4,3,2,1,0:T(8,128)S(1)}, f32[2,2,2,16,512]{4,3,2,1,0:T(8,128)S(1)}, u32[]{:S(2)}, u32[]{:S(2)}) collective-permute-start(f32[2,2,2,16,512]{4,3,2,1,0:T(8,128)S(1)} %get-tuple-element.28), channel_id=1, source_target_pairs={{0,2},{2,0},{4,6},{6,4},{8,10},{10,8},{12,14},{14,12},{16,18},{18,... | collective-permute-start | bytes 786440 | tf_op jit(solution)/shard_map/ppermute | solution.py:34
  28.6 7.6 %collective-permute-start.7 = (f32[2,2,32,512]{3,2,1,0:T(8,128)S(1)}, f32[2,2,32,512]{3,2,1,0:T(8,128)S(1)}, u32[]{:S(2)}, u32[]{:S(2)}) collective-permute-start(f32[2,2,32,512]{3,2,1,0:T(8,128)S(1)} %get-tuple-element.30), channel_id=1, source_target_pairs={{0,4},{2,6},{4,0},{6,2},{8,12},{10,14},{12,8},{14,10},{16,20},{18,... | collective-permute-start | bytes 786440 | tf_op jit(solution)/shard_map/ppermute | solution.py:34
  30.7 13.2 %collective-permute-start.3 = (f32[2,2,2,16,512]{4,3,2,1,0:T(8,128)S(1)}, f32[2,2,2,16,512]{4,3,2,1,0:T(8,128)}, u32[]{:S(2)}, u32[]{:S(2)}) collective-permute-start(f32[2,2,2,16,512]{4,3,2,1,0:T(8,128)S(1)} %get-tuple-element.32), channel_id=1, source_target_pairs={{0,2},{2,0},{4,6},{6,4},{8,10},{10,8},{12,14},{14,12},{16,18},{18,... | collective-permute-start | bytes 786440 | tf_op jit(solution)/shard_map/ppermute | solution.py:34
  36.2 0.7 copy-start.7
  38.0 15.0 %collective-permute-start.8 = (f32[2,2,2,32,512]{4,3,2,1,0:T(8,128)S(1)}, f32[2,2,2,32,512]{4,3,2,1,0:T(8,128)}, u32[]{:S(2)}, u32[]{:S(2)}) collective-permute-start(f32[2,2,2,32,512]{4,3,2,1,0:T(8,128)S(1)} %get-tuple-element.16), channel_id=1, source_target_pairs={{0,2},{2,0},{4,6},{6,4},{8,10},{10,8},{12,14},{14,12},{16,18},{18,... | collective-permute-start | bytes 1572872 | tf_op jit(solution)/shard_map/ppermute | solution.py:34
  45.1 37.5 %collective-permute-start.19 = (f32[256,1536]{1,0:T(8,128)}, f32[256,1536]{1,0:T(8,128)}, u32[]{:S(2)}, u32[]{:S(2)}) collective-permute-start(f32[256,1536]{1,0:T(8,128)} %fusion.1), channel_id=1, source_target_pairs={{0,1},{1,0},{2,3},{3,2},{4,5},{5,4},{6,7},{7,6},{8,9},{9,8},{10,11... | collective-permute-start | bytes 4718600 | tf_op jit(solution)/shard_map/ppermute | solution.py:39
  52.5 63.5 %collective-permute-start.10 = (f32[256,1536]{1,0:T(8,128)}, f32[256,1536]{1,0:T(8,128)}, u32[]{:S(2)}, u32[]{:S(2)}) collective-permute-start(f32[256,1536]{1,0:T(8,128)} %fusion), channel_id=1, source_target_pairs={{0,1},{1,0},{2,3},{3,2},{4,5},{5,4},{6,7},{7,6},{8,9},{9,8},{10,11... | collective-permute-start | bytes 4718600 | tf_op jit(solution)/shard_map/ppermute | solution.py:39
  63.6 21.5 %copy-start.1 = (f32[2048,500]{0,1:T(8,128)S(1)}, f32[2048,500]{0,1:T(8,128)}, u32[]{:S(2)}) copy-start(f32[2048,500]{0,1:T(8,128)} %param.9) | copy-start | bytes 12288004
  63.6 21.5 %copy-start.5 = (f32[256,512]{1,0:T(8,128)S(1)}, f32[256,512]{1,0:T(8,128)}, u32[]{:S(2)}) copy-start(f32[256,512]{1,0:T(8,128)} %fusion.15) | copy-start | bytes 1572868
  87.9 30.5 %copy-start.2 = (f32[2048,500]{0,1:T(8,128)S(1)}, f32[2048,500]{0,1:T(8,128)}, u32[]{:S(2)}) copy-start(f32[2048,500]{0,1:T(8,128)} %param.9) | copy-start | bytes 12288004
  87.9 30.5 %copy-start.3 = (f32[256,512]{1,0:T(8,128)S(1)}, f32[256,512]{1,0:T(8,128)}, u32[]{:S(2)}) copy-start(f32[256,512]{1,0:T(8,128)} %fusion.21) | copy-start | bytes 1572868
  88.0 35.9 %collective-permute-start.20 = (f32[8,16,500]{2,1,0:T(8,128)}, f32[8,16,500]{2,1,0:T(8,128)}, u32[]{:S(2)}, u32[]{:S(2)}) collective-permute-start(f32[8,16,500]{2,1,0:T(8,128)} %bitcast.34), channel_id=1, source_target_pairs={{0,2},{2,0},{4,6},{6,4},{8,10},{10,8},{12,14},{14,12},{16,18},{18,... | collective-permute-start | bytes 768008 | tf_op jit(solution)/shard_map/ppermute | solution.py:34
  123.0 5.9 %collective-permute-start.11 = (f32[8,16,500]{2,1,0:T(8,128)}, f32[8,16,500]{2,1,0:T(8,128)}, u32[]{:S(2)}, u32[]{:S(2)}) collective-permute-start(f32[8,16,500]{2,1,0:T(8,128)} %bitcast.97), channel_id=1, source_target_pairs={{0,2},{2,0},{4,6},{6,4},{8,10},{10,8},{12,14},{14,12},{16,18},{18,... | collective-permute-start | bytes 768008 | tf_op jit(solution)/shard_map/ppermute | solution.py:34
  125.6 6.1 %collective-permute-start.21 = (f32[4,16,500]{2,1,0:T(8,128)}, f32[4,16,500]{2,1,0:T(8,128)S(1)}, u32[]{:S(2)}, u32[]{:S(2)}) collective-permute-start(f32[4,16,500]{2,1,0:T(8,128)} %slice.129), channel_id=1, source_target_pairs={{0,4},{2,6},{4,0},{6,2},{8,12},{10,14},{12,8},{14,10},{16,20},{18,... | collective-permute-start | bytes 384008 | tf_op jit(solution)/shard_map/ppermute | solution.py:34
  128.9 16.1 %copy-start.8 = (f32[2,16,500]{2,1,0:T(8,128)S(1)}, f32[2,16,500]{2,1,0:T(8,128)}, u32[]{:S(2)}) copy-start(f32[2,16,500]{2,1,0:T(8,128)} %param.11) | copy-start | bytes 192004
  130.0 5.7 %collective-permute-start.12 = (f32[4,16,500]{2,1,0:T(8,128)S(1)}, f32[4,16,500]{2,1,0:T(8,128)S(1)}, u32[]{:S(2)}, u32[]{:S(2)}) collective-permute-start(f32[4,16,500]{2,1,0:T(8,128)S(1)} %slice.120), channel_id=1, source_target_pairs={{0,4},{2,6},{4,0},{6,2},{8,12},{10,14},{12,8},{14,10},{16,20},{18,... | collective-permute-start | bytes 384008 | tf_op jit(solution)/shard_map/ppermute | solution.py:34
  131.7 5.7 %collective-permute-start.22 = (f32[2,16,500]{2,1,0:T(8,128)S(1)}, f32[2,16,500]{2,1,0:T(8,128)S(1)}, u32[]{:S(2)}, u32[]{:S(2)}) collective-permute-start(f32[2,16,500]{2,1,0:T(8,128)S(1)} %slice.131), channel_id=1, source_target_pairs={{0,8},{2,10},{4,12},{6,14},{8,0},{10,2},{12,4},{14,6},{16,24},{18,... | collective-permute-start | bytes 192008 | tf_op jit(solution)/shard_map/ppermute | solution.py:34
  135.7 4.3 %collective-permute-start.13 = (f32[2,16,500]{2,1,0:T(8,128)S(1)}, f32[2,16,500]{2,1,0:T(8,128)S(1)}, u32[]{:S(2)}, u32[]{:S(2)}) collective-permute-start(f32[2,16,500]{2,1,0:T(8,128)S(1)} %slice.122), channel_id=1, source_target_pairs={{0,8},{2,10},{4,12},{6,14},{8,0},{10,2},{12,4},{14,6},{16,24},{18,... | collective-permute-start | bytes 192008 | tf_op jit(solution)/shard_map/ppermute | solution.py:34
  137.4 5.5 %collective-permute-start.23 = (f32[1,16,500]{2,1,0:T(8,128)S(1)}, f32[1,16,500]{2,1,0:T(8,128)S(1)}, u32[]{:S(2)}, u32[]{:S(2)}) collective-permute-start(f32[1,16,500]{2,1,0:T(8,128)S(1)} %slice.133), channel_id=1, source_target_pairs={{0,16},{2,18},{4,20},{6,22},{8,24},{10,26},{12,28},{14,30},{16,0},... | collective-permute-start | bytes 96008 | tf_op jit(solution)/shard_map/ppermute | solution.py:34
  140.1 29.0 %copy-start.6 = (f32[256,512]{1,0:T(8,128)S(1)}, f32[256,512]{1,0:T(8,128)}, u32[]{:S(2)}) copy-start(f32[256,512]{1,0:T(8,128)} %fusion.15) | copy-start | bytes 1572868
  140.1 4.9 %collective-permute-start.14 = (f32[1,16,500]{2,1,0:T(8,128)S(1)}, f32[1,16,500]{2,1,0:T(8,128)S(1)}, u32[]{:S(2)}, u32[]{:S(2)}) collective-permute-start(f32[1,16,500]{2,1,0:T(8,128)S(1)} %slice.124), channel_id=1, source_target_pairs={{0,16},{2,18},{4,20},{6,22},{8,24},{10,26},{12,28},{14,30},{16,0},... | collective-permute-start | bytes 96008 | tf_op jit(solution)/shard_map/ppermute | solution.py:34
  145.0 5.0 %collective-permute-start.24 = (f32[16,500]{1,0:T(8,128)S(1)}, f32[16,500]{1,0:T(8,128)S(1)}, u32[]{:S(2)}, u32[]{:S(2)}) collective-permute-start(f32[16,500]{1,0:T(8,128)S(1)} %bitcast.103), channel_id=1, source_target_pairs={{0,16},{2,18},{4,20},{6,22},{8,24},{10,26},{12,28},{14,30},{16,0},... | collective-permute-start | bytes 96008 | tf_op jit(solution)/shard_map/ppermute | solution.py:34
  148.0 4.8 %collective-permute-start.33 = (f32[16,500]{1,0:T(8,128)S(1)}, f32[16,500]{1,0:T(8,128)S(1)}, u32[]{:S(2)}, u32[]{:S(2)}) collective-permute-start(f32[16,500]{1,0:T(8,128)S(1)} %bitcast.102), channel_id=1, source_target_pairs={{0,16},{2,18},{4,20},{6,22},{8,24},{10,26},{12,28},{14,30},{16,0},... | collective-permute-start | bytes 96008 | tf_op jit(solution)/shard_map/ppermute | solution.py:34
  153.4 4.3 %collective-permute-start.34 = (f32[2,16,500]{2,1,0:T(8,128)S(1)}, f32[2,16,500]{2,1,0:T(8,128)S(1)}, u32[]{:S(2)}, u32[]{:S(2)}) collective-permute-start(f32[2,16,500]{2,1,0:T(8,128)S(1)} %get-tuple-element.54), channel_id=1, source_target_pairs={{0,8},{2,10},{4,12},{6,14},{8,0},{10,2},{12,4},{14,6},{16,24},{18,... | collective-permute-start | bytes 192008 | tf_op jit(solution)/shard_map/ppermute | solution.py:34
  157.7 5.0 %collective-permute-start.35 = (f32[2,2,16,500]{3,2,1,0:T(8,128)S(1)}, f32[2,2,16,500]{3,2,1,0:T(8,128)S(1)}, u32[]{:S(2)}, u32[]{:S(2)}) collective-permute-start(f32[2,2,16,500]{3,2,1,0:T(8,128)S(1)} %get-tuple-element.36), channel_id=1, source_target_pairs={{0,4},{2,6},{4,0},{6,2},{8,12},{10,14},{12,8},{14,10},{16,20},{18,... | collective-permute-start | bytes 384008 | tf_op jit(solution)/shard_map/ppermute | solution.py:34
  158.4 4.5 %collective-permute-start.25 = (f32[2,16,500]{2,1,0:T(8,128)S(1)}, f32[2,16,500]{2,1,0:T(8,128)S(1)}, u32[]{:S(2)}, u32[]{:S(2)}) collective-permute-start(f32[2,16,500]{2,1,0:T(8,128)S(1)} %get-tuple-element.44), channel_id=1, source_target_pairs={{0,8},{2,10},{4,12},{6,14},{8,0},{10,2},{12,4},{14,6},{16,24},{18,... | collective-permute-start | bytes 192008 | tf_op jit(solution)/shard_map/ppermute | solution.py:34
  162.8 6.2 %collective-permute-start.36 = (f32[2,2,2,16,500]{4,3,2,1,0:T(8,128)S(1)}, f32[2,2,2,16,500]{4,3,2,1,0:T(8,128)S(1)}, u32[]{:S(2)}, u32[]{:S(2)}) collective-permute-start(f32[2,2,2,16,500]{4,3,2,1,0:T(8,128)S(1)} %get-tuple-element.26), channel_id=1, source_target_pairs={{0,2},{2,0},{4,6},{6,4},{8,10},{10,8},{12,14},{14,12},{16,18},{18,... | collective-permute-start | bytes 768008 | tf_op jit(solution)/shard_map/ppermute | solution.py:34
  162.9 6.0 %collective-permute-start.26 = (f32[2,2,16,500]{3,2,1,0:T(8,128)S(1)}, f32[2,2,16,500]{3,2,1,0:T(8,128)S(1)}, u32[]{:S(2)}, u32[]{:S(2)}) collective-permute-start(f32[2,2,16,500]{3,2,1,0:T(8,128)S(1)} %get-tuple-element.34), channel_id=1, source_target_pairs={{0,4},{2,6},{4,0},{6,2},{8,12},{10,14},{12,8},{14,10},{16,20},{18,... | collective-permute-start | bytes 384008 | tf_op jit(solution)/shard_map/ppermute | solution.py:34
  168.9 6.2 %collective-permute-start.27 = (f32[2,2,2,16,500]{4,3,2,1,0:T(8,128)S(1)}, f32[2,2,2,16,500]{4,3,2,1,0:T(8,128)S(1)}, u32[]{:S(2)}, u32[]{:S(2)}) collective-permute-start(f32[2,2,2,16,500]{4,3,2,1,0:T(8,128)S(1)} %get-tuple-element.24), channel_id=1, source_target_pairs={{0,2},{2,0},{4,6},{6,4},{8,10},{10,8},{12,14},{14,12},{16,18},{18,... | collective-permute-start | bytes 768008 | tf_op jit(solution)/shard_map/ppermute | solution.py:34
  169.1 6.2 %copy-start.4 = (f32[256,512]{1,0:T(8,128)S(1)}, f32[256,512]{1,0:T(8,128)}, u32[]{:S(2)}) copy-start(f32[256,512]{1,0:T(8,128)} %fusion.21) | copy-start | bytes 1572868
  173.7 6.9 %collective-permute-start.37 = (f32[]{:T(128)}, f32[]{:T(128)}, u32[]{:S(2)}, u32[]{:S(2)}) collective-permute-start(f32[]{:T(128)} %get-tuple-element.58), channel_id=1, source_target_pairs={{0,1},{1,0},{2,3},{3,2},{4,5},{5,4},{6,7},{7,6},{8,9},{9,8},{10,11... | collective-permute-start | bytes 20 | tf_op jit(solution)/shard_map/ppermute | solution.py:39
  180.1 3.6 %collective-permute-start.28 = (f32[]{:T(128)}, f32[]{:T(128)}, u32[]{:S(2)}, u32[]{:S(2)}) collective-permute-start(f32[]{:T(128)} %get-tuple-element.60), channel_id=1, source_target_pairs={{0,1},{1,0},{2,3},{3,2},{4,5},{5,4},{6,7},{7,6},{8,9},{9,8},{10,11... | collective-permute-start | bytes 20 | tf_op jit(solution)/shard_map/ppermute | solution.py:39
  181.8 4.0 %collective-permute-start.38 = (f32[]{:T(128)}, f32[]{:T(128)}, u32[]{:S(2)}, u32[]{:S(2)}) collective-permute-start(f32[]{:T(128)} %add.192), channel_id=1, source_target_pairs={{0,2},{2,0},{4,6},{6,4},{8,10},{10,8},{12,14},{14,12},{16,18},{18,... | collective-permute-start | bytes 20 | tf_op jit(solution)/shard_map/ppermute | solution.py:34
  184.9 3.4 %collective-permute-start.29 = (f32[]{:T(128)}, f32[]{:T(128)}, u32[]{:S(2)}, u32[]{:S(2)}) collective-permute-start(f32[]{:T(128)} %add.186), channel_id=1, source_target_pairs={{0,2},{2,0},{4,6},{6,4},{8,10},{10,8},{12,14},{14,12},{16,18},{18,... | collective-permute-start | bytes 20 | tf_op jit(solution)/shard_map/ppermute | solution.py:34
  186.4 5.4 %collective-permute-start.39 = (f32[]{:T(128)}, f32[]{:T(128)}, u32[]{:S(2)}, u32[]{:S(2)}) collective-permute-start(f32[]{:T(128)} %add.193), channel_id=1, source_target_pairs={{0,4},{2,6},{4,0},{6,2},{8,12},{10,14},{12,8},{14,10},{16,20},{18,... | collective-permute-start | bytes 20 | tf_op jit(solution)/shard_map/ppermute | solution.py:34
  189.0 6.5 %collective-permute-start.30 = (f32[]{:T(128)}, f32[]{:T(128)}, u32[]{:S(2)}, u32[]{:S(2)}) collective-permute-start(f32[]{:T(128)} %add.187), channel_id=1, source_target_pairs={{0,4},{2,6},{4,0},{6,2},{8,12},{10,14},{12,8},{14,10},{16,20},{18,... | collective-permute-start | bytes 20 | tf_op jit(solution)/shard_map/ppermute | solution.py:34
  192.5 5.4 %collective-permute-start.40 = (f32[]{:T(128)}, f32[]{:T(128)}, u32[]{:S(2)}, u32[]{:S(2)}) collective-permute-start(f32[]{:T(128)} %add.194), channel_id=1, source_target_pairs={{0,8},{2,10},{4,12},{6,14},{8,0},{10,2},{12,4},{14,6},{16,24},{18,... | collective-permute-start | bytes 20 | tf_op jit(solution)/shard_map/ppermute | solution.py:34
  196.2 4.4 %collective-permute-start.31 = (f32[]{:T(128)}, f32[]{:T(128)}, u32[]{:S(2)}, u32[]{:S(2)}) collective-permute-start(f32[]{:T(128)} %add.188), channel_id=1, source_target_pairs={{0,8},{2,10},{4,12},{6,14},{8,0},{10,2},{12,4},{14,6},{16,24},{18,... | collective-permute-start | bytes 20 | tf_op jit(solution)/shard_map/ppermute | solution.py:34
  198.6 6.3 %collective-permute-start.41 = (f32[]{:T(128)}, f32[]{:T(128)}, u32[]{:S(2)}, u32[]{:S(2)}) collective-permute-start(f32[]{:T(128)} %add.195), channel_id=1, source_target_pairs={{0,16},{2,18},{4,20},{6,22},{8,24},{10,26},{12,28},{14,30},{16,0},... | collective-permute-start | bytes 20 | tf_op jit(solution)/shard_map/ppermute | solution.py:34
  201.2 4.6 %collective-permute-start.32 = (f32[]{:T(128)}, f32[]{:T(128)}, u32[]{:S(2)}, u32[]{:S(2)}) collective-permute-start(f32[]{:T(128)} %add.189), channel_id=1, source_target_pairs={{0,16},{2,18},{4,20},{6,22},{8,24},{10,26},{12,28},{14,30},{16,0},... | collective-permute-start | bytes 20 | tf_op jit(solution)/shard_map/ppermute | solution.py:34

commit v2 on v1

v2 whole, which is shorter than its diff:
```python
import functools
import math

import jax
import jax.numpy as jnp
from jax import lax
from jax.experimental import pallas as pl
from jax.experimental.pallas import tpu as pltpu
from jax.sharding import PartitionSpec as P

BLOCK = 256
SHARE = (1, 2)
LIMIT = 48 << 20
ROWS = ((1,), (1,))
ANY = pl.BlockSpec(memory_space=pl.ANY)
SCALARS = pl.BlockSpec(memory_space=pltpu.SMEM)


def dot(left, right, dims):
    return lax.dot_general(
        left, right, (dims, ((), ())), precision=lax.Precision.HIGHEST, preferred_element_type=jnp.float32
    )


def halves(x):
    high = x.astype(jnp.bfloat16)
    return high, (x - high.astype(jnp.float32)).astype(jnp.bfloat16)


def dot3(left, right, dims):
    one = functools.partial(lax.dot_general, dimension_numbers=(dims, ((), ())), preferred_element_type=jnp.float32)
    return one(left[0], right[0]) + (one(left[0], right[1]) + one(left[1], right[0]))


def laplace(squared, width):
    return jnp.exp(-jnp.sqrt(jnp.maximum(squared, 0.0)) / (0.5 * math.sqrt(width)))


def whole(x):
    return pl.BlockSpec(x.shape, lambda *_: (0,) * len(x.shape))


def call(kernel, grid, in_specs, out_specs, out_shape, scratch, flops, size):
    return pl.pallas_call(
        kernel,
        grid=grid,
        in_specs=in_specs,
        out_specs=out_specs,
        out_shape=out_shape,
        scratch_shapes=scratch,
        compiler_params=pltpu.CompilerParams(vmem_limit_bytes=LIMIT),
        cost_estimate=pl.CostEstimate(flops=flops, bytes_accessed=size, transcendentals=0),
    )


def f32(*shape):
    return jax.ShapeDtypeStruct(shape, jnp.float32)


def take(features, centres, batch_index, first, last):
    steps, rows = batch_index.shape
    copied = last > first

    def kernel(index, table, source, *rest):
        out = rest[0]
        sems = rest[-1]
        copies = []
        if copied:
            copies.append(pltpu.make_async_copy(source.at[pl.ds(first, last - first)], rest[1], sems.at[steps * rows]))
        for step in range(steps):
            for row in range(rows):
                spot = step * rows + row
                copies.append(
                    pltpu.make_async_copy(
                        table.at[pl.ds(index[step, row], 1)], out.at[pl.ds(spot, 1)], sems.at[spot]
                    )
                )
        for copy in copies:
            copy.start()
        for copy in copies:
            copy.wait()

    width = features.shape[1]
    shapes = [f32(steps * rows, width)] + ([f32(last - first, width)] if copied else [])
    return call(
        kernel, (), [SCALARS, ANY, ANY], [ANY] * len(shapes), shapes,
        [pltpu.SemaphoreType.DMA((steps * rows + 1,))], 0, 4 * width * (rows * steps + last - first),
    )(batch_index, features, centres)


def chunk_rows(ref, ranges):
    width = ref.shape[-1]
    return jnp.concatenate([ref[:, a:b].reshape(-1, width) for a, b in ranges])


def square_sums(x):
    return jnp.sum(x * x, axis=1, keepdims=True)


def square_row(x):
    return dot(jnp.ones((8, x.shape[1]), jnp.float32), x * x, ROWS)[:1]


def partial_squares(own, ranges, centres, start, order=()):
    count = own.shape[0]
    sizes = [count * (b - a) for a, b in ranges]
    late = centres.shape[0] - start

    def kernel(own_ref, centre_ref, *rest):
        outs = rest[len(order):]
        rows = chunk_rows(own_ref, ranges)
        block = centre_ref[...]
        square = square_sums(rows) + square_row(block) - 2.0 * dot(rows, block, ROWS)
        top = 0
        for out, size in zip(outs, sizes):
            out[...] = square[top : top + size]
            top += size

    total = sum(sizes)
    return call(
        kernel, (late // BLOCK,),
        [whole(own), pl.BlockSpec((BLOCK, own.shape[2]), lambda i: (i + start // BLOCK, 0))] + [ANY] * len(order),
        [pl.BlockSpec((size, BLOCK), lambda i: (0, i)) for size in sizes],
        [f32(size, late) for size in sizes],
        [], 12 * total * late * own.shape[2], 4 * (late * own.shape[2] + total * late),
    )(own, centres, *order)


def early_kernel(own, far, ranges, centres, fetched, width):
    sizes = [own.shape[0] * (b - a) for a, b in ranges]
    starts = [0]
    for part in fetched:
        starts.append(starts[-1] + part.shape[0] // BLOCK)

    def kernel(own_ref, far_ref, centre_ref, *rest):
        step = pl.program_id(0)
        outs = rest[len(fetched):]
        rows, others = chunk_rows(own_ref, ranges), chunk_rows(far_ref, ranges)
        block = centre_ref[...]
        near = square_sums(rows) + square_row(block) - 2.0 * dot(rows, block, ROWS)
        away = rest[0][...]
        for index in range(1, len(fetched)):
            away = jnp.where(step >= starts[index], rest[index][...], away)
        square = near + (square_sums(others) + square_row(away) - 2.0 * dot(others, away, ROWS))
        kern = laplace(square, width)
        top = 0
        for out, size in zip(outs, sizes):
            out[...] = kern[top : top + size]
            top += size

    def placed(index):
        blocks = starts[index + 1] - starts[index]
        return lambda i: (jnp.clip(i - starts[index], 0, blocks - 1), 0)

    depth = own.shape[2]
    total = sum(sizes)
    early = starts[-1] * BLOCK
    return call(
        kernel, (starts[-1],),
        [whole(own), whole(far), pl.BlockSpec((BLOCK, depth), lambda i: (i, 0))]
        + [pl.BlockSpec((BLOCK, depth), placed(index)) for index in range(len(fetched))],
        [pl.BlockSpec((size, BLOCK), lambda i: (0, i)) for size in sizes],
        [f32(size, early) for size in sizes],
        [], 24 * total * early * depth, 8 * early * depth + 4 * total * early,
    )(own, far, centres, *fetched)


def padded(outputs):
    return -(-outputs // 128) * 128


def predict(where, early, squares, coefs, targets, before, width, order=()):
    rows = squares[0].shape[0]
    centres, outputs = coefs.shape
    early_blocks = 0 if early is None else early.shape[1] // BLOCK
    pad = padded(outputs)
    columns = pad + sum(x.shape[0] for x in before) + rows
    own = targets.shape[0]
    quarter = rows // 4
    steps = centres // BLOCK
    ins = ([] if early is None else [early]) + list(squares) + [coefs, targets] + list(before) + list(order)

    def kernel(where_ref, *rest):
        rest = list(rest)
        early_ref = rest.pop(0) if early_blocks else None
        square_refs = [rest.pop(0) for _ in squares]
        coefs_ref, target_ref = rest.pop(0), rest.pop(0)
        before_refs = [rest.pop(0) for _ in before]
        kern_ref, out_ref, total = rest[len(order):]
        step = pl.program_id(0)

        @pl.when(step == 0)
        def _():
            total[...] = jnp.zeros_like(total)

        def late():
            square = square_refs[0][...]
            for ref in square_refs[1:]:
                square = square + ref[...]
            kern_ref[...] = laplace(square, width)

        if early_blocks:
            @pl.when(step < early_blocks)
            def _():
                kern_ref[...] = early_ref[...]

            pl.when(step >= early_blocks)(late)
        else:
            late()
        kern = halves(kern_ref[...])
        total[:, :outputs] += dot3(kern, halves(coefs_ref[...]), ((1,), (0,)))
        top = pad
        for ref in before_refs:
            total[:, top : top + ref.shape[0]] += dot3(kern, halves(ref[...]), ROWS)
            top += ref.shape[0]
        total[:, top:] += dot3(kern, kern, ROWS)

        @pl.when(step == steps - 1)
        def _():
            mine = pl.ds(pl.multiple_of(where_ref[0] * own, own), own)
            total[mine, :outputs] -= target_ref[...]
            for block in range(4):
                source = pl.multiple_of((where_ref[1] ^ block) * quarter, quarter)
                out_ref[block] = total[pl.ds(source, quarter), :]

    late_map = lambda i: (0, jnp.maximum(i - early_blocks, 0))
    specs = [SCALARS]
    if early_blocks:
        specs.append(pl.BlockSpec((rows, BLOCK), lambda i: (0, jnp.minimum(i, early_blocks - 1))))
    specs += [pl.BlockSpec((rows, BLOCK), late_map) for _ in squares]
    specs += [pl.BlockSpec((BLOCK, outputs), lambda i: (i, 0)), whole(targets)]
    specs += [pl.BlockSpec((x.shape[0], BLOCK), lambda i: (0, i)) for x in before]
    specs += [ANY] * len(order)
    return call(
        kernel, (steps,), specs,
        [pl.BlockSpec((rows, BLOCK), lambda i: (0, i)), pl.BlockSpec((4, quarter, columns), lambda i: (0, 0, 0))],
        [f32(rows, centres), f32(4, quarter, columns)],
        [pltpu.VMEM((rows, columns), jnp.float32)],
        6 * rows * centres * columns, 4 * centres * (outputs + 3 * rows),
    )(where, *ins)


def settle(where, near, far, outputs, own, before, square):
    quarter = near.shape[1]
    rows = 4 * quarter
    pad = padded(outputs)
    inner_columns = near.shape[2] - pad
    ins = [near, far] + list(before) + ([] if square is None else [square])

    def kernel(where_ref, near_ref, far_ref, *rest):
        before_refs = rest[: len(before)]
        resid_ref, own_ref, square_ref, inner = rest[-4:]
        for block in range(4):
            ref = (near_ref, far_ref)[block // 2]
            spot = pl.ds(pl.multiple_of((where_ref[1] ^ block) * quarter, quarter), quarter)
            resid_ref[spot, :] = ref[block % 2, :, :outputs]
            inner[spot, :] = ref[block % 2, :, pad:]
        resid = resid_ref[...]
        total = 0.0
        top = 0
        for ref in before_refs:
            part = inner[:, top : top + ref.shape[0]] * dot(resid, ref[...], ROWS)
            total = total + 2.0 * jnp.sum(part)
            top += ref.shape[0]
        total = total + jnp.sum(inner[:, top:] * dot(resid, resid, ROWS))
        if square is not None:
            square_ref[...] = rest[len(before)][...] + total
        else:
            square_ref[...] = jnp.full(square_ref.shape, total)
        own_ref[...] = resid_ref[pl.ds(pl.multiple_of(where_ref[0] * own, own), own), :]

    shapes = [f32(rows, outputs), f32(own, outputs), f32(8, 128)]
    return call(
        kernel, (1,), [SCALARS] + [whole(x) for x in ins], [whole(x) for x in shapes], shapes,
        [pltpu.VMEM((rows, inner_columns), jnp.float32)],
        12 * rows * inner_columns * outputs, 4 * near.size * 3,
    )(where, *ins)


def update(coefs, kerns, resids, squares, batch_total, entries):
    centres, outputs = coefs.shape
    count = len(kerns)

    def kernel(coefs_ref, *rest):
        square = rest[2 * count][:1, :1]
        for ref in rest[2 * count + 1 : -1]:
            square = square + ref[:1, :1]
        square = jnp.maximum(square, 0.0) / (batch_total * batch_total)
        scale = jnp.sqrt(square / entries + 1e-06)
        grad = 0.0
        for kern_ref, resid_ref in zip(rest[:count], rest[count:]):
            grad = grad + dot3(halves(kern_ref[...]), halves(resid_ref[...]), ((0,), (0,)))
        rest[-1][...] = coefs_ref[...] - (0.1 / batch_total) * grad / scale

    block = pl.BlockSpec((BLOCK, outputs), lambda i: (i, 0))
    rows = sum(x.shape[0] for x in kerns)
    return call(
        kernel, (centres // BLOCK,),
        [block] + [pl.BlockSpec((x.shape[0], BLOCK), lambda i: (0, i)) for x in kerns]
        + [whole(x) for x in list(resids) + list(squares)],
        block, f32(centres, outputs), [], 6 * rows * centres * outputs, 4 * centres * (rows + 2 * outputs),
    )(coefs, *kerns, *resids, *squares)


def swap(x, bit):
    n = lax.axis_size("cen")
    return lax.ppermute(x, "cen", [(i, i ^ bit) for i in range(n)])


def across(x):
    return lax.ppermute(x, "out", [(0, 1), (1, 0)])


def bits():
    n = lax.axis_size("cen")
    return [1 << b for b in range(n.bit_length() - 1)]


def mine(bit):
    return (lax.axis_index("cen") & bit) != 0


def gather(x):
    rest = x.shape
    for bit in reversed(bits()):
        far = swap(x, bit)
        x = jnp.where(mine(bit), jnp.stack([far, x]), jnp.stack([x, far]))
    return x.reshape((-1,) + rest)


def sum_cen(x):
    x = x[:2] + swap(x[2:], 1)
    first = x[0] + swap(x[1], 2)
    x = first
    for bit in bits()[2:]:
        x = x + swap(x, bit)
    x = jnp.stack([x, swap(x, 2)])
    return x, swap(x, 1), first


def body(features, centres, coefs, batch_index, targets):
    local_rows = batch_index.shape[1]
    devices = lax.axis_size("cen")
    batch_total = local_rows * devices
    outputs = coefs.shape[1]
    width = features.shape[1] * lax.axis_size("out")
    entries = centres.shape[0] * devices * outputs * lax.axis_size("out")
    pair = lax.axis_size("out") == 2
    sent = centres.shape[0] * SHARE[0] // SHARE[1] if pair else 0
    half = local_rows // 2
    chunks = [(0, 0, local_rows), (1, 0, half), (1, half, local_rows)]
    ranges = [(step * local_rows + a, step * local_rows + b) for step, a, b in chunks]

    place = 0
    for bit in bits():
        place = 2 * place + jnp.where(mine(bit), 1, 0)
    where = jnp.stack([place, 2 * jnp.where(mine(1), 1, 0) + jnp.where(mine(2), 1, 0)]).astype(jnp.int32)

    if pair:
        fetched = [across(centres[:BLOCK])]
        picked, more = take(features, centres, batch_index, BLOCK, sent)
        far = across(picked)
        fetched.append(across(more))
        own = gather(picked)
        far = gather(far)
    else:
        own = gather(take(features, centres, batch_index, 0, 0)[0])

    first = partial_squares(own, ranges[:1], centres, sent)
    partial = list(first) + list(partial_squares(own, ranges[1:], centres, sent, first))
    if pair:
        squares = [[x, across(x)] for x in partial]
        early = early_kernel(own, far, ranges, centres, fetched, width)
    else:
        squares = [[lax.psum(x, "out")] for x in partial]
        early = [None] * len(chunks)

    kerns, resids, results, sums = [[], []], [[], []], [], [None, None]
    gates = []
    for (step, a, b), near, square in zip(chunks, early, squares):
        kern, blocks = predict(where, near, square, coefs, targets[step, a:b], kerns[step], width, gates)
        summed, far_summed, gate = sum_cen(blocks)
        gates = [gate]
        resid, rows, sums[step] = settle(where, summed, far_summed, outputs, b - a, resids[step], sums[step])
        kerns[step].append(kern)
        resids[step].append(resid)
        results.append(rows)

    new_coefs = coefs
    for step in range(2):
        parts = [sums[step], across(sums[step])] if pair else [lax.psum(sums[step], "out")]
        new_coefs = update(new_coefs, kerns[step], resids[step], parts, batch_total, entries)
    return (jnp.stack([results[0], jnp.concatenate(results[1:])]), new_coefs)


def solution(mesh):
    placed = (
        P("cen", "out"),
        P("cen", "out"),
        P("cen", "out"),
        P(None, "cen"),
        P(None, "cen", "out"),
    )
    return jax.shard_map(
        body,
        mesh=mesh,
        in_specs=placed,
        out_specs=(P(None, "cen", "out"), P("cen", "out")),
        check_vma=False,
    )
```

time: 216 us -> 204 us (0.944)
  Pallas kernels: 0 us -> 68.7 us
  matrix products: 33.9 us -> 0 us
  other arithmetic: 24.3 us -> 1.59 us
  starting transfers between devices: 58.5 us -> 38.2 us
  between operations: 8.92 us -> 1.13 us
  waiting for transfers between devices: 75.8 us -> 78.4 us
    pallas_call x0 -> x12, Pallas kernels: none -> 68.7 us  [the longest x3 21.3 us: predict(): call(kernel, (steps,), specs, [pl.BlockSpec((rows, BLOCK), lambda i: (0,...]
    dot_general x10 -> x0, matrix products: 33.9 us -> none  [product(): lax.dot_general(left, right, (dims, ((), ())), precision=precision, prefe...]
    ppermute x36 -> x26, starting transfers between devices: 52.4 us -> 28.9 us  [swap(): return lax.ppermute(x, 'cen', [(i, i ^ bit) for i in range(n)])]
    ppermute x36 -> x26, waiting for transfers between devices: 28.1 us -> 42.6 us  [swap(): return lax.ppermute(x, 'cen', [(i, i ^ bit) for i in range(n)])]
    unnamed x18 -> x8, local copies, waits for them, and re-layouts: 0.73 us -> 13.5 us
    ppermute x6 -> x8, waiting for transfers between devices: 47.7 us -> 35.8 us  [across(): return lax.ppermute(x, 'out', [(0, 1), (1, 0)])]
    sub x2 -> x0, other arithmetic: 8.47 us -> none  [the longest x1 8.45 us: body(): new_coefs = new_coefs - 0.1 * grad / scale]
    slice x12 -> x4, local copies, waits for them, and re-layouts: 6.8 us -> 1.13 us  [the longest x1 1.08 us: body(): fetched = [across(centres[:BLOCK])]]
  transfers between devices with their start and end apart: 42 -> 34, of which waited for: 19 -> 19; matrix products, arithmetic and copies ran while one was open for 27% -> 4% of each run, Pallas kernels for 0% -> 21%
where the time goes in v2:
time: 204 us; the launch traced here: 203 us
  waiting for transfers between devices  78.4 us (38%)
  Pallas kernels  68.7 us (34%)
  starting transfers between devices  38.2 us (19%)
  local copies, waits for them, and re-layouts  14.7 us (7%)
    ppermute x26, waiting for transfers between devices, swap(): return lax.ppermute(x, 'cen', [(i, i ^ bit) for i in range(n)])  42.6 us
    ppermute x8, waiting for transfers between devices, across(): return lax.ppermute(x, 'out', [(0, 1), (1, 0)])  35.8 us
    ppermute x26, starting transfers between devices, swap(): return lax.ppermute(x, 'cen', [(i, i ^ bit) for i in range(n)])  28.9 us
    pallas_call x3, Pallas kernels, predict(): call(kernel, (steps,), specs, [pl.BlockSpec((rows, BLOCK), lambda i: (0,...  21.3 us
    pallas_call x2, Pallas kernels, update(): call(kernel, (centres // BLOCK,), [block] + [pl.BlockSpec((x.shape[0], BL...  16.9 us
    pallas_call x1, Pallas kernels, early_kernel(): call(kernel, (starts[-1],), [whole(own), whole(far), pl.BlockSpec((BLOCK,...  13.9 us
    unnamed x8, local copies, waits for them, and re-layouts  13.5 us
    pallas_call x2, Pallas kernels, partial_squares(): call(kernel, (late // BLOCK,), [whole(own), pl.BlockSpec((BLOCK, own.shap...  10.8 us
  transfers between devices with their start and end apart: 34, of which 19 were waited for; matrix products, arithmetic and copies ran while one was open for 4% of the time, Pallas kernels for 21%

profile of v2, /device:TPU:0, one launch (start us, length us, event | category | flops | bytes accessed | tf_op | source)
XLA Modules:
  0.0 202.8 jit_solution(12171468419096398770)
XLA Ops:
  0.6 2.2 %copy-done = f32[2048,512]{1,0:T(8,128)S(1)} copy-done((f32[2048,512]{1,0:T(8,128)S(1)}, f32[2048,512]{1,0:T(8,128)}, u32[]{:S(2)}) %copy-start) | copy-done | bytes 4194328
  2.8 0.7 copy-done.1
  3.5 2.3 %shard_map.68 = (f32[32,512]{1,0:T(8,128)S(1)}, f32[768,512]{1,0:T(8,128)S(1)}) custom-call(s32[2,16]{1,0:T(2,128)S(1)} %copy-done.1, f32[2048,512]{1,0:T(8,128)S(1)} %copy-done, f32[2048,512]{1,0:T(8,128)} %centre_ref.5), custom_call_target="tpu_custom_call" | custom-call | bytes 1638400 | tf_op jit(solution)/shard_map/pallas_call | solution.py:85
  5.8 4.1 %collective-permute-start = (f32[32,512]{1,0:T(8,128)S(1)}, f32[32,512]{1,0:T(8,128)S(1)}, u32[]{:S(2)}, u32[]{:S(2)}) collective-permute-start(f32[32,512]{1,0:T(8,128)S(1)} %get-tuple-element.24), channel_id=1, source_target_pairs={{0,16},{2,18},{4,20},{6,22},{8,24},{10,26},{12,28},{14,30},{16,0},... | collective-permute-start | bytes 196616 | tf_op jit(solution)/shard_map/ppermute | solution.py:307
  9.9 1.5 collective-permute-start.4
  11.4 1.1 slice.48
  12.5 0.6 collective-permute-start.9
  13.1 1.5 collective-permute-start.10
  14.6 5.3 %copy.7.rest_3_.coefs_ref = f32[2048,500]{1,0:T(8,128)} copy(f32[2048,500]{0,1:T(8,128)} %param.7) | data formatting | bytes 8192000 | tf_op args[2]
  20.0 1.6 collective-permute-start.1
  21.6 0.4 collective-permute-start.5
  22.0 5.4 %collective-permute-done.5 = f32[32,512]{1,0:T(8,128)S(1)} collective-permute-done((f32[32,512]{1,0:T(8,128)S(1)}, f32[32,512]{1,0:T(8,128)S(1)}, u32[]{:S(2)}, u32[]{:S(2)}) %collective-permute-start.5) | collective-permute-done | bytes 65568 | tf_op jit(solution)/shard_map/ppermute | solution.py:307
  27.6 1.6 collective-permute-start.2
  29.2 4.8 %collective-permute-done.2 = f32[2,2,32,512]{3,2,1,0:T(8,128)S(1)} collective-permute-done((f32[2,2,32,512]{3,2,1,0:T(8,128)S(1)}, f32[2,2,32,512]{3,2,1,0:T(8,128)S(1)}, u32[]{:S(2)}, u32[]{:S(2)}) %collective-permute-start.2) | collective-permute-done | bytes 262176 | tf_op jit(solution)/shard_map/ppermute | solution.py:307
  34.2 1.6 collective-permute-start.7
  35.9 7.1 %collective-permute-done.7 = f32[2,2,32,512]{3,2,1,0:T(8,128)S(1)} collective-permute-done((f32[2,2,32,512]{3,2,1,0:T(8,128)S(1)}, f32[2,2,32,512]{3,2,1,0:T(8,128)S(1)}, u32[]{:S(2)}, u32[]{:S(2)}) %collective-permute-start.7) | collective-permute-done | bytes 262176 | tf_op jit(solution)/shard_map/ppermute | solution.py:307
  43.0 0.1 collective-permute-start.8
  43.1 0.1 maximum_select_fusion
  43.2 5.4 %shard_map.70.rest_1_.rest_0_ = f32[256,1024]{1,0:T(8,128)S(1)} custom-call(f32[16,32,512]{2,1,0:T(8,128)S(1)} %bitcast.63, f32[2048,512]{1,0:T(8,128)} %centre_ref.5), custom_call_target="tpu_custom_call" | custom-call | flops 1610612736 | bytes 3145728 | tf_op jit(solution)/shard_map/pallas_call | solution.py:120
  48.6 0.6 collective-permute-start.11
  49.2 0.1 pad_add_fusion.where_ref
  49.4 0.1 maximum_select_fusion.1
  49.5 11.8 %collective-permute-done.10.rest_1_ = f32[768,512]{1,0:T(8,128)} collective-permute-done((f32[768,512]{1,0:T(8,128)S(1)}, f32[768,512]{1,0:T(8,128)}, u32[]{:S(2)}, u32[]{:S(2)}) %collective-permute-start.10) | collective-permute-done | bytes 1572896 | tf_op jit(solution)/shard_map/ppermute | solution.py:311
  61.2 13.9 %shard_map.69 = (f32[256,1024]{1,0:T(8,128)S(1)}, f32[128,1024]{1,0:T(8,128)S(1)}, f32[128,1024]{1,0:T(8,128)S(1)}) custom-call(f32[16,32,512]{2,1,0:T(8,128)S(1)} %bitcast.64, f32[16,32,512]{2,1,0:T(8,128)S(1)} %bitcast.66, f32[2048,512]{1,0:T(8,128)} %centre_ref.5, f32[256,512]{1,0:T(8,128)S(1)} %collective-permute-done.9.rest_0_, ...), custom_call_target="tpu_custom_call" | custom-call | flops 6442450944 | bytes 6291456 | tf_op jit(solution)/shard_map/pallas_call | solution.py:158
  75.1 6.7 %collective-permute-done.11.rest_2_ = f32[256,1024]{1,0:T(8,128)S(1)} collective-permute-done((f32[256,1024]{1,0:T(8,128)S(1)}, f32[256,1024]{1,0:T(8,128)S(1)}, u32[]{:S(2)}, u32[]{:S(2)}) %collective-permute-start.11) | collective-permute-done | bytes 1048608 | tf_op jit(solution)/shard_map/ppermute | solution.py:311
  81.8 7.7 %shard_map.71 = (f32[256,2048]{1,0:T(8,128)S(1)}, f32[4,64,768]{2,1,0:T(8,128)S(1)}) custom-call(s32[2]{0:T(128)S(1)} %pad_add_fusion.where_ref, f32[256,1024]{1,0:T(8,128)S(1)} %get-tuple-element.26.rest_0_, f32[256,1024]{1,0:T(8,128)S(1)} %shard_map.70.rest_1_.rest_0_, f32[256,1024]{1,0:T(8,128)S(1)} %collective-permute-done.11.rest_2_, ...), custom_call_target="tpu_custom_call" | custom-call | flops 2415919104 | bytes 10387456 | tf_op jit(solution)/shard_map/pallas_call | solution.py:234
  89.6 5.4 %shard_map.73 = (f32[128,1024]{1,0:T(8,128)S(1)}, f32[128,1024]{1,0:T(8,128)S(1)}) custom-call(f32[16,32,512]{2,1,0:T(8,128)S(1)} %bitcast.65, f32[2048,512]{1,0:T(8,128)} %centre_ref.5, f32[256,1024]{1,0:T(8,128)S(1)} %shard_map.70.rest_1_.rest_0_), custom_call_target="tpu_custom_call" | custom-call | flops 1610612736 | bytes 3145728 | tf_op jit(solution)/shard_map/pallas_call | solution.py:120
  95.0 1.3 collective-permute-start.18
  96.4 1.6 collective-permute-start.13
  98.0 5.5 %collective-permute-done.13 = f32[64,768]{1,0:T(8,128)S(1)} collective-permute-done((f32[64,768]{1,0:T(8,128)S(1)}, f32[64,768]{1,0:T(8,128)S(1)}, u32[]{:S(2)}, u32[]{:S(2)}) %collective-permute-start.13) | collective-permute-done | bytes 196640 | tf_op jit(solution)/shard_map/ppermute | solution.py:307
  103.5 5.9 %collective-permute-done.18.rest_2_ = f32[128,1024]{1,0:T(8,128)S(1)} collective-permute-done((f32[128,1024]{1,0:T(8,128)S(1)}, f32[128,1024]{1,0:T(8,128)S(1)}, u32[]{:S(2)}, u32[]{:S(2)}) %collective-permute-start.18) | collective-permute-done | bytes 524320 | tf_op jit(solution)/shard_map/ppermute | solution.py:311
  109.4 6.7 %shard_map.74 = (f32[128,2048]{1,0:T(8,128)S(1)}, f32[4,32,640]{2,1,0:T(8,128)S(1)}) custom-call(s32[2]{0:T(128)S(1)} %pad_add_fusion.where_ref, f32[128,1024]{1,0:T(8,128)S(1)} %get-tuple-element.29.rest_0_, f32[128,1024]{1,0:T(8,128)S(1)} %get-tuple-element.30.rest_1_, f32[128,1024]{1,0:T(8,128)S(1)} %collective-permute-done.18.rest_2_, ...), custom_call_target="tpu_custom_call" | custom-call | flops 1006632960 | bytes 7241728 | tf_op jit(solution)/shard_map/pallas_call | solution.py:234
  116.2 1.3 collective-permute-start.25
  117.5 0.1 collective-permute-done.19
  117.6 1.6 collective-permute-start.20
  119.2 1.6 collective-permute-start.14
  120.7 1.4 collective-permute-done.20
  122.2 8.3 %collective-permute-done.25.rest_2_ = f32[128,1024]{1,0:T(8,128)S(1)} collective-permute-done((f32[128,1024]{1,0:T(8,128)S(1)}, f32[128,1024]{1,0:T(8,128)S(1)}, u32[]{:S(2)}, u32[]{:S(2)}) %collective-permute-start.25) | collective-permute-done | bytes 524320 | tf_op jit(solution)/shard_map/ppermute | solution.py:311
  130.5 7.0 %shard_map.76 = (f32[128,2048]{1,0:T(8,128)S(1)}, f32[4,32,768]{2,1,0:T(8,128)S(1)}) custom-call(s32[2]{0:T(128)S(1)} %pad_add_fusion.where_ref, f32[128,1024]{1,0:T(8,128)S(1)} %get-tuple-element.33.rest_0_, f32[128,1024]{1,0:T(8,128)S(1)} %get-tuple-element.34.rest_1_, f32[128,1024]{1,0:T(8,128)S(1)} %collective-permute-done.25.rest_2_, ...), custom_call_target="tpu_custom_call" | custom-call | flops 1207959552 | bytes 7241728 | tf_op jit(solution)/shard_map/pallas_call | solution.py:234
  137.6 0.4 collective-permute-start.15
  138.0 1.0 collective-permute-done.26
  139.1 1.6 collective-permute-start.27
  140.7 1.5 collective-permute-start.21
  142.2 2.9 %collective-permute-done.21 = f32[32,640]{1,0:T(8,128)S(1)} collective-permute-done((f32[32,640]{1,0:T(8,128)S(1)}, f32[32,640]{1,0:T(8,128)S(1)}, u32[]{:S(2)}, u32[]{:S(2)}) %collective-permute-start.21) | collective-permute-done | bytes 81952 | tf_op jit(solution)/shard_map/ppermute | solution.py:307
  145.1 5.8 %collective-permute-start.22 = (f32[32,640]{1,0:T(8,128)S(1)}, f32[32,640]{1,0:T(8,128)S(1)}, u32[]{:S(2)}, u32[]{:S(2)}) collective-permute-start(f32[32,640]{1,0:T(8,128)S(1)} %add.55), channel_id=1, source_target_pairs={{0,16},{2,18},{4,20},{6,22},{8,24},{10,26},{12,28},{14,30},{16,0},... | collective-permute-start | bytes 245768 | tf_op jit(solution)/shard_map/ppermute | solution.py:307
  150.9 0.3 collective-permute-done.15
  151.2 2.5 %collective-permute-start.16 = (f32[64,768]{1,0:T(8,128)S(1)}, f32[64,768]{1,0:T(8,128)S(1)}, u32[]{:S(2)}, u32[]{:S(2)}) collective-permute-start(f32[64,768]{1,0:T(8,128)S(1)} %add.52), channel_id=1, source_target_pairs={{0,4},{2,6},{4,0},{6,2},{8,12},{10,14},{12,8},{14,10},{16,20},{18,... | collective-permute-start | bytes 589832 | tf_op jit(solution)/shard_map/ppermute | solution.py:307
  153.8 3.6 %collective-permute-done.16 = f32[64,768]{1,0:T(8,128)S(1)} collective-permute-done((f32[64,768]{1,0:T(8,128)S(1)}, f32[64,768]{1,0:T(8,128)S(1)}, u32[]{:S(2)}, u32[]{:S(2)}) %collective-permute-start.16) | collective-permute-done | bytes 196640 | tf_op jit(solution)/shard_map/ppermute | solution.py:307
  157.4 0.9 collective-permute-done.28
  158.5 1.2 collective-permute-start.23
  159.6 6.2 %collective-permute-done.29 = f32[32,768]{1,0:T(8,128)S(1)} collective-permute-done((f32[32,768]{1,0:T(8,128)S(1)}, f32[32,768]{1,0:T(8,128)S(1)}, u32[]{:S(2)}, u32[]{:S(2)}) %collective-permute-start.29) | collective-permute-done | bytes 98336 | tf_op jit(solution)/shard_map/ppermute | solution.py:307
  165.9 1.1 collective-permute-start.30
  167.1 3.5 %collective-permute-done.30 = f32[32,768]{1,0:T(8,128)S(1)} collective-permute-done((f32[32,768]{1,0:T(8,128)S(1)}, f32[32,768]{1,0:T(8,128)S(1)}, u32[]{:S(2)}, u32[]{:S(2)}) %collective-permute-start.30) | collective-permute-done | bytes 98336 | tf_op jit(solution)/shard_map/ppermute | solution.py:307
  170.7 1.3 shard_map.72
  172.0 1.3 collective-permute-start.32
  173.3 1.1 shard_map.75
  174.4 1.3 collective-permute-done.32.rest_3_
  175.7 8.1 %shard_map.78.coefs_ref = f32[2048,500]{1,0:T(8,128)} custom-call(f32[2048,500]{1,0:T(8,128)} %copy.7.rest_3_.coefs_ref, f32[256,2048]{1,0:T(8,128)S(1)} %get-tuple-element.40.rest_0_, f32[256,500]{1,0:T(8,128)S(1)} %get-tuple-element.41.rest_1_, f32[8,128]{1,0:T(8,128)S(1)} %get-tuple-element.42.rest_2_, f32[8,128]{1,0:T(8,128)S(1)} %collective-permute-done.32.rest_3_), custom_call_target="tpu_custom_call" | custom-call | flops 1572864000 | bytes 10289152 | tf_op jit(solution)/shard_map/pallas_call | solution.py:297
  183.7 1.3 shard_map.77
  185.0 1.3 collective-permute-start.33
  186.3 0.6 pad_maximum_fusion.3
  187.0 1.7 collective-permute-done.33.rest_5_
  188.7 8.8 %shard_map.79 = f32[2048,500]{1,0:T(8,128)} custom-call(f32[2048,500]{1,0:T(8,128)} %shard_map.78.coefs_ref, f32[128,2048]{1,0:T(8,128)S(1)} %get-tuple-element.35.rest_5_.rest_0_, f32[128,2048]{1,0:T(8,128)S(1)} %get-tuple-element.43.rest_1_, f32[128,500]{1,0:T(8,128)S(1)} %get-tuple-element.37.rest_0_.rest_2_, f32[128,500]{1,0:T(8,128)S(1)} %get-tuple-element.44.rest_3_, ...), custom_call_target="tpu_custom_call" | custom-call | flops 1572864000 | bytes 10289152 | tf_op jit(solution)/shard_map/pallas_call | solution.py:297
  197.5 5.3 %copy.11 = f32[2048,500]{0,1:T(8,128)} copy(f32[2048,500]{1,0:T(8,128)} %shard_map.79) | data formatting | bytes 8192000
  (69 shorter events, 1.5 us)
Async XLA Ops:
  0.6 2.2 %copy-start = (f32[2048,512]{1,0:T(8,128)S(1)}, f32[2048,512]{1,0:T(8,128)}, u32[]{:S(2)}) copy-start(f32[2048,512]{1,0:T(8,128)} %table.1) | copy-start | bytes 12582916
  2.8 0.7 copy-start.1
  3.5 11.1 %copy-start.2 = (f32[2,16,500]{2,1,0:T(8,128)S(1)}, f32[2,16,500]{2,1,0:T(8,128)}, u32[]{:S(2)}) copy-start(f32[2,16,500]{2,1,0:T(8,128)} %param.9) | copy-start | bytes 192004
  5.8 14.1 %collective-permute-start = (f32[32,512]{1,0:T(8,128)S(1)}, f32[32,512]{1,0:T(8,128)S(1)}, u32[]{:S(2)}, u32[]{:S(2)}) collective-permute-start(f32[32,512]{1,0:T(8,128)S(1)} %get-tuple-element.24), channel_id=1, source_target_pairs={{0,16},{2,18},{4,20},{6,22},{8,24},{10,26},{12,28},{14,30},{16,0},... | collective-permute-start | bytes 196616 | tf_op jit(solution)/shard_map/ppermute | solution.py:307
  9.9 11.7 %collective-permute-start.4 = (f32[32,512]{1,0:T(8,128)S(1)}, f32[32,512]{1,0:T(8,128)S(1)}, u32[]{:S(2)}, u32[]{:S(2)}) collective-permute-start(f32[32,512]{1,0:T(8,128)S(1)} %get-tuple-element.24), channel_id=1, source_target_pairs={{0,1},{1,0},{2,3},{3,2},{4,5},{5,4},{6,7},{7,6},{8,9},{9,8},{10,11... | collective-permute-start | bytes 196616 | tf_op jit(solution)/shard_map/ppermute | solution.py:311
  12.5 37.0 %collective-permute-start.9 = (f32[256,512]{1,0:T(8,128)S(1)}, f32[256,512]{1,0:T(8,128)S(1)}, u32[]{:S(2)}, u32[]{:S(2)}) collective-permute-start(f32[256,512]{1,0:T(8,128)S(1)} %slice.48), channel_id=1, source_target_pairs={{0,1},{1,0},{2,3},{3,2},{4,5},{5,4},{6,7},{7,6},{8,9},{9,8},{10,11... | collective-permute-start | bytes 1572872 | tf_op jit(solution)/shard_map/ppermute | solution.py:311
  13.1 48.1 %collective-permute-start.10 = (f32[768,512]{1,0:T(8,128)S(1)}, f32[768,512]{1,0:T(8,128)}, u32[]{:S(2)}, u32[]{:S(2)}) collective-permute-start(f32[768,512]{1,0:T(8,128)S(1)} %get-tuple-element.25), channel_id=1, source_target_pairs={{0,1},{1,0},{2,3},{3,2},{4,5},{5,4},{6,7},{7,6},{8,9},{9,8},{10,11... | collective-permute-start | bytes 4718600 | tf_op jit(solution)/shard_map/ppermute | solution.py:311
  20.0 7.6 %collective-permute-start.1 = (f32[2,32,512]{2,1,0:T(8,128)S(1)}, f32[2,32,512]{2,1,0:T(8,128)S(1)}, u32[]{:S(2)}, u32[]{:S(2)}) collective-permute-start(f32[2,32,512]{2,1,0:T(8,128)S(1)} %maximum_select_fusion.10), channel_id=1, source_target_pairs={{0,8},{2,10},{4,12},{6,14},{8,0},{10,2},{12,4},{14,6},{16,24},{18,... | collective-permute-start | bytes 393224 | tf_op jit(solution)/shard_map/ppermute | solution.py:307
  21.6 5.8 %collective-permute-start.5 = (f32[32,512]{1,0:T(8,128)S(1)}, f32[32,512]{1,0:T(8,128)S(1)}, u32[]{:S(2)}, u32[]{:S(2)}) collective-permute-start(f32[32,512]{1,0:T(8,128)S(1)} %collective-permute-done.4), channel_id=1, source_target_pairs={{0,16},{2,18},{4,20},{6,22},{8,24},{10,26},{12,28},{14,30},{16,0},... | collective-permute-start | bytes 196616 | tf_op jit(solution)/shard_map/ppermute | solution.py:307
  27.5 6.7 %collective-permute-start.6 = (f32[2,32,512]{2,1,0:T(8,128)S(1)}, f32[2,32,512]{2,1,0:T(8,128)S(1)}, u32[]{:S(2)}, u32[]{:S(2)}) collective-permute-start(f32[2,32,512]{2,1,0:T(8,128)S(1)} %maximum_select_fusion.12), channel_id=1, source_target_pairs={{0,8},{2,10},{4,12},{6,14},{8,0},{10,2},{12,4},{14,6},{16,24},{18,... | collective-permute-start | bytes 393224 | tf_op jit(solution)/shard_map/ppermute | solution.py:307
  27.6 6.4 %collective-permute-start.2 = (f32[2,2,32,512]{3,2,1,0:T(8,128)S(1)}, f32[2,2,32,512]{3,2,1,0:T(8,128)S(1)}, u32[]{:S(2)}, u32[]{:S(2)}) collective-permute-start(f32[2,2,32,512]{3,2,1,0:T(8,128)S(1)} %maximum_select_fusion.6), channel_id=1, source_target_pairs={{0,4},{2,6},{4,0},{6,2},{8,12},{10,14},{12,8},{14,10},{16,20},{18,... | collective-permute-start | bytes 786440 | tf_op jit(solution)/shard_map/ppermute | solution.py:307
  34.1 9.0 %collective-permute-start.3 = (f32[2,2,2,32,512]{4,3,2,1,0:T(8,128)S(1)}, f32[2,2,2,32,512]{4,3,2,1,0:T(8,128)S(1)}, u32[]{:S(2)}, u32[]{:S(2)}) collective-permute-start(f32[2,2,2,32,512]{4,3,2,1,0:T(8,128)S(1)} %maximum_select_fusion.2), channel_id=1, source_target_pairs={{0,2},{2,0},{4,6},{6,4},{8,10},{10,8},{12,14},{14,12},{16,18},{18,... | collective-permute-start | bytes 1572872 | tf_op jit(solution)/shard_map/ppermute | solution.py:307
  34.2 8.8 %collective-permute-start.7 = (f32[2,2,32,512]{3,2,1,0:T(8,128)S(1)}, f32[2,2,32,512]{3,2,1,0:T(8,128)S(1)}, u32[]{:S(2)}, u32[]{:S(2)}) collective-permute-start(f32[2,2,32,512]{3,2,1,0:T(8,128)S(1)} %maximum_select_fusion.8), channel_id=1, source_target_pairs={{0,4},{2,6},{4,0},{6,2},{8,12},{10,14},{12,8},{14,10},{16,20},{18,... | collective-permute-start | bytes 786440 | tf_op jit(solution)/shard_map/ppermute | solution.py:307
  43.0 6.3 %collective-permute-start.8 = (f32[2,2,2,32,512]{4,3,2,1,0:T(8,128)S(1)}, f32[2,2,2,32,512]{4,3,2,1,0:T(8,128)S(1)}, u32[]{:S(2)}, u32[]{:S(2)}) collective-permute-start(f32[2,2,2,32,512]{4,3,2,1,0:T(8,128)S(1)} %maximum_select_fusion.4), channel_id=1, source_target_pairs={{0,2},{2,0},{4,6},{6,4},{8,10},{10,8},{12,14},{14,12},{16,18},{18,... | collective-permute-start | bytes 1572872 | tf_op jit(solution)/shard_map/ppermute | solution.py:307
  48.6 33.3 %collective-permute-start.11 = (f32[256,1024]{1,0:T(8,128)S(1)}, f32[256,1024]{1,0:T(8,128)S(1)}, u32[]{:S(2)}, u32[]{:S(2)}) collective-permute-start(f32[256,1024]{1,0:T(8,128)S(1)} %shard_map.70.rest_1_.rest_0_), channel_id=1, source_target_pairs={{0,1},{1,0},{2,3},{3,2},{4,5},{5,4},{6,7},{7,6},{8,9},{9,8},{10,11... | collective-permute-start | bytes 3145736 | tf_op jit(solution)/shard_map/ppermute | solution.py:311
  89.5 6.8 %collective-permute-start.12 = (f32[2,64,768]{2,1,0:T(8,128)S(1)}, f32[2,64,768]{2,1,0:T(8,128)S(1)}, u32[]{:S(2)}, u32[]{:S(2)}) collective-permute-start(f32[2,64,768]{2,1,0:T(8,128)S(1)} %slice.51), channel_id=1, source_target_pairs={{0,2},{2,0},{4,6},{6,4},{8,10},{10,8},{12,14},{14,12},{16,18},{18,... | collective-permute-start | bytes 1179656 | tf_op jit(solution)/shard_map/ppermute | solution.py:307
  95.0 14.4 %collective-permute-start.18 = (f32[128,1024]{1,0:T(8,128)S(1)}, f32[128,1024]{1,0:T(8,128)S(1)}, u32[]{:S(2)}, u32[]{:S(2)}) collective-permute-start(f32[128,1024]{1,0:T(8,128)S(1)} %get-tuple-element.30.rest_1_), channel_id=1, source_target_pairs={{0,1},{1,0},{2,3},{3,2},{4,5},{5,4},{6,7},{7,6},{8,9},{9,8},{10,11... | collective-permute-start | bytes 1572872 | tf_op jit(solution)/shard_map/ppermute | solution.py:311
  96.4 7.1 %collective-permute-start.13 = (f32[64,768]{1,0:T(8,128)S(1)}, f32[64,768]{1,0:T(8,128)S(1)}, u32[]{:S(2)}, u32[]{:S(2)}) collective-permute-start(f32[64,768]{1,0:T(8,128)S(1)} %slice_bitcast_fusion), channel_id=1, source_target_pairs={{0,4},{2,6},{4,0},{6,2},{8,12},{10,14},{12,8},{14,10},{16,20},{18,... | collective-permute-start | bytes 589832 | tf_op jit(solution)/shard_map/ppermute | solution.py:307
  116.1 1.5 collective-permute-start.19
  116.2 14.3 %collective-permute-start.25 = (f32[128,1024]{1,0:T(8,128)S(1)}, f32[128,1024]{1,0:T(8,128)S(1)}, u32[]{:S(2)}, u32[]{:S(2)}) collective-permute-start(f32[128,1024]{1,0:T(8,128)S(1)} %get-tuple-element.34.rest_1_), channel_id=1, source_target_pairs={{0,1},{1,0},{2,3},{3,2},{4,5},{5,4},{6,7},{7,6},{8,9},{9,8},{10,11... | collective-permute-start | bytes 1572872 | tf_op jit(solution)/shard_map/ppermute | solution.py:311
  117.6 4.6 %collective-permute-start.20 = (f32[32,640]{1,0:T(8,128)S(1)}, f32[32,640]{1,0:T(8,128)S(1)}, u32[]{:S(2)}, u32[]{:S(2)}) collective-permute-start(f32[32,640]{1,0:T(8,128)S(1)} %slice_bitcast_fusion.4), channel_id=1, source_target_pairs={{0,4},{2,6},{4,0},{6,2},{8,12},{10,14},{12,8},{14,10},{16,20},{18,... | collective-permute-start | bytes 245768 | tf_op jit(solution)/shard_map/ppermute | solution.py:307
  119.2 18.4 %collective-permute-start.14 = (f32[64,768]{1,0:T(8,128)S(1)}, f32[64,768]{1,0:T(8,128)S(1)}, u32[]{:S(2)}, u32[]{:S(2)}) collective-permute-start(f32[64,768]{1,0:T(8,128)S(1)} %fusion.rest_5_), channel_id=1, source_target_pairs={{0,8},{2,10},{4,12},{6,14},{8,0},{10,2},{12,4},{14,6},{16,24},{18,... | collective-permute-start | bytes 589832 | tf_op jit(solution)/shard_map/ppermute | solution.py:307
  137.5 1.5 collective-permute-start.26
  137.6 13.5 %collective-permute-start.15 = (f32[64,768]{1,0:T(8,128)S(1)}, f32[64,768]{1,0:T(8,128)S(1)}, u32[]{:S(2)}, u32[]{:S(2)}) collective-permute-start(f32[64,768]{1,0:T(8,128)S(1)} %add.51), channel_id=1, source_target_pairs={{0,16},{2,18},{4,20},{6,22},{8,24},{10,26},{12,28},{14,30},{16,0},... | collective-permute-start | bytes 589832 | tf_op jit(solution)/shard_map/ppermute | solution.py:307
  139.1 14.6 %collective-permute-start.27 = (f32[32,768]{1,0:T(8,128)S(1)}, f32[32,768]{1,0:T(8,128)S(1)}, u32[]{:S(2)}, u32[]{:S(2)}) collective-permute-start(f32[32,768]{1,0:T(8,128)S(1)} %slice_bitcast_fusion.2), channel_id=1, source_target_pairs={{0,4},{2,6},{4,0},{6,2},{8,12},{10,14},{12,8},{14,10},{16,20},{18,... | collective-permute-start | bytes 294920 | tf_op jit(solution)/shard_map/ppermute | solution.py:307
  140.7 4.4 %collective-permute-start.21 = (f32[32,640]{1,0:T(8,128)S(1)}, f32[32,640]{1,0:T(8,128)S(1)}, u32[]{:S(2)}, u32[]{:S(2)}) collective-permute-start(f32[32,640]{1,0:T(8,128)S(1)} %fusion.2.rest_6_), channel_id=1, source_target_pairs={{0,8},{2,10},{4,12},{6,14},{8,0},{10,2},{12,4},{14,6},{16,24},{18,... | collective-permute-start | bytes 245768 | tf_op jit(solution)/shard_map/ppermute | solution.py:307
  145.1 13.3 %collective-permute-start.22 = (f32[32,640]{1,0:T(8,128)S(1)}, f32[32,640]{1,0:T(8,128)S(1)}, u32[]{:S(2)}, u32[]{:S(2)}) collective-permute-start(f32[32,640]{1,0:T(8,128)S(1)} %add.55), channel_id=1, source_target_pairs={{0,16},{2,18},{4,20},{6,22},{8,24},{10,26},{12,28},{14,30},{16,0},... | collective-permute-start | bytes 245768 | tf_op jit(solution)/shard_map/ppermute | solution.py:307
  151.2 6.1 %collective-permute-start.16 = (f32[64,768]{1,0:T(8,128)S(1)}, f32[64,768]{1,0:T(8,128)S(1)}, u32[]{:S(2)}, u32[]{:S(2)}) collective-permute-start(f32[64,768]{1,0:T(8,128)S(1)} %add.52), channel_id=1, source_target_pairs={{0,4},{2,6},{4,0},{6,2},{8,12},{10,14},{12,8},{14,10},{16,20},{18,... | collective-permute-start | bytes 589832 | tf_op jit(solution)/shard_map/ppermute | solution.py:307
  153.7 4.7 %collective-permute-start.28 = (f32[32,768]{1,0:T(8,128)S(1)}, f32[32,768]{1,0:T(8,128)S(1)}, u32[]{:S(2)}, u32[]{:S(2)}) collective-permute-start(f32[32,768]{1,0:T(8,128)S(1)} %fusion.1), channel_id=1, source_target_pairs={{0,8},{2,10},{4,12},{6,14},{8,0},{10,2},{12,4},{14,6},{16,24},{18,... | collective-permute-start | bytes 294920 | tf_op jit(solution)/shard_map/ppermute | solution.py:307
  157.3 13.3 %collective-permute-start.17 = (f32[2,64,768]{2,1,0:T(8,128)S(1)}, f32[2,64,768]{2,1,0:T(8,128)S(1)}, u32[]{:S(2)}, u32[]{:S(2)}) collective-permute-start(f32[2,64,768]{2,1,0:T(8,128)S(1)} %pad_maximum_fusion.near_ref), channel_id=1, source_target_pairs={{0,2},{2,0},{4,6},{6,4},{8,10},{10,8},{12,14},{14,12},{16,18},{18,... | collective-permute-start | bytes 1179656 | tf_op jit(solution)/shard_map/ppermute | solution.py:307
  158.4 7.5 %collective-permute-start.29 = (f32[32,768]{1,0:T(8,128)S(1)}, f32[32,768]{1,0:T(8,128)S(1)}, u32[]{:S(2)}, u32[]{:S(2)}) collective-permute-start(f32[32,768]{1,0:T(8,128)S(1)} %add.59), channel_id=1, source_target_pairs={{0,16},{2,18},{4,20},{6,22},{8,24},{10,26},{12,28},{14,30},{16,0},... | collective-permute-start | bytes 294920 | tf_op jit(solution)/shard_map/ppermute | solution.py:307
  158.5 8.5 %collective-permute-start.23 = (f32[32,640]{1,0:T(8,128)S(1)}, f32[32,640]{1,0:T(8,128)S(1)}, u32[]{:S(2)}, u32[]{:S(2)}) collective-permute-start(f32[32,640]{1,0:T(8,128)S(1)} %add.56), channel_id=1, source_target_pairs={{0,4},{2,6},{4,0},{6,2},{8,12},{10,14},{12,8},{14,10},{16,20},{18,... | collective-permute-start | bytes 245768 | tf_op jit(solution)/shard_map/ppermute | solution.py:307
  165.9 4.7 %collective-permute-start.30 = (f32[32,768]{1,0:T(8,128)S(1)}, f32[32,768]{1,0:T(8,128)S(1)}, u32[]{:S(2)}, u32[]{:S(2)}) collective-permute-start(f32[32,768]{1,0:T(8,128)S(1)} %add.60), channel_id=1, source_target_pairs={{0,4},{2,6},{4,0},{6,2},{8,12},{10,14},{12,8},{14,10},{16,20},{18,... | collective-permute-start | bytes 294920 | tf_op jit(solution)/shard_map/ppermute | solution.py:307
  167.0 6.3 %collective-permute-start.24 = (f32[2,32,640]{2,1,0:T(8,128)S(1)}, f32[2,32,640]{2,1,0:T(8,128)S(1)}, u32[]{:S(2)}, u32[]{:S(2)}) collective-permute-start(f32[2,32,640]{2,1,0:T(8,128)S(1)} %pad_maximum_fusion.2.near_ref), channel_id=1, source_target_pairs={{0,2},{2,0},{4,6},{6,4},{8,10},{10,8},{12,14},{14,12},{16,18},{18,... | collective-permute-start | bytes 491528 | tf_op jit(solution)/shard_map/ppermute | solution.py:307
  170.6 13.2 %collective-permute-start.31 = (f32[2,32,768]{2,1,0:T(8,128)S(1)}, f32[2,32,768]{2,1,0:T(8,128)S(1)}, u32[]{:S(2)}, u32[]{:S(2)}) collective-permute-start(f32[2,32,768]{2,1,0:T(8,128)S(1)} %pad_maximum_fusion.1.near_ref), channel_id=1, source_target_pairs={{0,2},{2,0},{4,6},{6,4},{8,10},{10,8},{12,14},{14,12},{16,18},{18,... | collective-permute-start | bytes 589832 | tf_op jit(solution)/shard_map/ppermute | solution.py:307
  172.0 3.7 %collective-permute-start.32 = (f32[8,128]{1,0:T(8,128)S(1)}, f32[8,128]{1,0:T(8,128)S(1)}, u32[]{:S(2)}, u32[]{:S(2)}) collective-permute-start(f32[8,128]{1,0:T(8,128)S(1)} %get-tuple-element.42.rest_2_), channel_id=1, source_target_pairs={{0,1},{1,0},{2,3},{3,2},{4,5},{5,4},{6,7},{7,6},{8,9},{9,8},{10,11... | collective-permute-start | bytes 12296 | tf_op jit(solution)/shard_map/ppermute | solution.py:311
  185.0 3.7 %collective-permute-start.33 = (f32[8,128]{1,0:T(8,128)S(1)}, f32[8,128]{1,0:T(8,128)S(1)}, u32[]{:S(2)}, u32[]{:S(2)}) collective-permute-start(f32[8,128]{1,0:T(8,128)S(1)} %get-tuple-element.45.rest_4_), channel_id=1, source_target_pairs={{0,1},{1,0},{2,3},{3,2},{4,5},{5,4},{6,7},{7,6},{8,9},{9,8},{10,11... | collective-permute-start | bytes 12296 | tf_op jit(solution)/shard_map/ppermute | solution.py:311

commit v3 on v2

v3 whole, which is shorter than its diff:
```python
import functools
import math

import jax
import jax.numpy as jnp
from jax import lax
from jax.experimental import pallas as pl
from jax.experimental.pallas import tpu as pltpu
from jax.sharding import PartitionSpec as P

BLOCK = 256
SHARE = (1, 2)
LIMIT = 48 << 20
ROWS = ((1,), (1,))
ANY = pl.BlockSpec(memory_space=pl.ANY)
HBM = pl.BlockSpec(memory_space=pltpu.HBM)
SCALARS = pl.BlockSpec(memory_space=pltpu.SMEM)


def dot(left, right, dims):
    return lax.dot_general(
        left, right, (dims, ((), ())), precision=lax.Precision.HIGHEST, preferred_element_type=jnp.float32
    )


def halves(x):
    high = x.astype(jnp.bfloat16)
    return high, (x - high.astype(jnp.float32)).astype(jnp.bfloat16)


def joined(parts, axis):
    return parts[0] if len(parts) == 1 else jnp.concatenate(parts, axis=axis)


def dot3(left, right, dims):
    left = joined([x for high, low in left for x in (high, high, low)], dims[0][0])
    right = joined([x for high, low in right for x in (high, low, high)], dims[1][0])
    return lax.dot_general(left, right, (dims, ((), ())), preferred_element_type=jnp.float32)


def laplace(squared, width):
    return jnp.exp(-jnp.sqrt(jnp.maximum(squared, 0.0)) / (0.5 * math.sqrt(width)))


def whole(x):
    return pl.BlockSpec(x.shape, lambda *_: (0,) * len(x.shape))


def call(kernel, grid, in_specs, out_specs, out_shape, scratch, flops, size):
    return pl.pallas_call(
        kernel,
        grid=grid,
        in_specs=in_specs,
        out_specs=out_specs,
        out_shape=out_shape,
        scratch_shapes=scratch,
        compiler_params=pltpu.CompilerParams(vmem_limit_bytes=LIMIT),
        cost_estimate=pl.CostEstimate(flops=flops, bytes_accessed=size, transcendentals=0),
    )


def f32(*shape):
    return jax.ShapeDtypeStruct(shape, jnp.float32)


def take(features, centres, batch_index, first, last, order=()):
    steps, rows = batch_index.shape
    copied = last > first

    def kernel(index, table, source, *rest):
        rest = rest[len(order):]
        out = rest[0]
        sems = rest[-1]
        copies = []
        if copied:
            copies.append(pltpu.make_async_copy(source.at[pl.ds(first, last - first)], rest[1], sems.at[steps * rows]))
        for step in range(steps):
            for row in range(rows):
                spot = step * rows + row
                copies.append(
                    pltpu.make_async_copy(
                        table.at[pl.ds(index[step, row], 1)], out.at[pl.ds(spot, 1)], sems.at[spot]
                    )
                )
        for copy in copies:
            copy.start()
        for copy in copies:
            copy.wait()

    width = features.shape[1]
    shapes = [f32(steps * rows, width)] + ([f32(last - first, width)] if copied else [])
    return call(
        kernel, (), [SCALARS, HBM, HBM] + [ANY] * len(order), [pl.BlockSpec(memory_space=pltpu.VMEM)] * len(shapes), shapes,
        [pltpu.SemaphoreType.DMA((steps * rows + 1,))], 0, 4 * width * (rows * steps + last - first),
    )(batch_index, features, centres, *order)


def chunk_rows(ref, ranges):
    width = ref.shape[-1]
    return jnp.concatenate([ref[:, a:b].reshape(-1, width) for a, b in ranges])


def square_sums(x):
    return jnp.sum(x * x, axis=1, keepdims=True)


def square_row(x):
    return dot(jnp.ones((8, x.shape[1]), jnp.float32), x * x, ROWS)[:1]


def partial_squares(own, ranges, centres, start, order=()):
    count = own.shape[0]
    sizes = [count * (b - a) for a, b in ranges]
    late = centres.shape[0] - start

    def kernel(own_ref, centre_ref, *rest):
        outs = rest[len(order):]
        rows = chunk_rows(own_ref, ranges)
        block = centre_ref[...]
        square = square_sums(rows) + square_row(block) - 2.0 * dot3([halves(rows)], [halves(block)], ROWS)
        top = 0
        for out, size in zip(outs, sizes):
            out[...] = square[top : top + size]
            top += size

    total = sum(sizes)
    return call(
        kernel, (late // BLOCK,),
        [whole(own), pl.BlockSpec((BLOCK, own.shape[2]), lambda i: (i + start // BLOCK, 0))] + [ANY] * len(order),
        [pl.BlockSpec((size, BLOCK), lambda i: (0, i)) for size in sizes],
        [f32(size, late) for size in sizes],
        [], 12 * total * late * own.shape[2], 4 * (late * own.shape[2] + total * late),
    )(own, centres, *order)


def padded(outputs):
    return (outputs // 128 + 1) * 128


def add_products(total, kern, coefs, outputs):
    kern = halves(kern)
    total[:, :outputs] += dot3([kern], [halves(coefs)], ROWS)
    if total.shape[1] > padded(outputs):
        total[:, padded(outputs):] += dot3([kern], [kern], ROWS)


def early_part(own, far, local_rows, centres, fetched, coefs, width, order=()):
    devices, both_rows, depth = own.shape
    steps = both_rows // local_rows
    rows = devices * local_rows
    outputs = coefs.shape[0]
    columns = [padded(outputs)] * (steps - 1) + [padded(outputs) + rows]
    starts = [0]
    for part in fetched:
        starts.append(starts[-1] + part.shape[0] // BLOCK)
    ranges = [(step * local_rows, (step + 1) * local_rows) for step in range(steps)]

    def kernel(own_ref, far_ref, centre_ref, coefs_ref, *rest):
        step = pl.program_id(0)
        outs = rest[len(fetched) + len(order): -5]
        near_high, near_low, far_high, far_low, row_square = rest[-5:]

        @pl.when(step == 0)
        def _():
            near, others = chunk_rows(own_ref, ranges), chunk_rows(far_ref, ranges)
            near_high[...], near_low[...] = halves(near)
            far_high[...], far_low[...] = halves(others)
            row_square[...] = jnp.broadcast_to(square_sums(near) + square_sums(others), row_square.shape)

        block = centre_ref[...]
        away = rest[0][...]
        for index in range(1, len(fetched)):
            away = jnp.where(step >= starts[index], rest[index][...], away)
        centre_square = square_row(block) + square_row(away)
        block, away = halves(block), halves(away)
        pairs = [(near_high[...], near_low[...]), (far_high[...], far_low[...])]
        inner = dot3(pairs, [block, away], ROWS)
        kern = laplace(row_square[:, :1] + centre_square - 2.0 * inner, width)
        both = halves(kern)
        predicted = dot3([both], [halves(coefs_ref[...])], ROWS)
        for index in range(steps):
            kern_ref, total = outs[index], outs[steps + index]
            span = slice(index * rows, (index + 1) * rows)
            part = (both[0][span], both[1][span])
            kern_ref[...] = kern[span]

            @pl.when(step == 0)
            def _():
                total[...] = jnp.zeros_like(total)

            total[:, :outputs] += predicted[span]
            if total.shape[1] > padded(outputs):
                total[:, padded(outputs):] += dot3([part], [part], ROWS)

    def placed(index):
        blocks = starts[index + 1] - starts[index]
        return lambda i: (jnp.clip(i - starts[index], 0, blocks - 1), 0)

    early = starts[-1] * BLOCK
    result = call(
        kernel, (starts[-1],),
        [whole(own), whole(far), pl.BlockSpec((BLOCK, depth), lambda i: (i, 0)), pl.BlockSpec((outputs, BLOCK), lambda i: (0, i))]
        + [pl.BlockSpec((BLOCK, depth), placed(index)) for index in range(len(fetched))] + [ANY] * len(order),
        [pl.BlockSpec((rows, BLOCK), lambda i: (0, i))] * steps + [pl.BlockSpec((rows, wide), lambda i: (0, 0)) for wide in columns],
        [f32(rows, early)] * steps + [f32(rows, wide) for wide in columns],
        [pltpu.VMEM((steps * rows, depth), jnp.bfloat16)] * 4 + [pltpu.VMEM((steps * rows, 128), jnp.float32)],
        12 * steps * rows * early * depth, 8 * early * depth + 4 * steps * rows * early,
    )(own, far, centres, coefs, *fetched, *order)
    return list(zip(result[:steps], result[steps:]))


def predict(where, early, squares, coefs, targets, width, with_inner, order=()):
    rows, late = squares[0].shape
    outputs, centres = coefs.shape
    columns = padded(outputs) + (rows if with_inner else 0)
    own = targets.shape[0]
    quarter = rows // 4
    steps = late // BLOCK
    skipped = centres // BLOCK - steps
    given = [] if early is None else [early[1]]
    ins = list(squares) + [coefs, targets] + given + list(order)

    def kernel(where_ref, *rest):
        square_refs, rest = rest[: len(squares)], rest[len(squares):]
        coefs_ref, target_ref = rest[:2]
        kern_ref, out_ref, total = rest[-3:]
        step = pl.program_id(0)

        @pl.when(step == 0)
        def _():
            total[...] = rest[2][...] if given else jnp.zeros_like(total)

        square = square_refs[0][...]
        for ref in square_refs[1:]:
            square = square + ref[...]
        kern = laplace(square, width)
        kern_ref[...] = kern
        add_products(total, kern, coefs_ref[...], outputs)

        @pl.when(step == steps - 1)
        def _():
            mine = pl.ds(pl.multiple_of(where_ref[0] * own, own), own)
            total[mine, :outputs] -= target_ref[...]
            for block in range(4):
                source = pl.multiple_of((where_ref[1] ^ block) * quarter, quarter)
                out_ref[block] = total[pl.ds(source, quarter), :]

    specs = [SCALARS] + [pl.BlockSpec((rows, BLOCK), lambda i: (0, i)) for _ in squares]
    specs += [pl.BlockSpec((outputs, BLOCK), lambda i: (0, i + skipped)), whole(targets)]
    specs += [whole(x) for x in given]
    specs += [ANY] * len(order)
    return call(
        kernel, (steps,), specs,
        [pl.BlockSpec((rows, BLOCK), lambda i: (0, i)), pl.BlockSpec((4, quarter, columns), lambda i: (0, 0, 0))],
        [f32(rows, late), f32(4, quarter, columns)],
        [pltpu.VMEM((rows, columns), jnp.float32)],
        6 * rows * late * columns, 4 * late * (outputs + 3 * rows),
    )(where, *ins)


def settle(where, near, far, outputs, own):
    quarter = near.shape[1]
    rows = 4 * quarter
    pad = padded(outputs)
    with_inner = near.shape[2] > pad

    def kernel(where_ref, near_ref, far_ref, turned_ref, own_ref, *rest):
        resid_ref = rest[-1]
        inner = rest[1] if with_inner else None
        marked = jnp.zeros((1, 1), jnp.float32)
        for block in range(4):
            ref = (near_ref, far_ref)[block // 2]
            spot = pl.ds(pl.multiple_of((where_ref[1] ^ block) * quarter, quarter), quarter)
            resid_ref[spot, :] = ref[block % 2, :, :pad]
            if with_inner:
                inner[spot, :] = ref[block % 2, :, pad:]
                marked = marked + ref[block % 2, :1, pad - 1 : pad]
        resid = resid_ref[...]
        if with_inner:
            resid = jnp.where(lax.broadcasted_iota(jnp.int32, resid.shape, 1) < outputs, resid, 0.0)
            rest[0][:8, :] = jnp.broadcast_to(marked, (8, 128))
            rest[0][8:, :] = jnp.full((8, 128), jnp.sum(inner[...] * dot(resid, resid, ROWS)))
        turned_ref[...] = resid.T[:outputs]
        own_ref[...] = resid_ref[pl.ds(pl.multiple_of(where_ref[0] * own, own), own), :][:, :outputs]

    shapes = [f32(outputs, rows), f32(own, outputs)] + ([f32(16, 128)] if with_inner else [])
    scratch = [pltpu.VMEM((rows, rows), jnp.float32)] if with_inner else []
    return call(
        kernel, (1,), [SCALARS, whole(near), whole(far)], [whole(x) for x in shapes], shapes,
        scratch + [pltpu.VMEM((rows, pad), jnp.float32)],
        12 * rows * rows * outputs, 4 * near.size * 3,
    )(where, near, far)


def pieces(kerns):
    wide = math.gcd(*[x.shape[1] for x in kerns], 2 * BLOCK)
    starts = [0]
    for kern in kerns:
        starts.append(starts[-1] + kern.shape[1] // wide)

    def placed(index):
        blocks = starts[index + 1] - starts[index]
        return lambda i: (0, jnp.clip(i - starts[index], 0, blocks - 1))

    return wide, starts, [pl.BlockSpec((x.shape[0], wide), placed(index)) for index, x in enumerate(kerns)]


def product_of(turned_ref, kern_refs, starts):
    kern = kern_refs[0][...]
    for index in range(1, len(kern_refs)):
        kern = jnp.where(pl.program_id(0) >= starts[index], kern_refs[index][...], kern)
    return dot3([halves(turned_ref[...])], [halves(kern)], ((1,), (0,)))


def gradient(kerns, turned, mark_shape, column, order=()):
    outputs, rows = turned.shape
    centres = sum(x.shape[1] for x in kerns)
    wide, starts, specs = pieces(kerns)

    def kernel(turned_ref, *rest):
        out_ref, mark_ref, total = rest[len(kerns) + len(order):]
        grad = product_of(turned_ref, rest[: len(kerns)], starts)
        out_ref[...] = grad
        square = jnp.sum(grad * grad, axis=0, keepdims=True)

        @pl.when(pl.program_id(0) == 0)
        def _():
            total[...] = jnp.zeros_like(total)

        total[...] += square

        @pl.when(pl.program_id(0) == centres // wide - 1)
        def _():
            marked = lax.broadcasted_iota(jnp.int32, mark_shape, 1) == column
            mark_ref[...] = jnp.where(marked, jnp.sum(total[...]), 0.0)

    return call(
        kernel, (centres // wide,), [whole(turned)] + specs + [ANY] * len(order),
        [pl.BlockSpec((outputs, wide), lambda i: (0, i)), pl.BlockSpec(mark_shape, lambda i: (0, 0))],
        [f32(outputs, centres), f32(*mark_shape)], [pltpu.VMEM((1, wide), jnp.float32)],
        6 * rows * centres * outputs, 4 * centres * (rows + outputs),
    )(turned, *kerns, *order)


def update(coefs, grad, kerns, turned, squares, batch_total, entries):
    outputs, centres = coefs.shape
    rows = turned.shape[1]
    wide, starts, specs = pieces(kerns)

    def kernel(coefs_ref, grad_ref, turned_ref, *rest):
        kern_refs, square_refs = rest[: len(kerns)], rest[len(kerns) : -1]

        def factor(row):
            square = square_refs[0][row : row + 1, :1]
            for more in square_refs[1:]:
                square = square + more[row : row + 1, :1]
            square = jnp.maximum(square, 0.0) / (batch_total * batch_total)
            return 0.1 / batch_total / jnp.sqrt(square / entries + 1e-06)

        result = coefs_ref[...] - grad_ref[...] * factor(0)
        rest[-1][...] = result - product_of(turned_ref, kern_refs, starts) * factor(8)

    block = pl.BlockSpec((outputs, wide), lambda i: (0, i))
    return call(
        kernel, (centres // wide,), [block, block, whole(turned)] + specs + [whole(x) for x in squares],
        block, f32(outputs, centres), [], 6 * rows * centres * outputs, 4 * centres * (rows + 3 * outputs),
    )(coefs, grad, turned, *kerns, *squares)


def swap(x, bit):
    n = lax.axis_size("cen")
    return lax.ppermute(x, "cen", [(i, i ^ bit) for i in range(n)])


def across(x):
    return lax.ppermute(x, "out", [(0, 1), (1, 0)])


def bits():
    n = lax.axis_size("cen")
    return [1 << b for b in range(n.bit_length() - 1)]


def mine(bit):
    return (lax.axis_index("cen") & bit) != 0


def grow(x, bit):
    far = swap(x, bit)
    return jnp.where(mine(bit), jnp.stack([far, x]), jnp.stack([x, far]))


def gathered(x):
    return x.reshape((-1,) + x.shape[-2:])


def after(x, token):
    return jnp.where(token == token, x, token)


def gather(own, ahead=None, far=None):
    for step, bit in enumerate(reversed(bits())):
        own = grow(own, bit)
        if far is not None:
            if step == 0:
                own = after(own, ahead[: own.size // own.shape[-1]].reshape(own.shape))
            else:
                token = own
                while token.ndim > far.ndim:
                    token = token[0]
                far = grow(after(far, token), bits()[-step])
    if far is None:
        return gathered(own)
    return gathered(own), gathered(grow(far, bits()[0]))


def sum_half(x):
    return x[:2] + swap(x[2:], 1)


def sum_rest(x, mark=None):
    x = x[0] + swap(x[1], 2)
    if mark is not None:
        x = x + mark
    for bit in bits()[2:]:
        x = x + swap(x, bit)
    x = jnp.stack([x, swap(x, 2)])
    return x, swap(x, 1)


def body(features, centres, coefs, batch_index, targets):
    local_rows = batch_index.shape[1]
    devices = lax.axis_size("cen")
    batch_total = local_rows * devices
    outputs = coefs.shape[1]
    width = features.shape[1] * lax.axis_size("out")
    entries = centres.shape[0] * devices * outputs * lax.axis_size("out")
    pair = lax.axis_size("out") == 2
    sent = centres.shape[0] * SHARE[0] // SHARE[1] if pair else 0
    ranges = [(step * local_rows, (step + 1) * local_rows) for step in range(2)]
    coefs = coefs.T

    place = 0
    for bit in bits():
        place = 2 * place + jnp.where(mine(bit), 1, 0)
    where = jnp.stack([place, 2 * jnp.where(mine(1), 1, 0) + jnp.where(mine(2), 1, 0)]).astype(jnp.int32)

    if pair:
        ahead = centres[:BLOCK]
        fetched = [across(ahead)]
        picked, more = take(features, centres, batch_index, BLOCK, sent, [ahead])
        far = across(picked)
        fetched.append(across(more))
        own, far = gather(picked, fetched[0], far)
    else:
        own = gather(take(features, centres, batch_index, 0, 0)[0])

    partial = partial_squares(own, ranges[:1], centres, sent)
    partial = list(partial) + list(partial_squares(own, ranges[1:], centres, sent, partial))
    if pair:
        squares = [[x, across(x)] for x in partial]
        early = early_part(own, far, local_rows, centres, fetched, coefs, width, partial)
    else:
        squares = [[lax.psum(x, "out")] for x in partial]
        early = [None, None]

    def kernels(step, kern):
        return [kern] if early[step] is None else [early[step][0], kern]

    kern, blocks = predict(where, early[0], squares[0], coefs, targets[0], width, False)
    turned, rows, *_ = settle(where, *sum_rest(sum_half(blocks)), outputs, local_rows)
    kern_next, blocks = predict(where, early[1], squares[1], coefs, targets[1], width, True, [turned])
    blocks = sum_half(blocks)
    grad, mark = gradient(kernels(0, kern), turned, blocks.shape[1:], padded(outputs) - 1, [blocks])
    turned, rows_next, square = settle(where, *sum_rest(blocks, mark), outputs, local_rows)
    parts = [square, across(square)] if pair else [lax.psum(square, "out")]
    new_coefs = update(coefs, grad, kernels(1, kern_next), turned, parts, batch_total, entries)
    return (jnp.stack([rows, rows_next]), new_coefs.T)


def solution(mesh):
    placed = (
        P("cen", "out"),
        P("cen", "out"),
        P("cen", "out"),
        P(None, "cen"),
        P(None, "cen", "out"),
    )
    return jax.shard_map(
        body,
        mesh=mesh,
        in_specs=placed,
        out_specs=(P(None, "cen", "out"), P("cen", "out")),
        check_vma=False,
    )
```

time: 204 us -> 156 us (0.76)
  Pallas kernels: 68.7 us -> 46.6 us
  local copies, waits for them, and re-layouts: 14.7 us -> 1.86 us
  waiting for transfers between devices: 78.4 us -> 67.4 us
    ppermute x8 -> x6, waiting for transfers between devices: 35.8 us -> 19 us  [across(): return lax.ppermute(x, 'out', [(0, 1), (1, 0)])]
    pallas_call x3 -> x2, Pallas kernels: 21.3 us -> 8.06 us  [predict(): call(kernel, (steps,), specs, [pl.BlockSpec((rows, BLOCK), lambda i: (0,...]
    unnamed x8 -> x12, local copies, waits for them, and re-layouts: 13.5 us -> 0.7 us
    pallas_call x7 -> x6, Pallas kernels: 36.7 us -> 29.4 us  [the longest x1 13.9 us: early_part(): call(kernel, (starts[-1],), [whole(own), whole(far), pl.BlockSpec((BLOCK,...]
    ppermute x26 -> x20, waiting for transfers between devices: 42.6 us -> 48.4 us  [swap(): return lax.ppermute(x, 'cen', [(i, i ^ bit) for i in range(n)])]
    ppermute x26 -> x20, starting transfers between devices: 28.9 us -> 27.6 us  [swap(): return lax.ppermute(x, 'cen', [(i, i ^ bit) for i in range(n)])]
    ppermute x8 -> x6, starting transfers between devices: 9.39 us -> 9.62 us  [across(): return lax.ppermute(x, 'out', [(0, 1), (1, 0)])]
  transfers between devices with their start and end apart: 34 -> 26, of which waited for: 19 -> 22; matrix products, arithmetic and copies ran while one was open for 4% -> 1% of each run, Pallas kernels for 21% -> 20%
where the time goes in v3:
time: 156 us
  waiting for transfers between devices  67.4 us (43%)
  Pallas kernels  46.6 us (30%)
  starting transfers between devices  37.2 us (24%)
  local copies, waits for them, and re-layouts  1.86 us (1%)
  other arithmetic  1.7 us (1%)
    ppermute x20, waiting for transfers between devices, swap(): return lax.ppermute(x, 'cen', [(i, i ^ bit) for i in range(n)])  48.4 us
    ppermute x20, starting transfers between devices, swap(): return lax.ppermute(x, 'cen', [(i, i ^ bit) for i in range(n)])  27.6 us
    ppermute x6, waiting for transfers between devices, across(): return lax.ppermute(x, 'out', [(0, 1), (1, 0)])  19 us
    pallas_call x1, Pallas kernels, early_part(): call(kernel, (starts[-1],), [whole(own), whole(far), pl.BlockSpec((BLOCK,...  13.9 us
    ppermute x6, starting transfers between devices, across(): return lax.ppermute(x, 'out', [(0, 1), (1, 0)])  9.62 us
    pallas_call x2, Pallas kernels, partial_squares(): call(kernel, (late // BLOCK,), [whole(own), pl.BlockSpec((BLOCK, own.shap...  9.18 us
    pallas_call x2, Pallas kernels, predict(): call(kernel, (steps,), specs, [pl.BlockSpec((rows, BLOCK), lambda i: (0,...  8.06 us
    pallas_call x1, Pallas kernels, update(): call(kernel, (centres // wide,), [block, block, whole(turned)] + specs +...  6.77 us
  transfers between devices with their start and end apart: 26, of which 22 were waited for; matrix products, arithmetic and copies ran while one was open for 1% of the time, Pallas kernels for 20%

profile of v3, /device:TPU:0, one launch (start us, length us, event | category | flops | bytes accessed | tf_op | source)
XLA Modules:
  0.0 155.7 jit_solution(2203972557764177724)
XLA Ops:
  0.6 1.1 slice.54.rest_0_
  1.7 3.0 %collective-permute-start = (f32[256,512]{1,0:T(8,128)S(1)}, f32[256,512]{1,0:T(8,128)S(1)}, u32[]{:S(2)}, u32[]{:S(2)}) collective-permute-start(f32[256,512]{1,0:T(8,128)S(1)} %slice.54.rest_0_), channel_id=1, source_target_pairs={{0,1},{1,0},{2,3},{3,2},{4,5},{5,4},{6,7},{7,6},{8,9},{9,8},{10,11... | collective-permute-start | bytes 1572872 | tf_op jit(solution)/shard_map/ppermute | solution.py:376
  4.7 0.7 copy-done.4
  5.4 2.3 %shard_map.68 = (f32[32,512]{1,0:T(8,128)S(1)}, f32[768,512]{1,0:T(8,128)S(1)}) custom-call(s32[2,16]{1,0:T(2,128)S(1)} %copy-done.4, f32[2048,512]{1,0:T(8,128)} %table.1, f32[2048,512]{1,0:T(8,128)} %centre_ref.5, f32[256,512]{1,0:T(8,128)S(1)} %slice.54.rest_0_), custom_call_target="tpu_custom_call" | custom-call | bytes 1638400 | tf_op jit(solution)/shard_map/pallas_call | solution.py:92
  7.7 2.7 %collective-permute-start.1 = (f32[32,512]{1,0:T(8,128)S(1)}, f32[32,512]{1,0:T(8,128)S(1)}, u32[]{:S(2)}, u32[]{:S(2)}) collective-permute-start(f32[32,512]{1,0:T(8,128)S(1)} %get-tuple-element.19), channel_id=1, source_target_pairs={{0,16},{2,18},{4,20},{6,22},{8,24},{10,26},{12,28},{14,30},{16,0},... | collective-permute-start | bytes 196616 | tf_op jit(solution)/shard_map/ppermute | solution.py:372
  10.4 0.5 collective-permute-start.6
  10.9 1.5 collective-permute-start.11
  12.4 0.1 pad_add_fusion.where_ref
  12.5 5.0 %collective-permute-done.rest_0_ = f32[256,512]{1,0:T(8,128)S(1)} collective-permute-done((f32[256,512]{1,0:T(8,128)S(1)}, f32[256,512]{1,0:T(8,128)S(1)}, u32[]{:S(2)}, u32[]{:S(2)}) %collective-permute-start) | collective-permute-done | bytes 524320 | tf_op jit(solution)/shard_map/ppermute | solution.py:376
  17.5 2.2 %collective-permute-start.2 = (f32[2,32,512]{2,1,0:T(8,128)S(1)}, f32[2,32,512]{2,1,0:T(8,128)S(1)}, u32[]{:S(2)}, u32[]{:S(2)}) collective-permute-start(f32[2,32,512]{2,1,0:T(8,128)S(1)} %compare_select_fusion.7), channel_id=1, source_target_pairs={{0,8},{2,10},{4,12},{6,14},{8,0},{10,2},{12,4},{14,6},{16,24},{18,... | collective-permute-start | bytes 393224 | tf_op jit(solution)/shard_map/ppermute | solution.py:372
  19.8 2.9 %collective-permute-done.2 = f32[2,32,512]{2,1,0:T(8,128)S(1)} collective-permute-done((f32[2,32,512]{2,1,0:T(8,128)S(1)}, f32[2,32,512]{2,1,0:T(8,128)S(1)}, u32[]{:S(2)}, u32[]{:S(2)}) %collective-permute-start.2) | collective-permute-done | bytes 131104 | tf_op jit(solution)/shard_map/ppermute | solution.py:372
  22.7 2.0 %collective-permute-start.3 = (f32[2,2,32,512]{3,2,1,0:T(8,128)S(1)}, f32[2,2,32,512]{3,2,1,0:T(8,128)S(1)}, u32[]{:S(2)}, u32[]{:S(2)}) collective-permute-start(f32[2,2,32,512]{3,2,1,0:T(8,128)S(1)} %maximum_select_fusion.6), channel_id=1, source_target_pairs={{0,4},{2,6},{4,0},{6,2},{8,12},{10,14},{12,8},{14,10},{16,20},{18,... | collective-permute-start | bytes 786440 | tf_op jit(solution)/shard_map/ppermute | solution.py:372
  24.7 2.7 %collective-permute-start.7 = (f32[32,512]{1,0:T(8,128)S(1)}, f32[32,512]{1,0:T(8,128)S(1)}, u32[]{:S(2)}, u32[]{:S(2)}) collective-permute-start(f32[32,512]{1,0:T(8,128)S(1)} %compare_select_fusion.8), channel_id=1, source_target_pairs={{0,16},{2,18},{4,20},{6,22},{8,24},{10,26},{12,28},{14,30},{16,0},... | collective-permute-start | bytes 196616 | tf_op jit(solution)/shard_map/ppermute | solution.py:372
  27.5 1.7 %collective-permute-done.3 = f32[2,2,32,512]{3,2,1,0:T(8,128)S(1)} collective-permute-done((f32[2,2,32,512]{3,2,1,0:T(8,128)S(1)}, f32[2,2,32,512]{3,2,1,0:T(8,128)S(1)}, u32[]{:S(2)}, u32[]{:S(2)}) %collective-permute-start.3) | collective-permute-done | bytes 262176 | tf_op jit(solution)/shard_map/ppermute | solution.py:372
  29.2 0.1 collective-permute-start.4
  29.3 0.7 collective-permute-done.7
  30.0 1.6 %collective-permute-start.8 = (f32[2,32,512]{2,1,0:T(8,128)S(1)}, f32[2,32,512]{2,1,0:T(8,128)S(1)}, u32[]{:S(2)}, u32[]{:S(2)}) collective-permute-start(f32[2,32,512]{2,1,0:T(8,128)S(1)} %compare_select_fusion.5), channel_id=1, source_target_pairs={{0,8},{2,10},{4,12},{6,14},{8,0},{10,2},{12,4},{14,6},{16,24},{18,... | collective-permute-start | bytes 393224 | tf_op jit(solution)/shard_map/ppermute | solution.py:372
  31.8 0.1 maximum_select_fusion
  31.9 3.7 %collective-permute-done.8 = f32[2,32,512]{2,1,0:T(8,128)S(1)} collective-permute-done((f32[2,32,512]{2,1,0:T(8,128)S(1)}, f32[2,32,512]{2,1,0:T(8,128)S(1)}, u32[]{:S(2)}, u32[]{:S(2)}) %collective-permute-start.8) | collective-permute-done | bytes 131104 | tf_op jit(solution)/shard_map/ppermute | solution.py:372
  35.6 1.7 %collective-permute-start.9 = (f32[2,2,32,512]{3,2,1,0:T(8,128)S(1)}, f32[2,2,32,512]{3,2,1,0:T(8,128)S(1)}, u32[]{:S(2)}, u32[]{:S(2)}) collective-permute-start(f32[2,2,32,512]{3,2,1,0:T(8,128)S(1)} %compare_select_fusion.2), channel_id=1, source_target_pairs={{0,4},{2,6},{4,0},{6,2},{8,12},{10,14},{12,8},{14,10},{16,20},{18,... | collective-permute-start | bytes 786440 | tf_op jit(solution)/shard_map/ppermute | solution.py:372
  37.3 4.6 %shard_map.69.rest_0_.rest_2_ = f32[256,1024]{1,0:T(8,128)S(1)} custom-call(f32[16,32,512]{2,1,0:T(8,128)S(1)} %bitcast.71, f32[2048,512]{1,0:T(8,128)} %centre_ref.5), custom_call_target="tpu_custom_call" | custom-call | flops 1610612736 | bytes 3145728 | tf_op jit(solution)/shard_map/pallas_call | solution.py:127
  41.9 1.6 collective-permute-start.5
  43.5 0.1 collective-permute-done.9
  43.7 0.1 collective-permute-start.10
  43.8 4.6 %shard_map.70.rest_3_.rest_0_ = f32[256,1024]{1,0:T(8,128)S(1)} custom-call(f32[16,32,512]{2,1,0:T(8,128)S(1)} %bitcast.72, f32[2048,512]{1,0:T(8,128)} %centre_ref.5, f32[256,1024]{1,0:T(8,128)S(1)} %shard_map.69.rest_0_.rest_2_), custom_call_target="tpu_custom_call" | custom-call | flops 1610612736 | bytes 3145728 | tf_op jit(solution)/shard_map/pallas_call | solution.py:127
  48.5 0.1 maximum_select_fusion.1
  48.6 4.1 %collective-permute-done.11.rest_1_ = f32[768,512]{1,0:T(8,128)} collective-permute-done((f32[768,512]{1,0:T(8,128)S(1)}, f32[768,512]{1,0:T(8,128)}, u32[]{:S(2)}, u32[]{:S(2)}) %collective-permute-start.11) | collective-permute-done | bytes 1572896 | tf_op jit(solution)/shard_map/ppermute | solution.py:376
  52.7 13.9 %shard_map.71 = (f32[256,1024]{1,0:T(8,128)S(1)}, f32[256,1024]{1,0:T(8,128)S(1)}, f32[256,512]{1,0:T(8,128)S(1)}, f32[256,768]{1,0:T(8,128)S(1)}) custom-call(f32[16,32,512]{2,1,0:T(8,128)S(1)} %bitcast.73, f32[16,32,512]{2,1,0:T(8,128)S(1)} %bitcast.74, f32[2048,512]{1,0:T(8,128)} %centre_ref.5, f32[500,2048]{1,0:T(8,128)} %bitcast.80, ...), custom_call_target="tpu_custom_call" | custom-call | flops 3221225472 | bytes 6291456 | tf_op jit(solution)/shard_map/pallas_call | solution.py:200
  66.6 7.6 %collective-permute-done.5.rest_1_ = f32[256,1024]{1,0:T(8,128)S(1)} collective-permute-done((f32[256,1024]{1,0:T(8,128)S(1)}, f32[256,1024]{1,0:T(8,128)S(1)}, u32[]{:S(2)}, u32[]{:S(2)}) %collective-permute-start.5) | collective-permute-done | bytes 1048608 | tf_op jit(solution)/shard_map/ppermute | solution.py:376
  74.2 3.9 %shard_map.72 = (f32[256,1024]{1,0:T(8,128)S(1)}, f32[4,64,512]{2,1,0:T(8,128)S(1)}) custom-call(s32[2]{0:T(128)S(1)} %pad_add_fusion.where_ref, f32[256,1024]{1,0:T(8,128)S(1)} %copy-done.1, f32[256,1024]{1,0:T(8,128)S(1)} %collective-permute-done.5.rest_1_, f32[500,2048]{1,0:T(8,128)} %bitcast.81, f32[16,500]{1,0:T(8,128)S(1)} %get-tuple-element.37.rest_3_, ...), custom_call_target="tpu_custom_call" | custom-call | flops 805306368 | bytes 5193728 | tf_op jit(solution)/shard_map/pallas_call | solution.py:252
  78.2 0.1 collective-permute-start.12
  78.3 1.5 collective-permute-done.12
  79.9 1.8 %collective-permute-start.13 = (f32[64,512]{1,0:T(8,128)S(1)}, f32[64,512]{1,0:T(8,128)S(1)}, u32[]{:S(2)}, u32[]{:S(2)}) collective-permute-start(f32[64,512]{1,0:T(8,128)S(1)} %slice_bitcast_fusion.2), channel_id=1, source_target_pairs={{0,4},{2,6},{4,0},{6,2},{8,12},{10,14},{12,8},{14,10},{16,20},{18,... | collective-permute-start | bytes 393224 | tf_op jit(solution)/shard_map/ppermute | solution.py:372
  81.7 1.5 collective-permute-start.18
  83.2 2.3 %collective-permute-done.13 = f32[64,512]{1,0:T(8,128)S(1)} collective-permute-done((f32[64,512]{1,0:T(8,128)S(1)}, f32[64,512]{1,0:T(8,128)S(1)}, u32[]{:S(2)}, u32[]{:S(2)}) %collective-permute-start.13) | collective-permute-done | bytes 131104 | tf_op jit(solution)/shard_map/ppermute | solution.py:372
  85.5 1.9 %collective-permute-start.14 = (f32[64,512]{1,0:T(8,128)S(1)}, f32[64,512]{1,0:T(8,128)S(1)}, u32[]{:S(2)}, u32[]{:S(2)}) collective-permute-start(f32[64,512]{1,0:T(8,128)S(1)} %fusion.2), channel_id=1, source_target_pairs={{0,8},{2,10},{4,12},{6,14},{8,0},{10,2},{12,4},{14,6},{16,24},{18,... | collective-permute-start | bytes 393224 | tf_op jit(solution)/shard_map/ppermute | solution.py:372
  87.4 3.2 %collective-permute-done.14 = f32[64,512]{1,0:T(8,128)S(1)} collective-permute-done((f32[64,512]{1,0:T(8,128)S(1)}, f32[64,512]{1,0:T(8,128)S(1)}, u32[]{:S(2)}, u32[]{:S(2)}) %collective-permute-start.14) | collective-permute-done | bytes 131104 | tf_op jit(solution)/shard_map/ppermute | solution.py:372
  90.6 2.9 %collective-permute-start.15 = (f32[64,512]{1,0:T(8,128)S(1)}, f32[64,512]{1,0:T(8,128)S(1)}, u32[]{:S(2)}, u32[]{:S(2)}) collective-permute-start(f32[64,512]{1,0:T(8,128)S(1)} %add.42), channel_id=1, source_target_pairs={{0,16},{2,18},{4,20},{6,22},{8,24},{10,26},{12,28},{14,30},{16,0},... | collective-permute-start | bytes 393224 | tf_op jit(solution)/shard_map/ppermute | solution.py:372
  93.4 4.9 %collective-permute-done.15 = f32[64,512]{1,0:T(8,128)S(1)} collective-permute-done((f32[64,512]{1,0:T(8,128)S(1)}, f32[64,512]{1,0:T(8,128)S(1)}, u32[]{:S(2)}, u32[]{:S(2)}) %collective-permute-start.15) | collective-permute-done | bytes 131104 | tf_op jit(solution)/shard_map/ppermute | solution.py:372
  98.4 1.6 %collective-permute-start.16 = (f32[64,512]{1,0:T(8,128)S(1)}, f32[64,512]{1,0:T(8,128)S(1)}, u32[]{:S(2)}, u32[]{:S(2)}) collective-permute-start(f32[64,512]{1,0:T(8,128)S(1)} %add.43), channel_id=1, source_target_pairs={{0,4},{2,6},{4,0},{6,2},{8,12},{10,14},{12,8},{14,10},{16,20},{18,... | collective-permute-start | bytes 393224 | tf_op jit(solution)/shard_map/ppermute | solution.py:372
  100.0 3.4 %collective-permute-done.16 = f32[64,512]{1,0:T(8,128)S(1)} collective-permute-done((f32[64,512]{1,0:T(8,128)S(1)}, f32[64,512]{1,0:T(8,128)S(1)}, u32[]{:S(2)}, u32[]{:S(2)}) %collective-permute-start.16) | collective-permute-done | bytes 131104 | tf_op jit(solution)/shard_map/ppermute | solution.py:372
  103.4 0.1 collective-permute-start.17
  103.5 1.5 collective-permute-done.17.far_ref
  105.0 0.8 shard_map.73
  105.8 0.8 collective-permute-done.18.rest_1_
  106.6 4.1 %shard_map.74 = (f32[256,1024]{1,0:T(8,128)S(1)}, f32[4,64,768]{2,1,0:T(8,128)S(1)}) custom-call(s32[2]{0:T(128)S(1)} %pad_add_fusion.where_ref, f32[256,1024]{1,0:T(8,128)S(1)} %copy-done.3, f32[256,1024]{1,0:T(8,128)S(1)} %collective-permute-done.18.rest_1_, f32[500,2048]{1,0:T(8,128)} %bitcast.82, f32[16,500]{1,0:T(8,128)S(1)} %get-tuple-element.36.rest_3_, ...), custom_call_target="tpu_custom_call" | custom-call | flops 1207959552 | bytes 5193728 | tf_op jit(solution)/shard_map/pallas_call | solution.py:252
  110.8 0.1 collective-permute-start.19
  110.9 1.7 %collective-permute-done.19 = f32[2,64,768]{2,1,0:T(8,128)S(1)} collective-permute-done((f32[2,64,768]{2,1,0:T(8,128)S(1)}, f32[2,64,768]{2,1,0:T(8,128)S(1)}, u32[]{:S(2)}, u32[]{:S(2)}) %collective-permute-start.19) | collective-permute-done | bytes 393248 | tf_op jit(solution)/shard_map/ppermute | solution.py:372
  112.6 0.9 collective-permute-start.20
  113.5 4.3 %shard_map.75 = (f32[500,2048]{1,0:T(8,128)}, f32[64,768]{1,0:T(8,128)S(1)}) custom-call(f32[500,256]{1,0:T(8,128)S(1)} %get-tuple-element.25.rest_5_.turned_ref, f32[256,1024]{1,0:T(8,128)S(1)} %get-tuple-element.27.rest_0_, f32[256,1024]{1,0:T(8,128)S(1)} %get-tuple-element.28.rest_1_, f32[2,64,768]{2,1,0:T(8,128)S(1)} %slice_add_fusion.rest_2_), custom_call_target="tpu_custom_call" | custom-call | flops 1572864000 | bytes 6193152 | tf_op jit(solution)/shard_map/pallas_call | solution.py:337
  117.8 1.8 %collective-permute-done.20 = f32[64,768]{1,0:T(8,128)S(1)} collective-permute-done((f32[64,768]{1,0:T(8,128)S(1)}, f32[64,768]{1,0:T(8,128)S(1)}, u32[]{:S(2)}, u32[]{:S(2)}) %collective-permute-start.20) | collective-permute-done | bytes 196640 | tf_op jit(solution)/shard_map/ppermute | solution.py:372
  119.7 1.6 %collective-permute-start.21 = (f32[64,768]{1,0:T(8,128)S(1)}, f32[64,768]{1,0:T(8,128)S(1)}, u32[]{:S(2)}, u32[]{:S(2)}) collective-permute-start(f32[64,768]{1,0:T(8,128)S(1)} %fusion.1), channel_id=1, source_target_pairs={{0,8},{2,10},{4,12},{6,14},{8,0},{10,2},{12,4},{14,6},{16,24},{18,... | collective-permute-start | bytes 589832 | tf_op jit(solution)/shard_map/ppermute | solution.py:372
  121.3 4.5 %collective-permute-done.21 = f32[64,768]{1,0:T(8,128)S(1)} collective-permute-done((f32[64,768]{1,0:T(8,128)S(1)}, f32[64,768]{1,0:T(8,128)S(1)}, u32[]{:S(2)}, u32[]{:S(2)}) %collective-permute-start.21) | collective-permute-done | bytes 196640 | tf_op jit(solution)/shard_map/ppermute | solution.py:372
  125.9 2.6 %collective-permute-start.22 = (f32[64,768]{1,0:T(8,128)S(1)}, f32[64,768]{1,0:T(8,128)S(1)}, u32[]{:S(2)}, u32[]{:S(2)}) collective-permute-start(f32[64,768]{1,0:T(8,128)S(1)} %add.47), channel_id=1, source_target_pairs={{0,16},{2,18},{4,20},{6,22},{8,24},{10,26},{12,28},{14,30},{16,0},... | collective-permute-start | bytes 589832 | tf_op jit(solution)/shard_map/ppermute | solution.py:372
  128.5 7.7 %collective-permute-done.22 = f32[64,768]{1,0:T(8,128)S(1)} collective-permute-done((f32[64,768]{1,0:T(8,128)S(1)}, f32[64,768]{1,0:T(8,128)S(1)}, u32[]{:S(2)}, u32[]{:S(2)}) %collective-permute-start.22) | collective-permute-done | bytes 196640 | tf_op jit(solution)/shard_map/ppermute | solution.py:372
  136.3 0.9 collective-permute-start.23
  137.2 4.9 %collective-permute-done.23 = f32[64,768]{1,0:T(8,128)S(1)} collective-permute-done((f32[64,768]{1,0:T(8,128)S(1)}, f32[64,768]{1,0:T(8,128)S(1)}, u32[]{:S(2)}, u32[]{:S(2)}) %collective-permute-start.23) | collective-permute-done | bytes 196640 | tf_op jit(solution)/shard_map/ppermute | solution.py:372
  142.1 0.1 collective-permute-start.24
  142.2 1.7 %collective-permute-done.24.far_ref = f32[2,64,768]{2,1,0:T(8,128)S(1)} collective-permute-done((f32[2,64,768]{2,1,0:T(8,128)S(1)}, f32[2,64,768]{2,1,0:T(8,128)S(1)}, u32[]{:S(2)}, u32[]{:S(2)}) %collective-permute-start.24) | collective-permute-done | bytes 393248 | tf_op jit(solution)/shard_map/ppermute | solution.py:372
  143.9 1.3 shard_map.76
  145.3 1.5 collective-permute-start.25
  146.8 0.6 pad_maximum_fusion.2
  147.4 1.5 collective-permute-done.25.rest_3_
  149.0 6.8 %shard_map.77 = f32[500,2048]{1,0:T(8,128)} custom-call(f32[500,2048]{1,0:T(8,128)} %bitcast.83, f32[500,2048]{1,0:T(8,128)} %get-tuple-element.31.grad_ref, f32[500,256]{1,0:T(8,128)S(1)} %get-tuple-element.32.turned_ref, f32[256,1024]{1,0:T(8,128)S(1)} %get-tuple-element.33.rest_0_, f32[256,1024]{1,0:T(8,128)S(1)} %get-tuple-element.34.rest_1_, ...), custom_call_target="tpu_custom_call" | custom-call | flops 1572864000 | bytes 14385152 | tf_op jit(solution)/shard_map/pallas_call | solution.py:364
  (49 shorter events, 0.9 us)
Async XLA Ops:
  1.7 15.8 %collective-permute-start = (f32[256,512]{1,0:T(8,128)S(1)}, f32[256,512]{1,0:T(8,128)S(1)}, u32[]{:S(2)}, u32[]{:S(2)}) collective-permute-start(f32[256,512]{1,0:T(8,128)S(1)} %slice.54.rest_0_), channel_id=1, source_target_pairs={{0,1},{1,0},{2,3},{3,2},{4,5},{5,4},{6,7},{7,6},{8,9},{9,8},{10,11... | collective-permute-start | bytes 1572872 | tf_op jit(solution)/shard_map/ppermute | solution.py:376
  4.7 0.7 copy-start.4
  5.4 7.0 %copy-start.5 = (f32[2,16,500]{2,1,0:T(8,128)S(1)}, f32[2,16,500]{2,1,0:T(8,128)}, u32[]{:S(2)}) copy-start(f32[2,16,500]{2,1,0:T(8,128)} %param.9) | copy-start | bytes 192004
  7.7 9.8 %collective-permute-start.1 = (f32[32,512]{1,0:T(8,128)S(1)}, f32[32,512]{1,0:T(8,128)S(1)}, u32[]{:S(2)}, u32[]{:S(2)}) collective-permute-start(f32[32,512]{1,0:T(8,128)S(1)} %get-tuple-element.19), channel_id=1, source_target_pairs={{0,16},{2,18},{4,20},{6,22},{8,24},{10,26},{12,28},{14,30},{16,0},... | collective-permute-start | bytes 196616 | tf_op jit(solution)/shard_map/ppermute | solution.py:372
  10.4 14.4 %collective-permute-start.6 = (f32[32,512]{1,0:T(8,128)S(1)}, f32[32,512]{1,0:T(8,128)S(1)}, u32[]{:S(2)}, u32[]{:S(2)}) collective-permute-start(f32[32,512]{1,0:T(8,128)S(1)} %get-tuple-element.19), channel_id=1, source_target_pairs={{0,1},{1,0},{2,3},{3,2},{4,5},{5,4},{6,7},{7,6},{8,9},{9,8},{10,11... | collective-permute-start | bytes 196616 | tf_op jit(solution)/shard_map/ppermute | solution.py:376
  10.9 41.8 %collective-permute-start.11 = (f32[768,512]{1,0:T(8,128)S(1)}, f32[768,512]{1,0:T(8,128)}, u32[]{:S(2)}, u32[]{:S(2)}) collective-permute-start(f32[768,512]{1,0:T(8,128)S(1)} %get-tuple-element.20), channel_id=1, source_target_pairs={{0,1},{1,0},{2,3},{3,2},{4,5},{5,4},{6,7},{7,6},{8,9},{9,8},{10,11... | collective-permute-start | bytes 4718600 | tf_op jit(solution)/shard_map/ppermute | solution.py:376
  17.5 5.2 %collective-permute-start.2 = (f32[2,32,512]{2,1,0:T(8,128)S(1)}, f32[2,32,512]{2,1,0:T(8,128)S(1)}, u32[]{:S(2)}, u32[]{:S(2)}) collective-permute-start(f32[2,32,512]{2,1,0:T(8,128)S(1)} %compare_select_fusion.7), channel_id=1, source_target_pairs={{0,8},{2,10},{4,12},{6,14},{8,0},{10,2},{12,4},{14,6},{16,24},{18,... | collective-permute-start | bytes 393224 | tf_op jit(solution)/shard_map/ppermute | solution.py:372
  22.7 6.4 %collective-permute-start.3 = (f32[2,2,32,512]{3,2,1,0:T(8,128)S(1)}, f32[2,2,32,512]{3,2,1,0:T(8,128)S(1)}, u32[]{:S(2)}, u32[]{:S(2)}) collective-permute-start(f32[2,2,32,512]{3,2,1,0:T(8,128)S(1)} %maximum_select_fusion.6), channel_id=1, source_target_pairs={{0,4},{2,6},{4,0},{6,2},{8,12},{10,14},{12,8},{14,10},{16,20},{18,... | collective-permute-start | bytes 786440 | tf_op jit(solution)/shard_map/ppermute | solution.py:372
  24.7 5.2 %collective-permute-start.7 = (f32[32,512]{1,0:T(8,128)S(1)}, f32[32,512]{1,0:T(8,128)S(1)}, u32[]{:S(2)}, u32[]{:S(2)}) collective-permute-start(f32[32,512]{1,0:T(8,128)S(1)} %compare_select_fusion.8), channel_id=1, source_target_pairs={{0,16},{2,18},{4,20},{6,22},{8,24},{10,26},{12,28},{14,30},{16,0},... | collective-permute-start | bytes 196616 | tf_op jit(solution)/shard_map/ppermute | solution.py:372
  29.2 2.6 %collective-permute-start.4 = (f32[2,2,2,32,512]{4,3,2,1,0:T(8,128)S(1)}, f32[2,2,2,32,512]{4,3,2,1,0:T(8,128)S(1)}, u32[]{:S(2)}, u32[]{:S(2)}) collective-permute-start(f32[2,2,2,32,512]{4,3,2,1,0:T(8,128)S(1)} %maximum_select_fusion.2), channel_id=1, source_target_pairs={{0,2},{2,0},{4,6},{6,4},{8,10},{10,8},{12,14},{14,12},{16,18},{18,... | collective-permute-start | bytes 1572872 | tf_op jit(solution)/shard_map/ppermute | solution.py:372
  30.0 5.5 %collective-permute-start.8 = (f32[2,32,512]{2,1,0:T(8,128)S(1)}, f32[2,32,512]{2,1,0:T(8,128)S(1)}, u32[]{:S(2)}, u32[]{:S(2)}) collective-permute-start(f32[2,32,512]{2,1,0:T(8,128)S(1)} %compare_select_fusion.5), channel_id=1, source_target_pairs={{0,8},{2,10},{4,12},{6,14},{8,0},{10,2},{12,4},{14,6},{16,24},{18,... | collective-permute-start | bytes 393224 | tf_op jit(solution)/shard_map/ppermute | solution.py:372
  35.6 8.0 %collective-permute-start.9 = (f32[2,2,32,512]{3,2,1,0:T(8,128)S(1)}, f32[2,2,32,512]{3,2,1,0:T(8,128)S(1)}, u32[]{:S(2)}, u32[]{:S(2)}) collective-permute-start(f32[2,2,32,512]{3,2,1,0:T(8,128)S(1)} %compare_select_fusion.2), channel_id=1, source_target_pairs={{0,4},{2,6},{4,0},{6,2},{8,12},{10,14},{12,8},{14,10},{16,20},{18,... | collective-permute-start | bytes 786440 | tf_op jit(solution)/shard_map/ppermute | solution.py:372
  41.9 6.5 %copy-start = (f32[256,1024]{1,0:T(8,128)}, f32[256,1024]{1,0:T(8,128)S(1)}, u32[]{:S(2)}) copy-start(f32[256,1024]{1,0:T(8,128)S(1)} %shard_map.69.rest_0_.rest_2_) | copy-start | bytes 3145732
  41.9 32.3 %collective-permute-start.5 = (f32[256,1024]{1,0:T(8,128)S(1)}, f32[256,1024]{1,0:T(8,128)S(1)}, u32[]{:S(2)}, u32[]{:S(2)}) collective-permute-start(f32[256,1024]{1,0:T(8,128)S(1)} %shard_map.69.rest_0_.rest_2_), channel_id=1, source_target_pairs={{0,1},{1,0},{2,3},{3,2},{4,5},{5,4},{6,7},{7,6},{8,9},{9,8},{10,11... | collective-permute-start | bytes 3145736 | tf_op jit(solution)/shard_map/ppermute | solution.py:376
  43.7 4.8 %collective-permute-start.10 = (f32[2,2,2,32,512]{4,3,2,1,0:T(8,128)S(1)}, f32[2,2,2,32,512]{4,3,2,1,0:T(8,128)S(1)}, u32[]{:S(2)}, u32[]{:S(2)}) collective-permute-start(f32[2,2,2,32,512]{4,3,2,1,0:T(8,128)S(1)} %maximum_select_fusion.4), channel_id=1, source_target_pairs={{0,2},{2,0},{4,6},{6,4},{8,10},{10,8},{12,14},{14,12},{16,18},{18,... | collective-permute-start | bytes 1572872 | tf_op jit(solution)/shard_map/ppermute | solution.py:372
  48.4 4.3 %copy-start.2 = (f32[256,1024]{1,0:T(8,128)}, f32[256,1024]{1,0:T(8,128)S(1)}, u32[]{:S(2)}) copy-start(f32[256,1024]{1,0:T(8,128)S(1)} %shard_map.70.rest_3_.rest_0_) | copy-start | bytes 3145732
  52.7 21.5 %copy-start.1 = (f32[256,1024]{1,0:T(8,128)S(1)}, f32[256,1024]{1,0:T(8,128)}, u32[]{:S(2)}) copy-start(f32[256,1024]{1,0:T(8,128)} %copy-done) | copy-start | bytes 3145732
  74.2 7.5 %copy-start.3 = (f32[256,1024]{1,0:T(8,128)S(1)}, f32[256,1024]{1,0:T(8,128)}, u32[]{:S(2)}) copy-start(f32[256,1024]{1,0:T(8,128)} %copy-done.2) | copy-start | bytes 3145732
  78.2 1.6 %collective-permute-start.12 = (f32[2,64,512]{2,1,0:T(8,128)S(1)}, f32[2,64,512]{2,1,0:T(8,128)S(1)}, u32[]{:S(2)}, u32[]{:S(2)}) collective-permute-start(f32[2,64,512]{2,1,0:T(8,128)S(1)} %slice.61), channel_id=1, source_target_pairs={{0,2},{2,0},{4,6},{6,4},{8,10},{10,8},{12,14},{14,12},{16,18},{18,... | collective-permute-start | bytes 786440 | tf_op jit(solution)/shard_map/ppermute | solution.py:372
  79.9 5.6 %collective-permute-start.13 = (f32[64,512]{1,0:T(8,128)S(1)}, f32[64,512]{1,0:T(8,128)S(1)}, u32[]{:S(2)}, u32[]{:S(2)}) collective-permute-start(f32[64,512]{1,0:T(8,128)S(1)} %slice_bitcast_fusion.2), channel_id=1, source_target_pairs={{0,4},{2,6},{4,0},{6,2},{8,12},{10,14},{12,8},{14,10},{16,20},{18,... | collective-permute-start | bytes 393224 | tf_op jit(solution)/shard_map/ppermute | solution.py:372
  81.7 24.9 %collective-permute-start.18 = (f32[256,1024]{1,0:T(8,128)S(1)}, f32[256,1024]{1,0:T(8,128)S(1)}, u32[]{:S(2)}, u32[]{:S(2)}) collective-permute-start(f32[256,1024]{1,0:T(8,128)S(1)} %copy-done.3), channel_id=1, source_target_pairs={{0,1},{1,0},{2,3},{3,2},{4,5},{5,4},{6,7},{7,6},{8,9},{9,8},{10,11... | collective-permute-start | bytes 3145736 | tf_op jit(solution)/shard_map/ppermute | solution.py:376
  85.5 5.0 %collective-permute-start.14 = (f32[64,512]{1,0:T(8,128)S(1)}, f32[64,512]{1,0:T(8,128)S(1)}, u32[]{:S(2)}, u32[]{:S(2)}) collective-permute-start(f32[64,512]{1,0:T(8,128)S(1)} %fusion.2), channel_id=1, source_target_pairs={{0,8},{2,10},{4,12},{6,14},{8,0},{10,2},{12,4},{14,6},{16,24},{18,... | collective-permute-start | bytes 393224 | tf_op jit(solution)/shard_map/ppermute | solution.py:372
  90.6 7.8 %collective-permute-start.15 = (f32[64,512]{1,0:T(8,128)S(1)}, f32[64,512]{1,0:T(8,128)S(1)}, u32[]{:S(2)}, u32[]{:S(2)}) collective-permute-start(f32[64,512]{1,0:T(8,128)S(1)} %add.42), channel_id=1, source_target_pairs={{0,16},{2,18},{4,20},{6,22},{8,24},{10,26},{12,28},{14,30},{16,0},... | collective-permute-start | bytes 393224 | tf_op jit(solution)/shard_map/ppermute | solution.py:372
  98.4 5.0 %collective-permute-start.16 = (f32[64,512]{1,0:T(8,128)S(1)}, f32[64,512]{1,0:T(8,128)S(1)}, u32[]{:S(2)}, u32[]{:S(2)}) collective-permute-start(f32[64,512]{1,0:T(8,128)S(1)} %add.43), channel_id=1, source_target_pairs={{0,4},{2,6},{4,0},{6,2},{8,12},{10,14},{12,8},{14,10},{16,20},{18,... | collective-permute-start | bytes 393224 | tf_op jit(solution)/shard_map/ppermute | solution.py:372
  103.4 1.6 %collective-permute-start.17 = (f32[2,64,512]{2,1,0:T(8,128)S(1)}, f32[2,64,512]{2,1,0:T(8,128)S(1)}, u32[]{:S(2)}, u32[]{:S(2)}) collective-permute-start(f32[2,64,512]{2,1,0:T(8,128)S(1)} %pad_maximum_fusion.1.near_ref), channel_id=1, source_target_pairs={{0,2},{2,0},{4,6},{6,4},{8,10},{10,8},{12,14},{14,12},{16,18},{18,... | collective-permute-start | bytes 786440 | tf_op jit(solution)/shard_map/ppermute | solution.py:372
  110.8 1.8 %collective-permute-start.19 = (f32[2,64,768]{2,1,0:T(8,128)S(1)}, f32[2,64,768]{2,1,0:T(8,128)S(1)}, u32[]{:S(2)}, u32[]{:S(2)}) collective-permute-start(f32[2,64,768]{2,1,0:T(8,128)S(1)} %slice.66), channel_id=1, source_target_pairs={{0,2},{2,0},{4,6},{6,4},{8,10},{10,8},{12,14},{14,12},{16,18},{18,... | collective-permute-start | bytes 1179656 | tf_op jit(solution)/shard_map/ppermute | solution.py:372
  112.6 7.0 %collective-permute-start.20 = (f32[64,768]{1,0:T(8,128)S(1)}, f32[64,768]{1,0:T(8,128)S(1)}, u32[]{:S(2)}, u32[]{:S(2)}) collective-permute-start(f32[64,768]{1,0:T(8,128)S(1)} %slice_bitcast_fusion), channel_id=1, source_target_pairs={{0,4},{2,6},{4,0},{6,2},{8,12},{10,14},{12,8},{14,10},{16,20},{18,... | collective-permute-start | bytes 589832 | tf_op jit(solution)/shard_map/ppermute | solution.py:372
  119.7 6.2 %collective-permute-start.21 = (f32[64,768]{1,0:T(8,128)S(1)}, f32[64,768]{1,0:T(8,128)S(1)}, u32[]{:S(2)}, u32[]{:S(2)}) collective-permute-start(f32[64,768]{1,0:T(8,128)S(1)} %fusion.1), channel_id=1, source_target_pairs={{0,8},{2,10},{4,12},{6,14},{8,0},{10,2},{12,4},{14,6},{16,24},{18,... | collective-permute-start | bytes 589832 | tf_op jit(solution)/shard_map/ppermute | solution.py:372
  125.9 10.4 %collective-permute-start.22 = (f32[64,768]{1,0:T(8,128)S(1)}, f32[64,768]{1,0:T(8,128)S(1)}, u32[]{:S(2)}, u32[]{:S(2)}) collective-permute-start(f32[64,768]{1,0:T(8,128)S(1)} %add.47), channel_id=1, source_target_pairs={{0,16},{2,18},{4,20},{6,22},{8,24},{10,26},{12,28},{14,30},{16,0},... | collective-permute-start | bytes 589832 | tf_op jit(solution)/shard_map/ppermute | solution.py:372
  136.3 5.8 %collective-permute-start.23 = (f32[64,768]{1,0:T(8,128)S(1)}, f32[64,768]{1,0:T(8,128)S(1)}, u32[]{:S(2)}, u32[]{:S(2)}) collective-permute-start(f32[64,768]{1,0:T(8,128)S(1)} %add.48), channel_id=1, source_target_pairs={{0,4},{2,6},{4,0},{6,2},{8,12},{10,14},{12,8},{14,10},{16,20},{18,... | collective-permute-start | bytes 589832 | tf_op jit(solution)/shard_map/ppermute | solution.py:372
  142.1 1.8 %collective-permute-start.24 = (f32[2,64,768]{2,1,0:T(8,128)S(1)}, f32[2,64,768]{2,1,0:T(8,128)S(1)}, u32[]{:S(2)}, u32[]{:S(2)}) collective-permute-start(f32[2,64,768]{2,1,0:T(8,128)S(1)} %pad_maximum_fusion.near_ref), channel_id=1, source_target_pairs={{0,2},{2,0},{4,6},{6,4},{8,10},{10,8},{12,14},{14,12},{16,18},{18,... | collective-permute-start | bytes 1179656 | tf_op jit(solution)/shard_map/ppermute | solution.py:372
  145.3 3.7 %collective-permute-start.25 = (f32[16,128]{1,0:T(8,128)S(1)}, f32[16,128]{1,0:T(8,128)S(1)}, u32[]{:S(2)}, u32[]{:S(2)}) collective-permute-start(f32[16,128]{1,0:T(8,128)S(1)} %get-tuple-element.35.rest_2_), channel_id=1, source_target_pairs={{0,1},{1,0},{2,3},{3,2},{4,5},{5,4},{6,7},{7,6},{8,9},{9,8},{10,11... | collective-permute-start | bytes 24584 | tf_op jit(solution)/shard_map/ppermute | solution.py:376

commit v4 on v3

--- a/solution.py
+++ b/solution.py
@@ -10,10 +10,11 @@
 
 BLOCK = 256
 SHARE = (1, 2)
-LIMIT = 48 << 20
+LIMIT = 28 << 20
+MOST = 60 << 20
+STRIPS = 16
 ROWS = ((1,), (1,))
 ANY = pl.BlockSpec(memory_space=pl.ANY)
-HBM = pl.BlockSpec(memory_space=pltpu.HBM)
 SCALARS = pl.BlockSpec(memory_space=pltpu.SMEM)
 
 
@@ -46,7 +47,7 @@
     return pl.BlockSpec(x.shape, lambda *_: (0,) * len(x.shape))
 
 
-def call(kernel, grid, in_specs, out_specs, out_shape, scratch, flops, size):
+def call(kernel, grid, in_specs, out_specs, out_shape, scratch, flops, size, limit=LIMIT):
     return pl.pallas_call(
         kernel,
         grid=grid,
@@ -54,7 +55,7 @@
         out_specs=out_specs,
         out_shape=out_shape,
         scratch_shapes=scratch,
-        compiler_params=pltpu.CompilerParams(vmem_limit_bytes=LIMIT),
+        compiler_params=pltpu.CompilerParams(vmem_limit_bytes=limit),
         cost_estimate=pl.CostEstimate(flops=flops, bytes_accessed=size, transcendentals=0),
     )
 
@@ -90,8 +91,8 @@
     width = features.shape[1]
     shapes = [f32(steps * rows, width)] + ([f32(last - first, width)] if copied else [])
     return call(
-        kernel, (), [SCALARS, HBM, HBM] + [ANY] * len(order), [pl.BlockSpec(memory_space=pltpu.VMEM)] * len(shapes), shapes,
-        [pltpu.SemaphoreType.DMA((steps * rows + 1,))], 0, 4 * width * (rows * steps + last - first),
+        kernel, (), [SCALARS, ANY, ANY] + [ANY] * len(order), [pl.BlockSpec(memory_space=pltpu.VMEM)] * len(shapes), shapes,
+        [pltpu.SemaphoreType.DMA((steps * rows + 1,))], 0, 4 * width * (rows * steps + last - first), MOST,
     )(batch_index, features, centres, *order)
 
 
@@ -108,33 +109,53 @@
     return dot(jnp.ones((8, x.shape[1]), jnp.float32), x * x, ROWS)[:1]
 
 
-def partial_squares(own, ranges, centres, start, order=()):
-    count = own.shape[0]
-    sizes = [count * (b - a) for a, b in ranges]
-    late = centres.shape[0] - start
+def partial_squares(own, span, centres, start, end, order=()):
+    rows = own.shape[0] * (span[1] - span[0])
 
     def kernel(own_ref, centre_ref, *rest):
-        outs = rest[len(order):]
-        rows = chunk_rows(own_ref, ranges)
-        block = centre_ref[...]
-        square = square_sums(rows) + square_row(block) - 2.0 * dot3([halves(rows)], [halves(block)], ROWS)
-        top = 0
-        for out, size in zip(outs, sizes):
-            out[...] = square[top : top + size]
-            top += size
-
-    total = sum(sizes)
+        part, block = chunk_rows(own_ref, [span]), centre_ref[...]
+        square = square_sums(part) + square_row(block) - 2.0 * dot3([halves(part)], [halves(block)], ROWS)
+        rest[-1][...] = square
+
+    late = end - start
     return call(
         kernel, (late // BLOCK,),
         [whole(own), pl.BlockSpec((BLOCK, own.shape[2]), lambda i: (i + start // BLOCK, 0))] + [ANY] * len(order),
-        [pl.BlockSpec((size, BLOCK), lambda i: (0, i)) for size in sizes],
-        [f32(size, late) for size in sizes],
-        [], 12 * total * late * own.shape[2], 4 * (late * own.shape[2] + total * late),
+        pl.BlockSpec((rows, BLOCK), lambda i: (0, i)), f32(rows, late),
+        [], 6 * rows * late * own.shape[2], 4 * (late * own.shape[2] + rows * late),
     )(own, centres, *order)
 
 
 def padded(outputs):
     return (outputs // 128 + 1) * 128
+
+
+def packs(rows, outputs):
+    half = rows // STRIPS // 2
+    return half % 8 == 0 and rows % 256 == 0 and half <= padded(outputs) - 1 - outputs
+
+
+def inner_columns(rows, outputs):
+    return rows // 2 if packs(rows, outputs) else rows
+
+
+def packed(strip, index, lane):
+    high, rows = strip.shape
+    half = high // 2
+    start = index * high
+
+    def turned(first, to):
+        return pltpu.roll(strip, (to - first) % rows, axis=1)
+
+    if index < STRIPS // 2:
+        rest = turned(start + rows // 2, lane)[:, :128]
+    else:
+        left = turned(start + rows // 2, lane)[half:, :128]
+        right = turned(start + rows // 2 + half, lane)[half:, :128]
+        rest = jnp.concatenate([right, left])
+    column = lax.broadcasted_iota(jnp.int32, rest.shape, 1)
+    used = (column >= lane) & (column < lane + half)
+    return turned(start, 0)[:, : rows // 2], rest, used
 
 
 def add_products(total, kern, coefs, outputs):
@@ -209,20 +230,23 @@
     return list(zip(result[:steps], result[steps:]))
 
 
-def predict(where, early, squares, coefs, targets, width, with_inner, order=()):
+def predict(where, given, squares, start, coefs, targets, width, with_inner, order=()):
     rows, late = squares[0].shape
     outputs, centres = coefs.shape
     columns = padded(outputs) + (rows if with_inner else 0)
     own = targets.shape[0]
     quarter = rows // 4
     steps = late // BLOCK
-    skipped = centres // BLOCK - steps
-    given = [] if early is None else [early[1]]
+    pad = padded(outputs)
+    sent = pad + inner_columns(rows, outputs) if with_inner else columns
+    skipped = start // BLOCK
+    last = start + late == centres
+    given = [] if given is None else [given]
     ins = list(squares) + [coefs, targets] + given + list(order)
 
     def kernel(where_ref, *rest):
         square_refs, rest = rest[: len(squares)], rest[len(squares):]
-        coefs_ref, target_ref = rest[:2]
+        coefs_ref, target_ref = rest[0], rest[1]
         kern_ref, out_ref, total = rest[-3:]
         step = pl.program_id(0)
 
@@ -239,20 +263,29 @@
 
         @pl.when(step == steps - 1)
         def _():
-            mine = pl.ds(pl.multiple_of(where_ref[0] * own, own), own)
-            total[mine, :outputs] -= target_ref[...]
-            for block in range(4):
-                source = pl.multiple_of((where_ref[1] ^ block) * quarter, quarter)
-                out_ref[block] = total[pl.ds(source, quarter), :]
-
+            if last:
+                mine = pl.ds(pl.multiple_of(where_ref[0] * own, own), own)
+                total[mine, :outputs] -= target_ref[...]
+                if sent < columns:
+                    for index in range(STRIPS):
+                        span = pl.ds(index * (rows // STRIPS), rows // STRIPS)
+                        most, rest, used = packed(total[span, pad:], index, outputs % 128)
+                        total[span, pad:sent] = most
+                        total[span, pad - 128 : pad] = jnp.where(used, rest, total[span, pad - 128 : pad])
+                for block in range(4):
+                    source = pl.multiple_of((where_ref[1] ^ block) * quarter, quarter)
+                    out_ref[block] = total[pl.ds(source, quarter), :sent]
+            else:
+                out_ref[...] = total[...]
+
+    shape = f32(4, quarter, sent) if last else f32(rows, columns)
     specs = [SCALARS] + [pl.BlockSpec((rows, BLOCK), lambda i: (0, i)) for _ in squares]
     specs += [pl.BlockSpec((outputs, BLOCK), lambda i: (0, i + skipped)), whole(targets)]
-    specs += [whole(x) for x in given]
-    specs += [ANY] * len(order)
+    specs += [whole(x) for x in given] + [ANY] * len(order)
     return call(
         kernel, (steps,), specs,
-        [pl.BlockSpec((rows, BLOCK), lambda i: (0, i)), pl.BlockSpec((4, quarter, columns), lambda i: (0, 0, 0))],
-        [f32(rows, late), f32(4, quarter, columns)],
+        [pl.BlockSpec((rows, BLOCK), lambda i: (0, i)), whole(shape)],
+        [f32(rows, late), shape],
         [pltpu.VMEM((rows, columns), jnp.float32)],
         6 * rows * late * columns, 4 * late * (outputs + 3 * rows),
     )(where, *ins)
@@ -279,12 +312,26 @@
         if with_inner:
             resid = jnp.where(lax.broadcasted_iota(jnp.int32, resid.shape, 1) < outputs, resid, 0.0)
             rest[0][:8, :] = jnp.broadcast_to(marked, (8, 128))
-            rest[0][8:, :] = jnp.full((8, 128), jnp.sum(inner[...] * dot(resid, resid, ROWS)))
+            alike = dot(resid, resid, ROWS)
+            if inner.shape[1] == rows:
+                square = jnp.sum(inner[...] * alike)
+            else:
+                high = rows // STRIPS
+                sums = jnp.zeros((high, rows // 2), jnp.float32)
+                rests = jnp.zeros((high, 128), jnp.float32)
+                for index in range(STRIPS):
+                    span = slice(index * high, (index + 1) * high)
+                    most, rest_of, used = packed(alike[span], index, outputs % 128)
+                    sums = sums + most * inner[span, :]
+                    rests = rests + jnp.where(used, rest_of * resid_ref[span, pad - 128 :], 0.0)
+                diagonal = lax.broadcasted_iota(jnp.int32, sums.shape, 1) < high
+                square = jnp.sum(jnp.where(diagonal, sums, 2.0 * sums)) + 2.0 * jnp.sum(rests)
+            rest[0][8:, :] = jnp.full((8, 128), square)
         turned_ref[...] = resid.T[:outputs]
         own_ref[...] = resid_ref[pl.ds(pl.multiple_of(where_ref[0] * own, own), own), :][:, :outputs]
 
     shapes = [f32(outputs, rows), f32(own, outputs)] + ([f32(16, 128)] if with_inner else [])
-    scratch = [pltpu.VMEM((rows, rows), jnp.float32)] if with_inner else []
+    scratch = [pltpu.VMEM((rows, near.shape[2] - pad), jnp.float32)] if with_inner else []
     return call(
         kernel, (1,), [SCALARS, whole(near), whole(far)], [whole(x) for x in shapes], shapes,
         scratch + [pltpu.VMEM((rows, pad), jnp.float32)],
@@ -455,26 +502,34 @@
     else:
         own = gather(take(features, centres, batch_index, 0, 0)[0])
 
-    partial = partial_squares(own, ranges[:1], centres, sent)
-    partial = list(partial) + list(partial_squares(own, ranges[1:], centres, sent, partial))
+    most, end = centres.shape[0] - BLOCK, centres.shape[0]
+    partial = [[partial_squares(own, ranges[0], centres, sent, most)]]
+    partial[0].append(partial_squares(own, ranges[0], centres, most, end, partial[0]))
+    partial.append([partial_squares(own, ranges[1], centres, sent, end, partial[0][1:])])
     if pair:
-        squares = [[x, across(x)] for x in partial]
-        early = early_part(own, far, local_rows, centres, fetched, coefs, width, partial)
+        squares = [[[x, across(x)] for x in parts] for parts in partial]
+        early = early_part(own, far, local_rows, centres, fetched, coefs, width, partial[1])
     else:
-        squares = [[lax.psum(x, "out")] for x in partial]
+        squares = [[[lax.psum(x, "out")] for x in parts] for parts in partial]
         early = [None, None]
 
-    def kernels(step, kern):
-        return [kern] if early[step] is None else [early[step][0], kern]
-
-    kern, blocks = predict(where, early[0], squares[0], coefs, targets[0], width, False)
+    def predicted(step, with_inner, order):
+        kerns, out = ([], None) if early[step] is None else ([early[step][0]], early[step][1])
+        start = sent
+        for square in squares[step]:
+            kern, out = predict(where, out, square, start, coefs, targets[step], width, with_inner, order)
+            kerns.append(kern)
+            start += kern.shape[1]
+        return kerns, out
+
+    kerns, blocks = predicted(0, False, [])
     turned, rows, *_ = settle(where, *sum_rest(sum_half(blocks)), outputs, local_rows)
-    kern_next, blocks = predict(where, early[1], squares[1], coefs, targets[1], width, True, [turned])
+    kerns_next, blocks = predicted(1, True, [turned])
     blocks = sum_half(blocks)
-    grad, mark = gradient(kernels(0, kern), turned, blocks.shape[1:], padded(outputs) - 1, [blocks])
+    grad, mark = gradient(kerns, turned, blocks.shape[1:], padded(outputs) - 1, [blocks])
     turned, rows_next, square = settle(where, *sum_rest(blocks, mark), outputs, local_rows)
     parts = [square, across(square)] if pair else [lax.psum(square, "out")]
-    new_coefs = update(coefs, grad, kernels(1, kern_next), turned, parts, batch_total, entries)
+    new_coefs = update(coefs, grad, kerns_next, turned, parts, batch_total, entries)
     return (jnp.stack([rows, rows_next]), new_coefs.T)
 
 

time: 156 us -> 147 us (0.942)
  waiting for transfers between devices: 67.4 us -> 61.2 us
  Pallas kernels: 46.6 us -> 40.7 us
  other arithmetic: 1.7 us -> 4.46 us
    ppermute x6 -> x7, waiting for transfers between devices: 19 us -> 12.1 us  [across(): return lax.ppermute(x, 'out', [(0, 1), (1, 0)])]
    pallas_call x2 -> x3, Pallas kernels: 9.18 us -> 6.72 us  [partial_squares(): call(kernel, (late // BLOCK,), [whole(own), pl.BlockSpec((BLOCK, own.shap...]
    pallas_call x1, Pallas kernels: 6.77 us -> 4.42 us  [update(): call(kernel, (centres // wide,), [block, block, whole(turned)] + specs +...]
    select_n x9, other arithmetic: 0.23 us -> 2.08 us  [after(): return jnp.where(token == token, x, token)]
    pallas_call x2 -> x3, Pallas kernels: 8.06 us -> 6.77 us  [predict(): call(kernel, (steps,), specs, [pl.BlockSpec((rows, BLOCK), lambda i: (0,...]
    ppermute x6 -> x7, starting transfers between devices: 9.62 us -> 10.2 us  [across(): return lax.ppermute(x, 'out', [(0, 1), (1, 0)])]
  transfers between devices with their start and end apart: 26 -> 27, of which waited for: 22 -> 22; matrix products, arithmetic and copies ran while one was open for 1% -> 3% of each run, Pallas kernels for 20% -> 21%
where the time goes in v4:
time: 147 us
  waiting for transfers between devices  61.2 us (42%)
  Pallas kernels  40.7 us (28%)
  starting transfers between devices  37.9 us (26%)
  other arithmetic  4.46 us (3%)
    ppermute x20, waiting for transfers between devices, swap(): return lax.ppermute(x, 'cen', [(i, i ^ bit) for i in range(n)])  49.1 us
    ppermute x20, starting transfers between devices, swap(): return lax.ppermute(x, 'cen', [(i, i ^ bit) for i in range(n)])  27.7 us
    pallas_call x1, Pallas kernels, early_part(): call(kernel, (starts[-1],), [whole(own), whole(far), pl.BlockSpec((BLOCK,...  12.8 us
    ppermute x7, waiting for transfers between devices, across(): return lax.ppermute(x, 'out', [(0, 1), (1, 0)])  12.1 us
    ppermute x7, starting transfers between devices, across(): return lax.ppermute(x, 'out', [(0, 1), (1, 0)])  10.2 us
    pallas_call x3, Pallas kernels, predict(): call(kernel, (steps,), specs, [pl.BlockSpec((rows, BLOCK), lambda i: (0,...  6.77 us
    pallas_call x3, Pallas kernels, partial_squares(): call(kernel, (late // BLOCK,), [whole(own), pl.BlockSpec((BLOCK, own.shap...  6.72 us
    pallas_call x1, Pallas kernels, update(): call(kernel, (centres // wide,), [block, block, whole(turned)] + specs +...  4.42 us
  transfers between devices with their start and end apart: 27, of which 22 were waited for; matrix products, arithmetic and copies ran while one was open for 3% of the time, Pallas kernels for 21%

profile of v4, /device:TPU:0, one launch (start us, length us, event | category | flops | bytes accessed | tf_op | source)
XLA Modules:
  0.0 146.5 jit_solution(17234180368592168064)
XLA Ops:
  0.6 1.1 slice.55.rest_0_
  1.7 3.0 %collective-permute-start = (f32[256,512]{1,0:T(8,128)S(1)}, f32[256,512]{1,0:T(8,128)S(1)}, u32[]{:S(2)}, u32[]{:S(2)}) collective-permute-start(f32[256,512]{1,0:T(8,128)S(1)} %slice.55.rest_0_), channel_id=1, source_target_pairs={{0,1},{1,0},{2,3},{3,2},{4,5},{5,4},{6,7},{7,6},{8,9},{9,8},{10,11... | collective-permute-start | bytes 1572872 | tf_op jit(solution)/shard_map/ppermute | solution.py:423
  4.7 3.6 %shard_map.68 = (f32[32,512]{1,0:T(8,128)}, f32[768,512]{1,0:T(8,128)}) custom-call(s32[2,16]{1,0:T(2,128)} %index.1, f32[2048,512]{1,0:T(8,128)} %table.1, f32[2048,512]{1,0:T(8,128)} %centre_ref.7, f32[256,512]{1,0:T(8,128)} %copy-done.2), custom_call_target="tpu_custom_call" | custom-call | bytes 1638400 | tf_op jit(solution)/shard_map/pallas_call | solution.py:93
  8.3 2.7 %collective-permute-start.1 = (f32[32,512]{1,0:T(8,128)}, f32[32,512]{1,0:T(8,128)S(1)}, u32[]{:S(2)}, u32[]{:S(2)}) collective-permute-start(f32[32,512]{1,0:T(8,128)} %get-tuple-element.21), channel_id=1, source_target_pairs={{0,16},{2,18},{4,20},{6,22},{8,24},{10,26},{12,28},{14,30},{16,0},... | collective-permute-start | bytes 196616 | tf_op jit(solution)/shard_map/ppermute | solution.py:419
  11.0 0.7 collective-permute-start.7
  11.7 1.3 collective-permute-start.12
  13.0 0.1 pad_add_fusion.where_ref
  13.1 4.4 %collective-permute-done.rest_0_ = f32[256,512]{1,0:T(8,128)S(1)} collective-permute-done((f32[256,512]{1,0:T(8,128)S(1)}, f32[256,512]{1,0:T(8,128)S(1)}, u32[]{:S(2)}, u32[]{:S(2)}) %collective-permute-start) | collective-permute-done | bytes 524320 | tf_op jit(solution)/shard_map/ppermute | solution.py:423
  17.5 0.9 compare_select_fusion.7
  18.5 2.2 %collective-permute-start.2 = (f32[2,32,512]{2,1,0:T(8,128)S(1)}, f32[2,32,512]{2,1,0:T(8,128)S(1)}, u32[]{:S(2)}, u32[]{:S(2)}) collective-permute-start(f32[2,32,512]{2,1,0:T(8,128)S(1)} %compare_select_fusion.7), channel_id=1, source_target_pairs={{0,8},{2,10},{4,12},{6,14},{8,0},{10,2},{12,4},{14,6},{16,24},{18,... | collective-permute-start | bytes 393224 | tf_op jit(solution)/shard_map/ppermute | solution.py:419
  20.7 0.9 fusion.5
  21.6 0.9 compare_select_fusion.6
  22.6 1.1 collective-permute-done.2
  23.6 2.0 %collective-permute-start.3 = (f32[2,2,32,512]{3,2,1,0:T(8,128)S(1)}, f32[2,2,32,512]{3,2,1,0:T(8,128)S(1)}, u32[]{:S(2)}, u32[]{:S(2)}) collective-permute-start(f32[2,2,32,512]{3,2,1,0:T(8,128)S(1)} %maximum_select_fusion.6), channel_id=1, source_target_pairs={{0,4},{2,6},{4,0},{6,2},{8,12},{10,14},{12,8},{14,10},{16,20},{18,... | collective-permute-start | bytes 786440 | tf_op jit(solution)/shard_map/ppermute | solution.py:419
  25.7 2.8 %collective-permute-start.8 = (f32[32,512]{1,0:T(8,128)S(1)}, f32[32,512]{1,0:T(8,128)S(1)}, u32[]{:S(2)}, u32[]{:S(2)}) collective-permute-start(f32[32,512]{1,0:T(8,128)S(1)} %compare_select_fusion.8), channel_id=1, source_target_pairs={{0,16},{2,18},{4,20},{6,22},{8,24},{10,26},{12,28},{14,30},{16,0},... | collective-permute-start | bytes 196616 | tf_op jit(solution)/shard_map/ppermute | solution.py:419
  28.5 1.6 %collective-permute-done.3 = f32[2,2,32,512]{3,2,1,0:T(8,128)S(1)} collective-permute-done((f32[2,2,32,512]{3,2,1,0:T(8,128)S(1)}, f32[2,2,32,512]{3,2,1,0:T(8,128)S(1)}, u32[]{:S(2)}, u32[]{:S(2)}) %collective-permute-start.3) | collective-permute-done | bytes 262176 | tf_op jit(solution)/shard_map/ppermute | solution.py:419
  30.2 0.7 collective-permute-done.8
  30.9 1.6 %collective-permute-start.9 = (f32[2,32,512]{2,1,0:T(8,128)S(1)}, f32[2,32,512]{2,1,0:T(8,128)S(1)}, u32[]{:S(2)}, u32[]{:S(2)}) collective-permute-start(f32[2,32,512]{2,1,0:T(8,128)S(1)} %compare_select_fusion.5), channel_id=1, source_target_pairs={{0,8},{2,10},{4,12},{6,14},{8,0},{10,2},{12,4},{14,6},{16,24},{18,... | collective-permute-start | bytes 393224 | tf_op jit(solution)/shard_map/ppermute | solution.py:419
  32.7 0.1 maximum_select_fusion
  32.8 3.7 %collective-permute-done.9 = f32[2,32,512]{2,1,0:T(8,128)S(1)} collective-permute-done((f32[2,32,512]{2,1,0:T(8,128)S(1)}, f32[2,32,512]{2,1,0:T(8,128)S(1)}, u32[]{:S(2)}, u32[]{:S(2)}) %collective-permute-start.9) | collective-permute-done | bytes 131104 | tf_op jit(solution)/shard_map/ppermute | solution.py:419
  36.5 1.7 %collective-permute-start.10 = (f32[2,2,32,512]{3,2,1,0:T(8,128)S(1)}, f32[2,2,32,512]{3,2,1,0:T(8,128)S(1)}, u32[]{:S(2)}, u32[]{:S(2)}) collective-permute-start(f32[2,2,32,512]{3,2,1,0:T(8,128)S(1)} %compare_select_fusion.2), channel_id=1, source_target_pairs={{0,4},{2,6},{4,0},{6,2},{8,12},{10,14},{12,8},{14,10},{16,20},{18,... | collective-permute-start | bytes 786440 | tf_op jit(solution)/shard_map/ppermute | solution.py:419
  38.3 6.1 %collective-permute-done.10 = f32[2,2,32,512]{3,2,1,0:T(8,128)S(1)} collective-permute-done((f32[2,2,32,512]{3,2,1,0:T(8,128)S(1)}, f32[2,2,32,512]{3,2,1,0:T(8,128)S(1)}, u32[]{:S(2)}, u32[]{:S(2)}) %collective-permute-start.10) | collective-permute-done | bytes 262176 | tf_op jit(solution)/shard_map/ppermute | solution.py:419
  44.6 2.5 %shard_map.69.rest_0_ = f32[256,768]{1,0:T(8,128)S(1)} custom-call(f32[16,32,512]{2,1,0:T(8,128)S(1)} %bitcast.76, f32[2048,512]{1,0:T(8,128)S(1)} %copy-done), custom_call_target="tpu_custom_call" | custom-call | flops 603979776 | bytes 2359296 | tf_op jit(solution)/shard_map/pallas_call | solution.py:121
  47.2 1.6 %collective-permute-start.6 = (f32[256,768]{1,0:T(8,128)S(1)}, f32[256,768]{1,0:T(8,128)S(1)}, u32[]{:S(2)}, u32[]{:S(2)}) collective-permute-start(f32[256,768]{1,0:T(8,128)S(1)} %shard_map.69.rest_0_), channel_id=1, source_target_pairs={{0,1},{1,0},{2,3},{3,2},{4,5},{5,4},{6,7},{7,6},{8,9},{9,8},{10,11... | collective-permute-start | bytes 2359304 | tf_op jit(solution)/shard_map/ppermute | solution.py:423
  48.7 0.8 shard_map.70.rest_0_
  49.6 0.6 collective-permute-start.5
  50.2 3.4 %shard_map.71.rest_2_.rest_0_ = f32[256,1024]{1,0:T(8,128)S(1)} custom-call(f32[16,32,512]{2,1,0:T(8,128)S(1)} %bitcast.78, f32[2048,512]{1,0:T(8,128)S(1)} %copy-done, f32[256,256]{1,0:T(8,128)S(1)} %shard_map.70.rest_0_), custom_call_target="tpu_custom_call" | custom-call | flops 805306368 | bytes 3145728 | tf_op jit(solution)/shard_map/pallas_call | solution.py:121
  53.6 0.1 maximum_select_fusion.1
  53.8 12.8 %shard_map.72 = (f32[256,1024]{1,0:T(8,128)S(1)}, f32[256,1024]{1,0:T(8,128)S(1)}, f32[256,512]{1,0:T(8,128)S(1)}, f32[256,768]{1,0:T(8,128)S(1)}) custom-call(f32[16,32,512]{2,1,0:T(8,128)S(1)} %bitcast.79, f32[16,32,512]{2,1,0:T(8,128)S(1)} %bitcast.80, f32[2048,512]{1,0:T(8,128)S(1)} %copy-done, f32[500,2048]{1,0:T(8,128)S(1)} %bitcast.71, ...), custom_call_target="tpu_custom_call" | custom-call | flops 3221225472 | bytes 6291456 | tf_op jit(solution)/shard_map/pallas_call | solution.py:221
  66.6 2.9 %collective-permute-done.6.rest_1_ = f32[256,768]{1,0:T(8,128)S(1)} collective-permute-done((f32[256,768]{1,0:T(8,128)S(1)}, f32[256,768]{1,0:T(8,128)S(1)}, u32[]{:S(2)}, u32[]{:S(2)}) %collective-permute-start.6) | collective-permute-done | bytes 786464 | tf_op jit(solution)/shard_map/ppermute | solution.py:423
  69.5 2.3 %shard_map.73 = (f32[256,768]{1,0:T(8,128)S(1)}, f32[256,512]{1,0:T(8,128)S(1)}) custom-call(s32[2]{0:T(128)S(1)} %pad_add_fusion.where_ref, f32[256,768]{1,0:T(8,128)S(1)} %shard_map.69.rest_0_, f32[256,768]{1,0:T(8,128)S(1)} %collective-permute-done.6.rest_1_, f32[500,2048]{1,0:T(8,128)S(1)} %bitcast.72, f32[16,500]{1,0:T(8,128)S(1)} %get-tuple-element.41.rest_3_, ...), custom_call_target="tpu_custom_call" | custom-call | flops 603979776 | bytes 3895296 | tf_op jit(solution)/shard_map/pallas_call | solution.py:285
  71.7 2.5 %collective-permute-done.5.rest_1_ = f32[256,256]{1,0:T(8,128)S(1)} collective-permute-done((f32[256,256]{1,0:T(8,128)S(1)}, f32[256,256]{1,0:T(8,128)S(1)}, u32[]{:S(2)}, u32[]{:S(2)}) %collective-permute-start.5) | collective-permute-done | bytes 262176 | tf_op jit(solution)/shard_map/ppermute | solution.py:423
  74.2 1.1 shard_map.74
  75.3 0.1 collective-permute-start.13
  75.4 1.5 %collective-permute-done.13 = f32[2,64,512]{2,1,0:T(8,128)S(1)} collective-permute-done((f32[2,64,512]{2,1,0:T(8,128)S(1)}, f32[2,64,512]{2,1,0:T(8,128)S(1)}, u32[]{:S(2)}, u32[]{:S(2)}) %collective-permute-start.13) | collective-permute-done | bytes 262176 | tf_op jit(solution)/shard_map/ppermute | solution.py:419
  77.0 1.8 %collective-permute-start.14 = (f32[64,512]{1,0:T(8,128)S(1)}, f32[64,512]{1,0:T(8,128)S(1)}, u32[]{:S(2)}, u32[]{:S(2)}) collective-permute-start(f32[64,512]{1,0:T(8,128)S(1)} %slice_bitcast_fusion.2), channel_id=1, source_target_pairs={{0,4},{2,6},{4,0},{6,2},{8,12},{10,14},{12,8},{14,10},{16,20},{18,... | collective-permute-start | bytes 393224 | tf_op jit(solution)/shard_map/ppermute | solution.py:419
  78.8 1.5 %collective-permute-start.19 = (f32[256,1024]{1,0:T(8,128)S(1)}, f32[256,1024]{1,0:T(8,128)S(1)}, u32[]{:S(2)}, u32[]{:S(2)}) collective-permute-start(f32[256,1024]{1,0:T(8,128)S(1)} %shard_map.71.rest_2_.rest_0_), channel_id=1, source_target_pairs={{0,1},{1,0},{2,3},{3,2},{4,5},{5,4},{6,7},{7,6},{8,9},{9,8},{10,11... | collective-permute-start | bytes 3145736 | tf_op jit(solution)/shard_map/ppermute | solution.py:423
  80.3 2.3 %collective-permute-done.14 = f32[64,512]{1,0:T(8,128)S(1)} collective-permute-done((f32[64,512]{1,0:T(8,128)S(1)}, f32[64,512]{1,0:T(8,128)S(1)}, u32[]{:S(2)}, u32[]{:S(2)}) %collective-permute-start.14) | collective-permute-done | bytes 131104 | tf_op jit(solution)/shard_map/ppermute | solution.py:419
  82.6 1.9 %collective-permute-start.15 = (f32[64,512]{1,0:T(8,128)S(1)}, f32[64,512]{1,0:T(8,128)S(1)}, u32[]{:S(2)}, u32[]{:S(2)}) collective-permute-start(f32[64,512]{1,0:T(8,128)S(1)} %fusion.2), channel_id=1, source_target_pairs={{0,8},{2,10},{4,12},{6,14},{8,0},{10,2},{12,4},{14,6},{16,24},{18,... | collective-permute-start | bytes 393224 | tf_op jit(solution)/shard_map/ppermute | solution.py:419
  84.5 3.2 %collective-permute-done.15 = f32[64,512]{1,0:T(8,128)S(1)} collective-permute-done((f32[64,512]{1,0:T(8,128)S(1)}, f32[64,512]{1,0:T(8,128)S(1)}, u32[]{:S(2)}, u32[]{:S(2)}) %collective-permute-start.15) | collective-permute-done | bytes 131104 | tf_op jit(solution)/shard_map/ppermute | solution.py:419
  87.7 2.9 %collective-permute-start.16 = (f32[64,512]{1,0:T(8,128)S(1)}, f32[64,512]{1,0:T(8,128)S(1)}, u32[]{:S(2)}, u32[]{:S(2)}) collective-permute-start(f32[64,512]{1,0:T(8,128)S(1)} %add.42), channel_id=1, source_target_pairs={{0,16},{2,18},{4,20},{6,22},{8,24},{10,26},{12,28},{14,30},{16,0},... | collective-permute-start | bytes 393224 | tf_op jit(solution)/shard_map/ppermute | solution.py:419
  90.6 4.9 %collective-permute-done.16 = f32[64,512]{1,0:T(8,128)S(1)} collective-permute-done((f32[64,512]{1,0:T(8,128)S(1)}, f32[64,512]{1,0:T(8,128)S(1)}, u32[]{:S(2)}, u32[]{:S(2)}) %collective-permute-start.16) | collective-permute-done | bytes 131104 | tf_op jit(solution)/shard_map/ppermute | solution.py:419
  95.5 1.6 %collective-permute-start.17 = (f32[64,512]{1,0:T(8,128)S(1)}, f32[64,512]{1,0:T(8,128)S(1)}, u32[]{:S(2)}, u32[]{:S(2)}) collective-permute-start(f32[64,512]{1,0:T(8,128)S(1)} %add.43), channel_id=1, source_target_pairs={{0,4},{2,6},{4,0},{6,2},{8,12},{10,14},{12,8},{14,10},{16,20},{18,... | collective-permute-start | bytes 393224 | tf_op jit(solution)/shard_map/ppermute | solution.py:419
  97.2 3.4 %collective-permute-done.17 = f32[64,512]{1,0:T(8,128)S(1)} collective-permute-done((f32[64,512]{1,0:T(8,128)S(1)}, f32[64,512]{1,0:T(8,128)S(1)}, u32[]{:S(2)}, u32[]{:S(2)}) %collective-permute-start.17) | collective-permute-done | bytes 131104 | tf_op jit(solution)/shard_map/ppermute | solution.py:419
  100.6 1.5 %collective-permute-done.18.far_ref = f32[2,64,512]{2,1,0:T(8,128)S(1)} collective-permute-done((f32[2,64,512]{2,1,0:T(8,128)S(1)}, f32[2,64,512]{2,1,0:T(8,128)S(1)}, u32[]{:S(2)}, u32[]{:S(2)}) %collective-permute-start.18) | collective-permute-done | bytes 262176 | tf_op jit(solution)/shard_map/ppermute | solution.py:419
  102.2 0.8 shard_map.75
  102.9 0.8 collective-permute-done.19.rest_1_
  103.7 3.4 %shard_map.76 = (f32[256,1024]{1,0:T(8,128)S(1)}, f32[4,64,640]{2,1,0:T(8,128)S(1)}) custom-call(s32[2]{0:T(128)S(1)} %pad_add_fusion.where_ref, f32[256,1024]{1,0:T(8,128)S(1)} %shard_map.71.rest_2_.rest_0_, f32[256,1024]{1,0:T(8,128)S(1)} %collective-permute-done.19.rest_1_, f32[500,2048]{1,0:T(8,128)S(1)} %bitcast.74, ...), custom_call_target="tpu_custom_call" | custom-call | flops 1207959552 | bytes 5193728 | tf_op jit(solution)/shard_map/pallas_call | solution.py:285
  107.3 1.6 %collective-permute-done.20 = f32[2,64,640]{2,1,0:T(8,128)S(1)} collective-permute-done((f32[2,64,640]{2,1,0:T(8,128)S(1)}, f32[2,64,640]{2,1,0:T(8,128)S(1)}, u32[]{:S(2)}, u32[]{:S(2)}) %collective-permute-start.20) | collective-permute-done | bytes 327712 | tf_op jit(solution)/shard_map/ppermute | solution.py:419
  109.0 0.9 collective-permute-start.21
  109.8 4.2 %shard_map.77 = (f32[500,2048]{1,0:T(8,128)S(1)}, f32[64,640]{1,0:T(8,128)S(1)}) custom-call(f32[500,256]{1,0:T(8,128)S(1)} %get-tuple-element.28.rest_5_.turned_ref, f32[256,1024]{1,0:T(8,128)S(1)} %get-tuple-element.30.rest_0_, f32[256,768]{1,0:T(8,128)S(1)} %get-tuple-element.31.rest_1_, f32[256,256]{1,0:T(8,128)S(1)} %get-tuple-element.32.rest_2_, ...), custom_call_target="tpu_custom_call" | custom-call | flops 1572864000 | bytes 6193152 | tf_op jit(solution)/shard_map/pallas_call | solution.py:384
  114.0 1.3 collective-permute-done.21
  115.3 1.6 %collective-permute-start.22 = (f32[64,640]{1,0:T(8,128)S(1)}, f32[64,640]{1,0:T(8,128)S(1)}, u32[]{:S(2)}, u32[]{:S(2)}) collective-permute-start(f32[64,640]{1,0:T(8,128)S(1)} %fusion.1), channel_id=1, source_target_pairs={{0,8},{2,10},{4,12},{6,14},{8,0},{10,2},{12,4},{14,6},{16,24},{18,... | collective-permute-start | bytes 491528 | tf_op jit(solution)/shard_map/ppermute | solution.py:419
  116.9 3.8 %collective-permute-done.22 = f32[64,640]{1,0:T(8,128)S(1)} collective-permute-done((f32[64,640]{1,0:T(8,128)S(1)}, f32[64,640]{1,0:T(8,128)S(1)}, u32[]{:S(2)}, u32[]{:S(2)}) %collective-permute-start.22) | collective-permute-done | bytes 163872 | tf_op jit(solution)/shard_map/ppermute | solution.py:419
  120.8 2.7 %collective-permute-start.23 = (f32[64,640]{1,0:T(8,128)S(1)}, f32[64,640]{1,0:T(8,128)S(1)}, u32[]{:S(2)}, u32[]{:S(2)}) collective-permute-start(f32[64,640]{1,0:T(8,128)S(1)} %add.47), channel_id=1, source_target_pairs={{0,16},{2,18},{4,20},{6,22},{8,24},{10,26},{12,28},{14,30},{16,0},... | collective-permute-start | bytes 491528 | tf_op jit(solution)/shard_map/ppermute | solution.py:419
  123.5 6.3 %collective-permute-done.23 = f32[64,640]{1,0:T(8,128)S(1)} collective-permute-done((f32[64,640]{1,0:T(8,128)S(1)}, f32[64,640]{1,0:T(8,128)S(1)}, u32[]{:S(2)}, u32[]{:S(2)}) %collective-permute-start.23) | collective-permute-done | bytes 163872 | tf_op jit(solution)/shard_map/ppermute | solution.py:419
  129.8 0.9 collective-permute-start.24
  130.7 4.5 %collective-permute-done.24 = f32[64,640]{1,0:T(8,128)S(1)} collective-permute-done((f32[64,640]{1,0:T(8,128)S(1)}, f32[64,640]{1,0:T(8,128)S(1)}, u32[]{:S(2)}, u32[]{:S(2)}) %collective-permute-start.24) | collective-permute-done | bytes 163872 | tf_op jit(solution)/shard_map/ppermute | solution.py:419
  135.3 1.6 %collective-permute-done.25.far_ref = f32[2,64,640]{2,1,0:T(8,128)S(1)} collective-permute-done((f32[2,64,640]{2,1,0:T(8,128)S(1)}, f32[2,64,640]{2,1,0:T(8,128)S(1)}, u32[]{:S(2)}, u32[]{:S(2)}) %collective-permute-start.25) | collective-permute-done | bytes 327712 | tf_op jit(solution)/shard_map/ppermute | solution.py:419
  136.9 1.5 shard_map.78
  138.4 1.6 %collective-permute-start.26 = (f32[16,128]{1,0:T(8,128)S(1)}, f32[16,128]{1,0:T(8,128)S(1)}, u32[]{:S(2)}, u32[]{:S(2)}) collective-permute-start(f32[16,128]{1,0:T(8,128)S(1)} %get-tuple-element.39.rest_2_), channel_id=1, source_target_pairs={{0,1},{1,0},{2,3},{3,2},{4,5},{5,4},{6,7},{7,6},{8,9},{9,8},{10,11... | collective-permute-start | bytes 24584 | tf_op jit(solution)/shard_map/ppermute | solution.py:423
  139.9 0.6 pad_maximum_fusion.2
  140.6 1.5 %collective-permute-done.26.rest_3_ = f32[16,128]{1,0:T(8,128)S(1)} collective-permute-done((f32[16,128]{1,0:T(8,128)S(1)}, f32[16,128]{1,0:T(8,128)S(1)}, u32[]{:S(2)}, u32[]{:S(2)}) %collective-permute-start.26) | collective-permute-done | bytes 8224 | tf_op jit(solution)/shard_map/ppermute | solution.py:423
  142.1 4.4 %shard_map.79 = f32[500,2048]{1,0:T(8,128)} custom-call(f32[500,2048]{1,0:T(8,128)S(1)} %bitcast.75, f32[500,2048]{1,0:T(8,128)S(1)} %get-tuple-element.35.grad_ref, f32[500,256]{1,0:T(8,128)S(1)} %get-tuple-element.36.turned_ref, f32[256,1024]{1,0:T(8,128)S(1)} %get-tuple-element.37.rest_0_, f32[256,1024]{1,0:T(8,128)S(1)} %get-tuple-element.38.rest_1_, ...), custom_call_target="tpu_custom_call" | custom-call | flops 1572864000 | bytes 14385152 | tf_op jit(solution)/shard_map/pallas_call | solution.py:411
  (49 shorter events, 1.1 us)
Async XLA Ops:
  1.7 3.0 %copy-start.2 = (f32[256,512]{1,0:T(8,128)}, f32[256,512]{1,0:T(8,128)S(1)}, u32[]{:S(2)}) copy-start(f32[256,512]{1,0:T(8,128)S(1)} %slice.55.rest_0_) | copy-start | bytes 1572868
  1.7 11.3 %copy-start.3 = (f32[2,16,500]{2,1,0:T(8,128)S(1)}, f32[2,16,500]{2,1,0:T(8,128)}, u32[]{:S(2)}) copy-start(f32[2,16,500]{2,1,0:T(8,128)} %param.9) | copy-start | bytes 192004
  1.7 15.8 %collective-permute-start = (f32[256,512]{1,0:T(8,128)S(1)}, f32[256,512]{1,0:T(8,128)S(1)}, u32[]{:S(2)}, u32[]{:S(2)}) collective-permute-start(f32[256,512]{1,0:T(8,128)S(1)} %slice.55.rest_0_), channel_id=1, source_target_pairs={{0,1},{1,0},{2,3},{3,2},{4,5},{5,4},{6,7},{7,6},{8,9},{9,8},{10,11... | collective-permute-start | bytes 1572872 | tf_op jit(solution)/shard_map/ppermute | solution.py:423
  8.3 9.2 %collective-permute-start.1 = (f32[32,512]{1,0:T(8,128)}, f32[32,512]{1,0:T(8,128)S(1)}, u32[]{:S(2)}, u32[]{:S(2)}) collective-permute-start(f32[32,512]{1,0:T(8,128)} %get-tuple-element.21), channel_id=1, source_target_pairs={{0,16},{2,18},{4,20},{6,22},{8,24},{10,26},{12,28},{14,30},{16,0},... | collective-permute-start | bytes 196616 | tf_op jit(solution)/shard_map/ppermute | solution.py:419
  11.0 14.7 %collective-permute-start.7 = (f32[32,512]{1,0:T(8,128)}, f32[32,512]{1,0:T(8,128)S(1)}, u32[]{:S(2)}, u32[]{:S(2)}) collective-permute-start(f32[32,512]{1,0:T(8,128)} %get-tuple-element.21), channel_id=1, source_target_pairs={{0,1},{1,0},{2,3},{3,2},{4,5},{5,4},{6,7},{7,6},{8,9},{9,8},{10,11... | collective-permute-start | bytes 196616 | tf_op jit(solution)/shard_map/ppermute | solution.py:423
  11.7 42.1 %collective-permute-start.12 = (f32[768,512]{1,0:T(8,128)}, f32[768,512]{1,0:T(8,128)S(1)}, u32[]{:S(2)}, u32[]{:S(2)}) collective-permute-start(f32[768,512]{1,0:T(8,128)} %get-tuple-element.22), channel_id=1, source_target_pairs={{0,1},{1,0},{2,3},{3,2},{4,5},{5,4},{6,7},{7,6},{8,9},{9,8},{10,11... | collective-permute-start | bytes 4718600 | tf_op jit(solution)/shard_map/ppermute | solution.py:423
  18.5 5.2 %collective-permute-start.2 = (f32[2,32,512]{2,1,0:T(8,128)S(1)}, f32[2,32,512]{2,1,0:T(8,128)S(1)}, u32[]{:S(2)}, u32[]{:S(2)}) collective-permute-start(f32[2,32,512]{2,1,0:T(8,128)S(1)} %compare_select_fusion.7), channel_id=1, source_target_pairs={{0,8},{2,10},{4,12},{6,14},{8,0},{10,2},{12,4},{14,6},{16,24},{18,... | collective-permute-start | bytes 393224 | tf_op jit(solution)/shard_map/ppermute | solution.py:419
  23.6 6.4 %collective-permute-start.3 = (f32[2,2,32,512]{3,2,1,0:T(8,128)S(1)}, f32[2,2,32,512]{3,2,1,0:T(8,128)S(1)}, u32[]{:S(2)}, u32[]{:S(2)}) collective-permute-start(f32[2,2,32,512]{3,2,1,0:T(8,128)S(1)} %maximum_select_fusion.6), channel_id=1, source_target_pairs={{0,4},{2,6},{4,0},{6,2},{8,12},{10,14},{12,8},{14,10},{16,20},{18,... | collective-permute-start | bytes 786440 | tf_op jit(solution)/shard_map/ppermute | solution.py:419
  25.7 5.2 %collective-permute-start.8 = (f32[32,512]{1,0:T(8,128)S(1)}, f32[32,512]{1,0:T(8,128)S(1)}, u32[]{:S(2)}, u32[]{:S(2)}) collective-permute-start(f32[32,512]{1,0:T(8,128)S(1)} %compare_select_fusion.8), channel_id=1, source_target_pairs={{0,16},{2,18},{4,20},{6,22},{8,24},{10,26},{12,28},{14,30},{16,0},... | collective-permute-start | bytes 196616 | tf_op jit(solution)/shard_map/ppermute | solution.py:419
  30.1 14.5 %copy-start = (f32[2048,512]{1,0:T(8,128)S(1)}, f32[2048,512]{1,0:T(8,128)}, u32[]{:S(2)}) copy-start(f32[2048,512]{1,0:T(8,128)} %centre_ref.7) | copy-start | bytes 12582916
  30.1 2.5 %collective-permute-start.4 = (f32[2,2,2,32,512]{4,3,2,1,0:T(8,128)S(1)}, f32[2,2,2,32,512]{4,3,2,1,0:T(8,128)S(1)}, u32[]{:S(2)}, u32[]{:S(2)}) collective-permute-start(f32[2,2,2,32,512]{4,3,2,1,0:T(8,128)S(1)} %maximum_select_fusion.2), channel_id=1, source_target_pairs={{0,2},{2,0},{4,6},{6,4},{8,10},{10,8},{12,14},{14,12},{16,18},{18,... | collective-permute-start | bytes 1572872 | tf_op jit(solution)/shard_map/ppermute | solution.py:419
  30.9 5.5 %collective-permute-start.9 = (f32[2,32,512]{2,1,0:T(8,128)S(1)}, f32[2,32,512]{2,1,0:T(8,128)S(1)}, u32[]{:S(2)}, u32[]{:S(2)}) collective-permute-start(f32[2,32,512]{2,1,0:T(8,128)S(1)} %compare_select_fusion.5), channel_id=1, source_target_pairs={{0,8},{2,10},{4,12},{6,14},{8,0},{10,2},{12,4},{14,6},{16,24},{18,... | collective-permute-start | bytes 393224 | tf_op jit(solution)/shard_map/ppermute | solution.py:419
  36.5 7.9 %collective-permute-start.10 = (f32[2,2,32,512]{3,2,1,0:T(8,128)S(1)}, f32[2,2,32,512]{3,2,1,0:T(8,128)S(1)}, u32[]{:S(2)}, u32[]{:S(2)}) collective-permute-start(f32[2,2,32,512]{3,2,1,0:T(8,128)S(1)} %compare_select_fusion.2), channel_id=1, source_target_pairs={{0,4},{2,6},{4,0},{6,2},{8,12},{10,14},{12,8},{14,10},{16,20},{18,... | collective-permute-start | bytes 786440 | tf_op jit(solution)/shard_map/ppermute | solution.py:419
  44.5 9.1 %collective-permute-start.11 = (f32[2,2,2,32,512]{4,3,2,1,0:T(8,128)S(1)}, f32[2,2,2,32,512]{4,3,2,1,0:T(8,128)S(1)}, u32[]{:S(2)}, u32[]{:S(2)}) collective-permute-start(f32[2,2,2,32,512]{4,3,2,1,0:T(8,128)S(1)} %maximum_select_fusion.4), channel_id=1, source_target_pairs={{0,2},{2,0},{4,6},{6,4},{8,10},{10,8},{12,14},{14,12},{16,18},{18,... | collective-permute-start | bytes 1572872 | tf_op jit(solution)/shard_map/ppermute | solution.py:419
  47.2 22.3 %collective-permute-start.6 = (f32[256,768]{1,0:T(8,128)S(1)}, f32[256,768]{1,0:T(8,128)S(1)}, u32[]{:S(2)}, u32[]{:S(2)}) collective-permute-start(f32[256,768]{1,0:T(8,128)S(1)} %shard_map.69.rest_0_), channel_id=1, source_target_pairs={{0,1},{1,0},{2,3},{3,2},{4,5},{5,4},{6,7},{7,6},{8,9},{9,8},{10,11... | collective-permute-start | bytes 2359304 | tf_op jit(solution)/shard_map/ppermute | solution.py:423
  49.6 4.2 %copy-start.1 = (f32[2048,500]{0,1:T(8,128)S(1)}, f32[2048,500]{0,1:T(8,128)}, u32[]{:S(2)}) copy-start(f32[2048,500]{0,1:T(8,128)} %param.7) | copy-start | bytes 12288004
  49.6 24.7 %collective-permute-start.5 = (f32[256,256]{1,0:T(8,128)S(1)}, f32[256,256]{1,0:T(8,128)S(1)}, u32[]{:S(2)}, u32[]{:S(2)}) collective-permute-start(f32[256,256]{1,0:T(8,128)S(1)} %shard_map.70.rest_0_), channel_id=1, source_target_pairs={{0,1},{1,0},{2,3},{3,2},{4,5},{5,4},{6,7},{7,6},{8,9},{9,8},{10,11... | collective-permute-start | bytes 786440 | tf_op jit(solution)/shard_map/ppermute | solution.py:423
  75.3 1.6 %collective-permute-start.13 = (f32[2,64,512]{2,1,0:T(8,128)S(1)}, f32[2,64,512]{2,1,0:T(8,128)S(1)}, u32[]{:S(2)}, u32[]{:S(2)}) collective-permute-start(f32[2,64,512]{2,1,0:T(8,128)S(1)} %slice.62), channel_id=1, source_target_pairs={{0,2},{2,0},{4,6},{6,4},{8,10},{10,8},{12,14},{14,12},{16,18},{18,... | collective-permute-start | bytes 786440 | tf_op jit(solution)/shard_map/ppermute | solution.py:419
  77.0 5.6 %collective-permute-start.14 = (f32[64,512]{1,0:T(8,128)S(1)}, f32[64,512]{1,0:T(8,128)S(1)}, u32[]{:S(2)}, u32[]{:S(2)}) collective-permute-start(f32[64,512]{1,0:T(8,128)S(1)} %slice_bitcast_fusion.2), channel_id=1, source_target_pairs={{0,4},{2,6},{4,0},{6,2},{8,12},{10,14},{12,8},{14,10},{16,20},{18,... | collective-permute-start | bytes 393224 | tf_op jit(solution)/shard_map/ppermute | solution.py:419
  78.8 24.9 %collective-permute-start.19 = (f32[256,1024]{1,0:T(8,128)S(1)}, f32[256,1024]{1,0:T(8,128)S(1)}, u32[]{:S(2)}, u32[]{:S(2)}) collective-permute-start(f32[256,1024]{1,0:T(8,128)S(1)} %shard_map.71.rest_2_.rest_0_), channel_id=1, source_target_pairs={{0,1},{1,0},{2,3},{3,2},{4,5},{5,4},{6,7},{7,6},{8,9},{9,8},{10,11... | collective-permute-start | bytes 3145736 | tf_op jit(solution)/shard_map/ppermute | solution.py:423
  82.6 5.0 %collective-permute-start.15 = (f32[64,512]{1,0:T(8,128)S(1)}, f32[64,512]{1,0:T(8,128)S(1)}, u32[]{:S(2)}, u32[]{:S(2)}) collective-permute-start(f32[64,512]{1,0:T(8,128)S(1)} %fusion.2), channel_id=1, source_target_pairs={{0,8},{2,10},{4,12},{6,14},{8,0},{10,2},{12,4},{14,6},{16,24},{18,... | collective-permute-start | bytes 393224 | tf_op jit(solution)/shard_map/ppermute | solution.py:419
  87.7 7.8 %collective-permute-start.16 = (f32[64,512]{1,0:T(8,128)S(1)}, f32[64,512]{1,0:T(8,128)S(1)}, u32[]{:S(2)}, u32[]{:S(2)}) collective-permute-start(f32[64,512]{1,0:T(8,128)S(1)} %add.42), channel_id=1, source_target_pairs={{0,16},{2,18},{4,20},{6,22},{8,24},{10,26},{12,28},{14,30},{16,0},... | collective-permute-start | bytes 393224 | tf_op jit(solution)/shard_map/ppermute | solution.py:419
  95.5 5.0 %collective-permute-start.17 = (f32[64,512]{1,0:T(8,128)S(1)}, f32[64,512]{1,0:T(8,128)S(1)}, u32[]{:S(2)}, u32[]{:S(2)}) collective-permute-start(f32[64,512]{1,0:T(8,128)S(1)} %add.43), channel_id=1, source_target_pairs={{0,4},{2,6},{4,0},{6,2},{8,12},{10,14},{12,8},{14,10},{16,20},{18,... | collective-permute-start | bytes 393224 | tf_op jit(solution)/shard_map/ppermute | solution.py:419
  100.6 1.6 %collective-permute-start.18 = (f32[2,64,512]{2,1,0:T(8,128)S(1)}, f32[2,64,512]{2,1,0:T(8,128)S(1)}, u32[]{:S(2)}, u32[]{:S(2)}) collective-permute-start(f32[2,64,512]{2,1,0:T(8,128)S(1)} %pad_maximum_fusion.1.near_ref), channel_id=1, source_target_pairs={{0,2},{2,0},{4,6},{6,4},{8,10},{10,8},{12,14},{14,12},{16,18},{18,... | collective-permute-start | bytes 786440 | tf_op jit(solution)/shard_map/ppermute | solution.py:419
  107.2 1.7 %collective-permute-start.20 = (f32[2,64,640]{2,1,0:T(8,128)S(1)}, f32[2,64,640]{2,1,0:T(8,128)S(1)}, u32[]{:S(2)}, u32[]{:S(2)}) collective-permute-start(f32[2,64,640]{2,1,0:T(8,128)S(1)} %slice.67), channel_id=1, source_target_pairs={{0,2},{2,0},{4,6},{6,4},{8,10},{10,8},{12,14},{14,12},{16,18},{18,... | collective-permute-start | bytes 983048 | tf_op jit(solution)/shard_map/ppermute | solution.py:419
  109.0 6.3 %collective-permute-start.21 = (f32[64,640]{1,0:T(8,128)S(1)}, f32[64,640]{1,0:T(8,128)S(1)}, u32[]{:S(2)}, u32[]{:S(2)}) collective-permute-start(f32[64,640]{1,0:T(8,128)S(1)} %slice_bitcast_fusion), channel_id=1, source_target_pairs={{0,4},{2,6},{4,0},{6,2},{8,12},{10,14},{12,8},{14,10},{16,20},{18,... | collective-permute-start | bytes 491528 | tf_op jit(solution)/shard_map/ppermute | solution.py:419
  115.3 5.5 %collective-permute-start.22 = (f32[64,640]{1,0:T(8,128)S(1)}, f32[64,640]{1,0:T(8,128)S(1)}, u32[]{:S(2)}, u32[]{:S(2)}) collective-permute-start(f32[64,640]{1,0:T(8,128)S(1)} %fusion.1), channel_id=1, source_target_pairs={{0,8},{2,10},{4,12},{6,14},{8,0},{10,2},{12,4},{14,6},{16,24},{18,... | collective-permute-start | bytes 491528 | tf_op jit(solution)/shard_map/ppermute | solution.py:419
  120.8 9.0 %collective-permute-start.23 = (f32[64,640]{1,0:T(8,128)S(1)}, f32[64,640]{1,0:T(8,128)S(1)}, u32[]{:S(2)}, u32[]{:S(2)}) collective-permute-start(f32[64,640]{1,0:T(8,128)S(1)} %add.47), channel_id=1, source_target_pairs={{0,16},{2,18},{4,20},{6,22},{8,24},{10,26},{12,28},{14,30},{16,0},... | collective-permute-start | bytes 491528 | tf_op jit(solution)/shard_map/ppermute | solution.py:419
  129.8 5.4 %collective-permute-start.24 = (f32[64,640]{1,0:T(8,128)S(1)}, f32[64,640]{1,0:T(8,128)S(1)}, u32[]{:S(2)}, u32[]{:S(2)}) collective-permute-start(f32[64,640]{1,0:T(8,128)S(1)} %add.48), channel_id=1, source_target_pairs={{0,4},{2,6},{4,0},{6,2},{8,12},{10,14},{12,8},{14,10},{16,20},{18,... | collective-permute-start | bytes 491528 | tf_op jit(solution)/shard_map/ppermute | solution.py:419
  135.2 1.7 %collective-permute-start.25 = (f32[2,64,640]{2,1,0:T(8,128)S(1)}, f32[2,64,640]{2,1,0:T(8,128)S(1)}, u32[]{:S(2)}, u32[]{:S(2)}) collective-permute-start(f32[2,64,640]{2,1,0:T(8,128)S(1)} %pad_maximum_fusion.near_ref), channel_id=1, source_target_pairs={{0,2},{2,0},{4,6},{6,4},{8,10},{10,8},{12,14},{14,12},{16,18},{18,... | collective-permute-start | bytes 983048 | tf_op jit(solution)/shard_map/ppermute | solution.py:419
  138.4 3.7 %collective-permute-start.26 = (f32[16,128]{1,0:T(8,128)S(1)}, f32[16,128]{1,0:T(8,128)S(1)}, u32[]{:S(2)}, u32[]{:S(2)}) collective-permute-start(f32[16,128]{1,0:T(8,128)S(1)} %get-tuple-element.39.rest_2_), channel_id=1, source_target_pairs={{0,1},{1,0},{2,3},{3,2},{4,5},{5,4},{6,7},{7,6},{8,9},{9,8},{10,11... | collective-permute-start | bytes 24584 | tf_op jit(solution)/shard_map/ppermute | solution.py:423

commit v5 on v4

--- a/solution.py
+++ b/solution.py
@@ -236,10 +236,11 @@
     columns = padded(outputs) + (rows if with_inner else 0)
     own = targets.shape[0]
     quarter = rows // 4
-    steps = late // BLOCK
+    wide = math.gcd(late, start, 2 * BLOCK)
+    steps = late // wide
     pad = padded(outputs)
     sent = pad + inner_columns(rows, outputs) if with_inner else columns
-    skipped = start // BLOCK
+    skipped = start // wide
     last = start + late == centres
     given = [] if given is None else [given]
     ins = list(squares) + [coefs, targets] + given + list(order)
@@ -279,12 +280,12 @@
                 out_ref[...] = total[...]
 
     shape = f32(4, quarter, sent) if last else f32(rows, columns)
-    specs = [SCALARS] + [pl.BlockSpec((rows, BLOCK), lambda i: (0, i)) for _ in squares]
-    specs += [pl.BlockSpec((outputs, BLOCK), lambda i: (0, i + skipped)), whole(targets)]
+    specs = [SCALARS] + [pl.BlockSpec((rows, wide), lambda i: (0, i)) for _ in squares]
+    specs += [pl.BlockSpec((outputs, wide), lambda i: (0, i + skipped)), whole(targets)]
     specs += [whole(x) for x in given] + [ANY] * len(order)
     return call(
         kernel, (steps,), specs,
-        [pl.BlockSpec((rows, BLOCK), lambda i: (0, i)), whole(shape)],
+        [pl.BlockSpec((rows, wide), lambda i: (0, i)), whole(shape)],
         [f32(rows, late), shape],
         [pltpu.VMEM((rows, columns), jnp.float32)],
         6 * rows * late * columns, 4 * late * (outputs + 3 * rows),
@@ -502,7 +503,7 @@
     else:
         own = gather(take(features, centres, batch_index, 0, 0)[0])
 
-    most, end = centres.shape[0] - BLOCK, centres.shape[0]
+    most, end = centres.shape[0] - 2 * BLOCK, centres.shape[0]
     partial = [[partial_squares(own, ranges[0], centres, sent, most)]]
     partial[0].append(partial_squares(own, ranges[0], centres, most, end, partial[0]))
     partial.append([partial_squares(own, ranges[1], centres, sent, end, partial[0][1:])])
@@ -523,8 +524,9 @@
         return kerns, out
 
     kerns, blocks = predicted(0, False, [])
-    turned, rows, *_ = settle(where, *sum_rest(sum_half(blocks)), outputs, local_rows)
-    kerns_next, blocks = predicted(1, True, [turned])
+    near, away = sum_rest(sum_half(blocks))
+    turned, rows, *_ = settle(where, near, away, outputs, local_rows)
+    kerns_next, blocks = predicted(1, True, [near])
     blocks = sum_half(blocks)
     grad, mark = gradient(kerns, turned, blocks.shape[1:], padded(outputs) - 1, [blocks])
     turned, rows_next, square = settle(where, *sum_rest(blocks, mark), outputs, local_rows)

time: 147 us -> 144 us (0.980)
  waiting for transfers between devices: 61.2 us -> 58.8 us
  Pallas kernels: 40.7 us -> 38.8 us
  starting transfers between devices: 37.9 us -> 39.7 us
    ppermute x20, waiting for transfers between devices: 49.1 us -> 46.2 us  [swap(): return lax.ppermute(x, 'cen', [(i, i ^ bit) for i in range(n)])]
    ppermute x20, starting transfers between devices: 27.7 us -> 29.3 us  [swap(): return lax.ppermute(x, 'cen', [(i, i ^ bit) for i in range(n)])]
  transfers between devices with their start and end apart: 27 -> 27, of which waited for: 22 -> 19; matrix products, arithmetic and copies ran while one was open for 3% -> 3% of each run, Pallas kernels for 21% -> 20%
where the time goes in v5:
time: 144 us
  waiting for transfers between devices  58.8 us (41%)
  starting transfers between devices  39.7 us (28%)
  Pallas kernels  38.8 us (27%)
  other arithmetic  4.46 us (3%)
    ppermute x20, waiting for transfers between devices, swap(): return lax.ppermute(x, 'cen', [(i, i ^ bit) for i in range(n)])  46.2 us
    ppermute x20, starting transfers between devices, swap(): return lax.ppermute(x, 'cen', [(i, i ^ bit) for i in range(n)])  29.3 us
    pallas_call x1, Pallas kernels, early_part(): call(kernel, (starts[-1],), [whole(own), whole(far), pl.BlockSpec((BLOCK,...  12.8 us
    ppermute x7, waiting for transfers between devices, across(): return lax.ppermute(x, 'out', [(0, 1), (1, 0)])  12.6 us
    ppermute x7, starting transfers between devices, across(): return lax.ppermute(x, 'out', [(0, 1), (1, 0)])  10.4 us
    pallas_call x3, Pallas kernels, partial_squares(): call(kernel, (late // BLOCK,), [whole(own), pl.BlockSpec((BLOCK, own.shap...  6.75 us
    pallas_call x3, Pallas kernels, predict(): call(kernel, (steps,), specs, [pl.BlockSpec((rows, wide), lambda i: (0, i...  5.67 us
    pallas_call x1, Pallas kernels, update(): call(kernel, (centres // wide,), [block, block, whole(turned)] + specs +...  4.42 us
  transfers between devices with their start and end apart: 27, of which 19 were waited for; matrix products, arithmetic and copies ran while one was open for 3% of the time, Pallas kernels for 20%

profile of v5, /device:TPU:0, one launch (start us, length us, event | category | flops | bytes accessed | tf_op | source)
XLA Modules:
  0.0 144.0 jit_solution(2600312550544139527)
XLA Ops:
  0.6 1.1 slice.55.rest_0_
  1.7 3.0 %collective-permute-start = (f32[256,512]{1,0:T(8,128)S(1)}, f32[256,512]{1,0:T(8,128)S(1)}, u32[]{:S(2)}, u32[]{:S(2)}) collective-permute-start(f32[256,512]{1,0:T(8,128)S(1)} %slice.55.rest_0_), channel_id=1, source_target_pairs={{0,1},{1,0},{2,3},{3,2},{4,5},{5,4},{6,7},{7,6},{8,9},{9,8},{10,11... | collective-permute-start | bytes 1572872 | tf_op jit(solution)/shard_map/ppermute | solution.py:424
  4.7 3.6 %shard_map.68 = (f32[32,512]{1,0:T(8,128)}, f32[768,512]{1,0:T(8,128)}) custom-call(s32[2,16]{1,0:T(2,128)} %index.1, f32[2048,512]{1,0:T(8,128)} %table.1, f32[2048,512]{1,0:T(8,128)} %centre_ref.7, f32[256,512]{1,0:T(8,128)} %copy-done.2), custom_call_target="tpu_custom_call" | custom-call | bytes 1638400 | tf_op jit(solution)/shard_map/pallas_call | solution.py:93
  8.3 2.7 %collective-permute-start.1 = (f32[32,512]{1,0:T(8,128)}, f32[32,512]{1,0:T(8,128)S(1)}, u32[]{:S(2)}, u32[]{:S(2)}) collective-permute-start(f32[32,512]{1,0:T(8,128)} %get-tuple-element.21), channel_id=1, source_target_pairs={{0,16},{2,18},{4,20},{6,22},{8,24},{10,26},{12,28},{14,30},{16,0},... | collective-permute-start | bytes 196616 | tf_op jit(solution)/shard_map/ppermute | solution.py:420
  11.0 0.7 collective-permute-start.7
  11.7 1.3 collective-permute-start.12
  13.0 0.1 pad_add_fusion.where_ref
  13.1 4.4 %collective-permute-done.rest_0_ = f32[256,512]{1,0:T(8,128)S(1)} collective-permute-done((f32[256,512]{1,0:T(8,128)S(1)}, f32[256,512]{1,0:T(8,128)S(1)}, u32[]{:S(2)}, u32[]{:S(2)}) %collective-permute-start) | collective-permute-done | bytes 524320 | tf_op jit(solution)/shard_map/ppermute | solution.py:424
  17.5 0.9 compare_select_fusion.7
  18.5 2.2 %collective-permute-start.2 = (f32[2,32,512]{2,1,0:T(8,128)S(1)}, f32[2,32,512]{2,1,0:T(8,128)S(1)}, u32[]{:S(2)}, u32[]{:S(2)}) collective-permute-start(f32[2,32,512]{2,1,0:T(8,128)S(1)} %compare_select_fusion.7), channel_id=1, source_target_pairs={{0,8},{2,10},{4,12},{6,14},{8,0},{10,2},{12,4},{14,6},{16,24},{18,... | collective-permute-start | bytes 393224 | tf_op jit(solution)/shard_map/ppermute | solution.py:420
  20.7 0.9 fusion.5
  21.6 0.9 compare_select_fusion.6
  22.6 1.1 collective-permute-done.2
  23.6 2.0 %collective-permute-start.3 = (f32[2,2,32,512]{3,2,1,0:T(8,128)S(1)}, f32[2,2,32,512]{3,2,1,0:T(8,128)S(1)}, u32[]{:S(2)}, u32[]{:S(2)}) collective-permute-start(f32[2,2,32,512]{3,2,1,0:T(8,128)S(1)} %maximum_select_fusion.6), channel_id=1, source_target_pairs={{0,4},{2,6},{4,0},{6,2},{8,12},{10,14},{12,8},{14,10},{16,20},{18,... | collective-permute-start | bytes 786440 | tf_op jit(solution)/shard_map/ppermute | solution.py:420
  25.7 2.8 %collective-permute-start.8 = (f32[32,512]{1,0:T(8,128)S(1)}, f32[32,512]{1,0:T(8,128)S(1)}, u32[]{:S(2)}, u32[]{:S(2)}) collective-permute-start(f32[32,512]{1,0:T(8,128)S(1)} %compare_select_fusion.8), channel_id=1, source_target_pairs={{0,16},{2,18},{4,20},{6,22},{8,24},{10,26},{12,28},{14,30},{16,0},... | collective-permute-start | bytes 196616 | tf_op jit(solution)/shard_map/ppermute | solution.py:420
  28.5 1.6 %collective-permute-done.3 = f32[2,2,32,512]{3,2,1,0:T(8,128)S(1)} collective-permute-done((f32[2,2,32,512]{3,2,1,0:T(8,128)S(1)}, f32[2,2,32,512]{3,2,1,0:T(8,128)S(1)}, u32[]{:S(2)}, u32[]{:S(2)}) %collective-permute-start.3) | collective-permute-done | bytes 262176 | tf_op jit(solution)/shard_map/ppermute | solution.py:420
  30.1 0.1 collective-permute-start.4
  30.2 0.7 collective-permute-done.8
  30.9 1.6 %collective-permute-start.9 = (f32[2,32,512]{2,1,0:T(8,128)S(1)}, f32[2,32,512]{2,1,0:T(8,128)S(1)}, u32[]{:S(2)}, u32[]{:S(2)}) collective-permute-start(f32[2,32,512]{2,1,0:T(8,128)S(1)} %compare_select_fusion.5), channel_id=1, source_target_pairs={{0,8},{2,10},{4,12},{6,14},{8,0},{10,2},{12,4},{14,6},{16,24},{18,... | collective-permute-start | bytes 393224 | tf_op jit(solution)/shard_map/ppermute | solution.py:420
  32.7 0.1 maximum_select_fusion
  32.8 3.7 %collective-permute-done.9 = f32[2,32,512]{2,1,0:T(8,128)S(1)} collective-permute-done((f32[2,32,512]{2,1,0:T(8,128)S(1)}, f32[2,32,512]{2,1,0:T(8,128)S(1)}, u32[]{:S(2)}, u32[]{:S(2)}) %collective-permute-start.9) | collective-permute-done | bytes 131104 | tf_op jit(solution)/shard_map/ppermute | solution.py:420
  36.5 1.7 %collective-permute-start.10 = (f32[2,2,32,512]{3,2,1,0:T(8,128)S(1)}, f32[2,2,32,512]{3,2,1,0:T(8,128)S(1)}, u32[]{:S(2)}, u32[]{:S(2)}) collective-permute-start(f32[2,2,32,512]{3,2,1,0:T(8,128)S(1)} %compare_select_fusion.2), channel_id=1, source_target_pairs={{0,4},{2,6},{4,0},{6,2},{8,12},{10,14},{12,8},{14,10},{16,20},{18,... | collective-permute-start | bytes 786440 | tf_op jit(solution)/shard_map/ppermute | solution.py:420
  38.3 6.1 %collective-permute-done.10 = f32[2,2,32,512]{3,2,1,0:T(8,128)S(1)} collective-permute-done((f32[2,2,32,512]{3,2,1,0:T(8,128)S(1)}, f32[2,2,32,512]{3,2,1,0:T(8,128)S(1)}, u32[]{:S(2)}, u32[]{:S(2)}) %collective-permute-start.10) | collective-permute-done | bytes 262176 | tf_op jit(solution)/shard_map/ppermute | solution.py:420
  44.5 0.1 collective-permute-start.11
  44.6 1.7 %shard_map.69.rest_0_ = f32[256,512]{1,0:T(8,128)S(1)} custom-call(f32[16,32,512]{2,1,0:T(8,128)S(1)} %bitcast.76, f32[2048,512]{1,0:T(8,128)S(1)} %copy-done), custom_call_target="tpu_custom_call" | custom-call | flops 402653184 | bytes 1572864 | tf_op jit(solution)/shard_map/pallas_call | solution.py:121
  46.3 1.6 %collective-permute-start.6 = (f32[256,512]{1,0:T(8,128)S(1)}, f32[256,512]{1,0:T(8,128)S(1)}, u32[]{:S(2)}, u32[]{:S(2)}) collective-permute-start(f32[256,512]{1,0:T(8,128)S(1)} %shard_map.69.rest_0_), channel_id=1, source_target_pairs={{0,1},{1,0},{2,3},{3,2},{4,5},{5,4},{6,7},{7,6},{8,9},{9,8},{10,11... | collective-permute-start | bytes 1572872 | tf_op jit(solution)/shard_map/ppermute | solution.py:424
  47.9 1.7 %shard_map.70.rest_0_ = f32[256,512]{1,0:T(8,128)S(1)} custom-call(f32[16,32,512]{2,1,0:T(8,128)S(1)} %bitcast.77, f32[2048,512]{1,0:T(8,128)S(1)} %copy-done, f32[256,512]{1,0:T(8,128)S(1)} %shard_map.69.rest_0_), custom_call_target="tpu_custom_call" | custom-call | flops 402653184 | bytes 1572864 | tf_op jit(solution)/shard_map/pallas_call | solution.py:121
  49.6 0.6 collective-permute-start.5
  50.2 3.4 %shard_map.71.rest_2_.rest_0_ = f32[256,1024]{1,0:T(8,128)S(1)} custom-call(f32[16,32,512]{2,1,0:T(8,128)S(1)} %bitcast.78, f32[2048,512]{1,0:T(8,128)S(1)} %copy-done, f32[256,512]{1,0:T(8,128)S(1)} %shard_map.70.rest_0_), custom_call_target="tpu_custom_call" | custom-call | flops 805306368 | bytes 3145728 | tf_op jit(solution)/shard_map/pallas_call | solution.py:121
  53.7 0.1 maximum_select_fusion.1
  53.8 12.8 %shard_map.72 = (f32[256,1024]{1,0:T(8,128)S(1)}, f32[256,1024]{1,0:T(8,128)S(1)}, f32[256,512]{1,0:T(8,128)S(1)}, f32[256,768]{1,0:T(8,128)S(1)}) custom-call(f32[16,32,512]{2,1,0:T(8,128)S(1)} %bitcast.79, f32[16,32,512]{2,1,0:T(8,128)S(1)} %bitcast.80, f32[2048,512]{1,0:T(8,128)S(1)} %copy-done, f32[500,2048]{1,0:T(8,128)S(1)} %bitcast.71, ...), custom_call_target="tpu_custom_call" | custom-call | flops 3221225472 | bytes 6291456 | tf_op jit(solution)/shard_map/pallas_call | solution.py:221
  66.6 1.3 shard_map.73
  67.9 6.3 %collective-permute-done.5.rest_1_ = f32[256,512]{1,0:T(8,128)S(1)} collective-permute-done((f32[256,512]{1,0:T(8,128)S(1)}, f32[256,512]{1,0:T(8,128)S(1)}, u32[]{:S(2)}, u32[]{:S(2)}) %collective-permute-start.5) | collective-permute-done | bytes 524320 | tf_op jit(solution)/shard_map/ppermute | solution.py:424
  74.2 1.3 shard_map.74
  75.7 1.8 %collective-permute-start.19 = (f32[256,1024]{1,0:T(8,128)S(1)}, f32[256,1024]{1,0:T(8,128)S(1)}, u32[]{:S(2)}, u32[]{:S(2)}) collective-permute-start(f32[256,1024]{1,0:T(8,128)S(1)} %shard_map.71.rest_2_.rest_0_), channel_id=1, source_target_pairs={{0,1},{1,0},{2,3},{3,2},{4,5},{5,4},{6,7},{7,6},{8,9},{9,8},{10,11... | collective-permute-start | bytes 3145736 | tf_op jit(solution)/shard_map/ppermute | solution.py:424
  77.6 1.6 %collective-permute-start.14 = (f32[64,512]{1,0:T(8,128)S(1)}, f32[64,512]{1,0:T(8,128)S(1)}, u32[]{:S(2)}, u32[]{:S(2)}) collective-permute-start(f32[64,512]{1,0:T(8,128)S(1)} %slice_bitcast_fusion.2), channel_id=1, source_target_pairs={{0,4},{2,6},{4,0},{6,2},{8,12},{10,14},{12,8},{14,10},{16,20},{18,... | collective-permute-start | bytes 393224 | tf_op jit(solution)/shard_map/ppermute | solution.py:420
  79.1 4.0 %collective-permute-done.14 = f32[64,512]{1,0:T(8,128)S(1)} collective-permute-done((f32[64,512]{1,0:T(8,128)S(1)}, f32[64,512]{1,0:T(8,128)S(1)}, u32[]{:S(2)}, u32[]{:S(2)}) %collective-permute-start.14) | collective-permute-done | bytes 131104 | tf_op jit(solution)/shard_map/ppermute | solution.py:420
  83.2 1.6 %collective-permute-start.15 = (f32[64,512]{1,0:T(8,128)S(1)}, f32[64,512]{1,0:T(8,128)S(1)}, u32[]{:S(2)}, u32[]{:S(2)}) collective-permute-start(f32[64,512]{1,0:T(8,128)S(1)} %fusion.2), channel_id=1, source_target_pairs={{0,8},{2,10},{4,12},{6,14},{8,0},{10,2},{12,4},{14,6},{16,24},{18,... | collective-permute-start | bytes 393224 | tf_op jit(solution)/shard_map/ppermute | solution.py:420
  84.9 3.4 %collective-permute-done.15 = f32[64,512]{1,0:T(8,128)S(1)} collective-permute-done((f32[64,512]{1,0:T(8,128)S(1)}, f32[64,512]{1,0:T(8,128)S(1)}, u32[]{:S(2)}, u32[]{:S(2)}) %collective-permute-start.15) | collective-permute-done | bytes 131104 | tf_op jit(solution)/shard_map/ppermute | solution.py:420
  88.3 2.7 %collective-permute-start.16 = (f32[64,512]{1,0:T(8,128)S(1)}, f32[64,512]{1,0:T(8,128)S(1)}, u32[]{:S(2)}, u32[]{:S(2)}) collective-permute-start(f32[64,512]{1,0:T(8,128)S(1)} %add.42), channel_id=1, source_target_pairs={{0,16},{2,18},{4,20},{6,22},{8,24},{10,26},{12,28},{14,30},{16,0},... | collective-permute-start | bytes 393224 | tf_op jit(solution)/shard_map/ppermute | solution.py:420
  90.9 5.0 %collective-permute-done.16 = f32[64,512]{1,0:T(8,128)S(1)} collective-permute-done((f32[64,512]{1,0:T(8,128)S(1)}, f32[64,512]{1,0:T(8,128)S(1)}, u32[]{:S(2)}, u32[]{:S(2)}) %collective-permute-start.16) | collective-permute-done | bytes 131104 | tf_op jit(solution)/shard_map/ppermute | solution.py:420
  96.0 1.6 %collective-permute-start.17 = (f32[64,512]{1,0:T(8,128)S(1)}, f32[64,512]{1,0:T(8,128)S(1)}, u32[]{:S(2)}, u32[]{:S(2)}) collective-permute-start(f32[64,512]{1,0:T(8,128)S(1)} %add.43), channel_id=1, source_target_pairs={{0,4},{2,6},{4,0},{6,2},{8,12},{10,14},{12,8},{14,10},{16,20},{18,... | collective-permute-start | bytes 393224 | tf_op jit(solution)/shard_map/ppermute | solution.py:420
  97.5 3.4 %collective-permute-done.17 = f32[64,512]{1,0:T(8,128)S(1)} collective-permute-done((f32[64,512]{1,0:T(8,128)S(1)}, f32[64,512]{1,0:T(8,128)S(1)}, u32[]{:S(2)}, u32[]{:S(2)}) %collective-permute-start.17) | collective-permute-done | bytes 131104 | tf_op jit(solution)/shard_map/ppermute | solution.py:420
  101.0 0.3 collective-permute-done.19.rest_1_
  101.3 3.0 %shard_map.76 = (f32[256,1024]{1,0:T(8,128)S(1)}, f32[4,64,640]{2,1,0:T(8,128)S(1)}) custom-call(s32[2]{0:T(128)S(1)} %pad_add_fusion.where_ref, f32[256,1024]{1,0:T(8,128)S(1)} %shard_map.71.rest_2_.rest_0_, f32[256,1024]{1,0:T(8,128)S(1)} %collective-permute-done.19.rest_1_, f32[500,2048]{1,0:T(8,128)S(1)} %bitcast.74, ...), custom_call_target="tpu_custom_call" | custom-call | flops 1207959552 | bytes 5193728 | tf_op jit(solution)/shard_map/pallas_call | solution.py:286
  104.4 0.5 collective-permute-start.18
  104.9 1.1 collective-permute-done.20
  106.1 1.8 %collective-permute-start.21 = (f32[64,640]{1,0:T(8,128)S(1)}, f32[64,640]{1,0:T(8,128)S(1)}, u32[]{:S(2)}, u32[]{:S(2)}) collective-permute-start(f32[64,640]{1,0:T(8,128)S(1)} %slice_bitcast_fusion), channel_id=1, source_target_pairs={{0,4},{2,6},{4,0},{6,2},{8,12},{10,14},{12,8},{14,10},{16,20},{18,... | collective-permute-start | bytes 491528 | tf_op jit(solution)/shard_map/ppermute | solution.py:420
  107.9 0.8 shard_map.75
  108.7 3.3 %shard_map.77 = (f32[500,2048]{1,0:T(8,128)S(1)}, f32[64,640]{1,0:T(8,128)S(1)}) custom-call(f32[500,256]{1,0:T(8,128)S(1)} %get-tuple-element.29.turned_ref, f32[256,1024]{1,0:T(8,128)S(1)} %get-tuple-element.30.rest_0_, f32[256,512]{1,0:T(8,128)S(1)} %get-tuple-element.31.rest_1_, f32[256,512]{1,0:T(8,128)S(1)} %get-tuple-element.32.rest_2_, ...), custom_call_target="tpu_custom_call" | custom-call | flops 1572864000 | bytes 6193152 | tf_op jit(solution)/shard_map/pallas_call | solution.py:385
  112.0 0.4 collective-permute-done.21
  112.4 1.9 %collective-permute-start.22 = (f32[64,640]{1,0:T(8,128)S(1)}, f32[64,640]{1,0:T(8,128)S(1)}, u32[]{:S(2)}, u32[]{:S(2)}) collective-permute-start(f32[64,640]{1,0:T(8,128)S(1)} %fusion.1), channel_id=1, source_target_pairs={{0,8},{2,10},{4,12},{6,14},{8,0},{10,2},{12,4},{14,6},{16,24},{18,... | collective-permute-start | bytes 491528 | tf_op jit(solution)/shard_map/ppermute | solution.py:420
  114.3 3.8 %collective-permute-done.22 = f32[64,640]{1,0:T(8,128)S(1)} collective-permute-done((f32[64,640]{1,0:T(8,128)S(1)}, f32[64,640]{1,0:T(8,128)S(1)}, u32[]{:S(2)}, u32[]{:S(2)}) %collective-permute-start.22) | collective-permute-done | bytes 163872 | tf_op jit(solution)/shard_map/ppermute | solution.py:420
  118.1 2.7 %collective-permute-start.23 = (f32[64,640]{1,0:T(8,128)S(1)}, f32[64,640]{1,0:T(8,128)S(1)}, u32[]{:S(2)}, u32[]{:S(2)}) collective-permute-start(f32[64,640]{1,0:T(8,128)S(1)} %add.47), channel_id=1, source_target_pairs={{0,16},{2,18},{4,20},{6,22},{8,24},{10,26},{12,28},{14,30},{16,0},... | collective-permute-start | bytes 491528 | tf_op jit(solution)/shard_map/ppermute | solution.py:420
  120.8 6.4 %collective-permute-done.23 = f32[64,640]{1,0:T(8,128)S(1)} collective-permute-done((f32[64,640]{1,0:T(8,128)S(1)}, f32[64,640]{1,0:T(8,128)S(1)}, u32[]{:S(2)}, u32[]{:S(2)}) %collective-permute-start.23) | collective-permute-done | bytes 163872 | tf_op jit(solution)/shard_map/ppermute | solution.py:420
  127.2 1.5 %collective-permute-start.24 = (f32[64,640]{1,0:T(8,128)S(1)}, f32[64,640]{1,0:T(8,128)S(1)}, u32[]{:S(2)}, u32[]{:S(2)}) collective-permute-start(f32[64,640]{1,0:T(8,128)S(1)} %add.48), channel_id=1, source_target_pairs={{0,4},{2,6},{4,0},{6,2},{8,12},{10,14},{12,8},{14,10},{16,20},{18,... | collective-permute-start | bytes 491528 | tf_op jit(solution)/shard_map/ppermute | solution.py:420
  128.7 3.9 %collective-permute-done.24 = f32[64,640]{1,0:T(8,128)S(1)} collective-permute-done((f32[64,640]{1,0:T(8,128)S(1)}, f32[64,640]{1,0:T(8,128)S(1)}, u32[]{:S(2)}, u32[]{:S(2)}) %collective-permute-start.24) | collective-permute-done | bytes 163872 | tf_op jit(solution)/shard_map/ppermute | solution.py:420
  132.7 0.1 collective-permute-start.25
  132.7 1.6 %collective-permute-done.25.far_ref = f32[2,64,640]{2,1,0:T(8,128)S(1)} collective-permute-done((f32[2,64,640]{2,1,0:T(8,128)S(1)}, f32[2,64,640]{2,1,0:T(8,128)S(1)}, u32[]{:S(2)}, u32[]{:S(2)}) %collective-permute-start.25) | collective-permute-done | bytes 327712 | tf_op jit(solution)/shard_map/ppermute | solution.py:420
  134.4 1.5 %shard_map.78 = (f32[500,256]{1,0:T(8,128)S(1)}, f32[16,500]{1,0:T(8,128)S(1)}, f32[16,128]{1,0:T(8,128)S(1)}) custom-call(s32[2]{0:T(128)S(1)} %pad_add_fusion.where_ref, f32[2,64,640]{2,1,0:T(8,128)S(1)} %pad_maximum_fusion.near_ref, f32[2,64,640]{2,1,0:T(8,128)S(1)} %collective-permute-done.25.far_ref), custom_call_target="tpu_custom_call" | custom-call | flops 393216000 | bytes 983040 | tf_op jit(solution)/shard_map/pallas_call | solution.py:336
  135.8 1.5 %collective-permute-start.26 = (f32[16,128]{1,0:T(8,128)S(1)}, f32[16,128]{1,0:T(8,128)S(1)}, u32[]{:S(2)}, u32[]{:S(2)}) collective-permute-start(f32[16,128]{1,0:T(8,128)S(1)} %get-tuple-element.39.rest_2_), channel_id=1, source_target_pairs={{0,1},{1,0},{2,3},{3,2},{4,5},{5,4},{6,7},{7,6},{8,9},{9,8},{10,11... | collective-permute-start | bytes 24584 | tf_op jit(solution)/shard_map/ppermute | solution.py:424
  137.3 0.6 pad_maximum_fusion.2
  137.9 1.6 %collective-permute-done.26.rest_3_ = f32[16,128]{1,0:T(8,128)S(1)} collective-permute-done((f32[16,128]{1,0:T(8,128)S(1)}, f32[16,128]{1,0:T(8,128)S(1)}, u32[]{:S(2)}, u32[]{:S(2)}) %collective-permute-start.26) | collective-permute-done | bytes 8224 | tf_op jit(solution)/shard_map/ppermute | solution.py:424
  139.5 4.4 %shard_map.79 = f32[500,2048]{1,0:T(8,128)} custom-call(f32[500,2048]{1,0:T(8,128)S(1)} %bitcast.75, f32[500,2048]{1,0:T(8,128)S(1)} %get-tuple-element.35.grad_ref, f32[500,256]{1,0:T(8,128)S(1)} %get-tuple-element.36.turned_ref, f32[256,1024]{1,0:T(8,128)S(1)} %get-tuple-element.37.rest_0_, f32[256,1024]{1,0:T(8,128)S(1)} %get-tuple-element.38.rest_1_, ...), custom_call_target="tpu_custom_call" | custom-call | flops 1572864000 | bytes 14385152 | tf_op jit(solution)/shard_map/pallas_call | solution.py:412
  (49 shorter events, 0.9 us)
Async XLA Ops:
  1.7 3.0 %copy-start.2 = (f32[256,512]{1,0:T(8,128)}, f32[256,512]{1,0:T(8,128)S(1)}, u32[]{:S(2)}) copy-start(f32[256,512]{1,0:T(8,128)S(1)} %slice.55.rest_0_) | copy-start | bytes 1572868
  1.7 11.3 %copy-start.3 = (f32[2,16,500]{2,1,0:T(8,128)S(1)}, f32[2,16,500]{2,1,0:T(8,128)}, u32[]{:S(2)}) copy-start(f32[2,16,500]{2,1,0:T(8,128)} %param.9) | copy-start | bytes 192004
  1.7 15.8 %collective-permute-start = (f32[256,512]{1,0:T(8,128)S(1)}, f32[256,512]{1,0:T(8,128)S(1)}, u32[]{:S(2)}, u32[]{:S(2)}) collective-permute-start(f32[256,512]{1,0:T(8,128)S(1)} %slice.55.rest_0_), channel_id=1, source_target_pairs={{0,1},{1,0},{2,3},{3,2},{4,5},{5,4},{6,7},{7,6},{8,9},{9,8},{10,11... | collective-permute-start | bytes 1572872 | tf_op jit(solution)/shard_map/ppermute | solution.py:424
  8.3 9.2 %collective-permute-start.1 = (f32[32,512]{1,0:T(8,128)}, f32[32,512]{1,0:T(8,128)S(1)}, u32[]{:S(2)}, u32[]{:S(2)}) collective-permute-start(f32[32,512]{1,0:T(8,128)} %get-tuple-element.21), channel_id=1, source_target_pairs={{0,16},{2,18},{4,20},{6,22},{8,24},{10,26},{12,28},{14,30},{16,0},... | collective-permute-start | bytes 196616 | tf_op jit(solution)/shard_map/ppermute | solution.py:420
  11.0 14.7 %collective-permute-start.7 = (f32[32,512]{1,0:T(8,128)}, f32[32,512]{1,0:T(8,128)S(1)}, u32[]{:S(2)}, u32[]{:S(2)}) collective-permute-start(f32[32,512]{1,0:T(8,128)} %get-tuple-element.21), channel_id=1, source_target_pairs={{0,1},{1,0},{2,3},{3,2},{4,5},{5,4},{6,7},{7,6},{8,9},{9,8},{10,11... | collective-permute-start | bytes 196616 | tf_op jit(solution)/shard_map/ppermute | solution.py:424
  11.7 42.1 %collective-permute-start.12 = (f32[768,512]{1,0:T(8,128)}, f32[768,512]{1,0:T(8,128)S(1)}, u32[]{:S(2)}, u32[]{:S(2)}) collective-permute-start(f32[768,512]{1,0:T(8,128)} %get-tuple-element.22), channel_id=1, source_target_pairs={{0,1},{1,0},{2,3},{3,2},{4,5},{5,4},{6,7},{7,6},{8,9},{9,8},{10,11... | collective-permute-start | bytes 4718600 | tf_op jit(solution)/shard_map/ppermute | solution.py:424
  18.5 5.2 %collective-permute-start.2 = (f32[2,32,512]{2,1,0:T(8,128)S(1)}, f32[2,32,512]{2,1,0:T(8,128)S(1)}, u32[]{:S(2)}, u32[]{:S(2)}) collective-permute-start(f32[2,32,512]{2,1,0:T(8,128)S(1)} %compare_select_fusion.7), channel_id=1, source_target_pairs={{0,8},{2,10},{4,12},{6,14},{8,0},{10,2},{12,4},{14,6},{16,24},{18,... | collective-permute-start | bytes 393224 | tf_op jit(solution)/shard_map/ppermute | solution.py:420
  23.6 6.4 %collective-permute-start.3 = (f32[2,2,32,512]{3,2,1,0:T(8,128)S(1)}, f32[2,2,32,512]{3,2,1,0:T(8,128)S(1)}, u32[]{:S(2)}, u32[]{:S(2)}) collective-permute-start(f32[2,2,32,512]{3,2,1,0:T(8,128)S(1)} %maximum_select_fusion.6), channel_id=1, source_target_pairs={{0,4},{2,6},{4,0},{6,2},{8,12},{10,14},{12,8},{14,10},{16,20},{18,... | collective-permute-start | bytes 786440 | tf_op jit(solution)/shard_map/ppermute | solution.py:420
  25.7 5.2 %collective-permute-start.8 = (f32[32,512]{1,0:T(8,128)S(1)}, f32[32,512]{1,0:T(8,128)S(1)}, u32[]{:S(2)}, u32[]{:S(2)}) collective-permute-start(f32[32,512]{1,0:T(8,128)S(1)} %compare_select_fusion.8), channel_id=1, source_target_pairs={{0,16},{2,18},{4,20},{6,22},{8,24},{10,26},{12,28},{14,30},{16,0},... | collective-permute-start | bytes 196616 | tf_op jit(solution)/shard_map/ppermute | solution.py:420
  30.1 14.5 %copy-start = (f32[2048,512]{1,0:T(8,128)S(1)}, f32[2048,512]{1,0:T(8,128)}, u32[]{:S(2)}) copy-start(f32[2048,512]{1,0:T(8,128)} %centre_ref.7) | copy-start | bytes 12582916
  30.1 2.5 %collective-permute-start.4 = (f32[2,2,2,32,512]{4,3,2,1,0:T(8,128)S(1)}, f32[2,2,2,32,512]{4,3,2,1,0:T(8,128)S(1)}, u32[]{:S(2)}, u32[]{:S(2)}) collective-permute-start(f32[2,2,2,32,512]{4,3,2,1,0:T(8,128)S(1)} %maximum_select_fusion.2), channel_id=1, source_target_pairs={{0,2},{2,0},{4,6},{6,4},{8,10},{10,8},{12,14},{14,12},{16,18},{18,... | collective-permute-start | bytes 1572872 | tf_op jit(solution)/shard_map/ppermute | solution.py:420
  30.9 5.5 %collective-permute-start.9 = (f32[2,32,512]{2,1,0:T(8,128)S(1)}, f32[2,32,512]{2,1,0:T(8,128)S(1)}, u32[]{:S(2)}, u32[]{:S(2)}) collective-permute-start(f32[2,32,512]{2,1,0:T(8,128)S(1)} %compare_select_fusion.5), channel_id=1, source_target_pairs={{0,8},{2,10},{4,12},{6,14},{8,0},{10,2},{12,4},{14,6},{16,24},{18,... | collective-permute-start | bytes 393224 | tf_op jit(solution)/shard_map/ppermute | solution.py:420
  36.5 7.9 %collective-permute-start.10 = (f32[2,2,32,512]{3,2,1,0:T(8,128)S(1)}, f32[2,2,32,512]{3,2,1,0:T(8,128)S(1)}, u32[]{:S(2)}, u32[]{:S(2)}) collective-permute-start(f32[2,2,32,512]{3,2,1,0:T(8,128)S(1)} %compare_select_fusion.2), channel_id=1, source_target_pairs={{0,4},{2,6},{4,0},{6,2},{8,12},{10,14},{12,8},{14,10},{16,20},{18,... | collective-permute-start | bytes 786440 | tf_op jit(solution)/shard_map/ppermute | solution.py:420
  44.5 9.2 %collective-permute-start.11 = (f32[2,2,2,32,512]{4,3,2,1,0:T(8,128)S(1)}, f32[2,2,2,32,512]{4,3,2,1,0:T(8,128)S(1)}, u32[]{:S(2)}, u32[]{:S(2)}) collective-permute-start(f32[2,2,2,32,512]{4,3,2,1,0:T(8,128)S(1)} %maximum_select_fusion.4), channel_id=1, source_target_pairs={{0,2},{2,0},{4,6},{6,4},{8,10},{10,8},{12,14},{14,12},{16,18},{18,... | collective-permute-start | bytes 1572872 | tf_op jit(solution)/shard_map/ppermute | solution.py:420
  46.3 20.3 %collective-permute-start.6 = (f32[256,512]{1,0:T(8,128)S(1)}, f32[256,512]{1,0:T(8,128)S(1)}, u32[]{:S(2)}, u32[]{:S(2)}) collective-permute-start(f32[256,512]{1,0:T(8,128)S(1)} %shard_map.69.rest_0_), channel_id=1, source_target_pairs={{0,1},{1,0},{2,3},{3,2},{4,5},{5,4},{6,7},{7,6},{8,9},{9,8},{10,11... | collective-permute-start | bytes 1572872 | tf_op jit(solution)/shard_map/ppermute | solution.py:424
  49.6 4.2 %copy-start.1 = (f32[2048,500]{0,1:T(8,128)S(1)}, f32[2048,500]{0,1:T(8,128)}, u32[]{:S(2)}) copy-start(f32[2048,500]{0,1:T(8,128)} %param.7) | copy-start | bytes 12288004
  49.6 24.7 %collective-permute-start.5 = (f32[256,512]{1,0:T(8,128)S(1)}, f32[256,512]{1,0:T(8,128)S(1)}, u32[]{:S(2)}, u32[]{:S(2)}) collective-permute-start(f32[256,512]{1,0:T(8,128)S(1)} %shard_map.70.rest_0_), channel_id=1, source_target_pairs={{0,1},{1,0},{2,3},{3,2},{4,5},{5,4},{6,7},{7,6},{8,9},{9,8},{10,11... | collective-permute-start | bytes 1572872 | tf_op jit(solution)/shard_map/ppermute | solution.py:424
  75.6 1.9 %collective-permute-start.13 = (f32[2,64,512]{2,1,0:T(8,128)S(1)}, f32[2,64,512]{2,1,0:T(8,128)S(1)}, u32[]{:S(2)}, u32[]{:S(2)}) collective-permute-start(f32[2,64,512]{2,1,0:T(8,128)S(1)} %slice.62), channel_id=1, source_target_pairs={{0,2},{2,0},{4,6},{6,4},{8,10},{10,8},{12,14},{14,12},{16,18},{18,... | collective-permute-start | bytes 786440 | tf_op jit(solution)/shard_map/ppermute | solution.py:420
  75.7 25.6 %collective-permute-start.19 = (f32[256,1024]{1,0:T(8,128)S(1)}, f32[256,1024]{1,0:T(8,128)S(1)}, u32[]{:S(2)}, u32[]{:S(2)}) collective-permute-start(f32[256,1024]{1,0:T(8,128)S(1)} %shard_map.71.rest_2_.rest_0_), channel_id=1, source_target_pairs={{0,1},{1,0},{2,3},{3,2},{4,5},{5,4},{6,7},{7,6},{8,9},{9,8},{10,11... | collective-permute-start | bytes 3145736 | tf_op jit(solution)/shard_map/ppermute | solution.py:424
  77.6 5.6 %collective-permute-start.14 = (f32[64,512]{1,0:T(8,128)S(1)}, f32[64,512]{1,0:T(8,128)S(1)}, u32[]{:S(2)}, u32[]{:S(2)}) collective-permute-start(f32[64,512]{1,0:T(8,128)S(1)} %slice_bitcast_fusion.2), channel_id=1, source_target_pairs={{0,4},{2,6},{4,0},{6,2},{8,12},{10,14},{12,8},{14,10},{16,20},{18,... | collective-permute-start | bytes 393224 | tf_op jit(solution)/shard_map/ppermute | solution.py:420
  83.2 5.0 %collective-permute-start.15 = (f32[64,512]{1,0:T(8,128)S(1)}, f32[64,512]{1,0:T(8,128)S(1)}, u32[]{:S(2)}, u32[]{:S(2)}) collective-permute-start(f32[64,512]{1,0:T(8,128)S(1)} %fusion.2), channel_id=1, source_target_pairs={{0,8},{2,10},{4,12},{6,14},{8,0},{10,2},{12,4},{14,6},{16,24},{18,... | collective-permute-start | bytes 393224 | tf_op jit(solution)/shard_map/ppermute | solution.py:420
  88.3 7.7 %collective-permute-start.16 = (f32[64,512]{1,0:T(8,128)S(1)}, f32[64,512]{1,0:T(8,128)S(1)}, u32[]{:S(2)}, u32[]{:S(2)}) collective-permute-start(f32[64,512]{1,0:T(8,128)S(1)} %add.42), channel_id=1, source_target_pairs={{0,16},{2,18},{4,20},{6,22},{8,24},{10,26},{12,28},{14,30},{16,0},... | collective-permute-start | bytes 393224 | tf_op jit(solution)/shard_map/ppermute | solution.py:420
  96.0 5.0 %collective-permute-start.17 = (f32[64,512]{1,0:T(8,128)S(1)}, f32[64,512]{1,0:T(8,128)S(1)}, u32[]{:S(2)}, u32[]{:S(2)}) collective-permute-start(f32[64,512]{1,0:T(8,128)S(1)} %add.43), channel_id=1, source_target_pairs={{0,4},{2,6},{4,0},{6,2},{8,12},{10,14},{12,8},{14,10},{16,20},{18,... | collective-permute-start | bytes 393224 | tf_op jit(solution)/shard_map/ppermute | solution.py:420
  104.3 1.7 %collective-permute-start.20 = (f32[2,64,640]{2,1,0:T(8,128)S(1)}, f32[2,64,640]{2,1,0:T(8,128)S(1)}, u32[]{:S(2)}, u32[]{:S(2)}) collective-permute-start(f32[2,64,640]{2,1,0:T(8,128)S(1)} %slice.67), channel_id=1, source_target_pairs={{0,2},{2,0},{4,6},{6,4},{8,10},{10,8},{12,14},{14,12},{16,18},{18,... | collective-permute-start | bytes 983048 | tf_op jit(solution)/shard_map/ppermute | solution.py:420
  104.4 3.5 %collective-permute-start.18 = (f32[2,64,512]{2,1,0:T(8,128)S(1)}, f32[2,64,512]{2,1,0:T(8,128)S(1)}, u32[]{:S(2)}, u32[]{:S(2)}) collective-permute-start(f32[2,64,512]{2,1,0:T(8,128)S(1)} %pad_maximum_fusion.1.near_ref.rest_5_), channel_id=1, source_target_pairs={{0,2},{2,0},{4,6},{6,4},{8,10},{10,8},{12,14},{14,12},{16,18},{18,... | collective-permute-start | bytes 786440 | tf_op jit(solution)/shard_map/ppermute | solution.py:420
  106.1 6.3 %collective-permute-start.21 = (f32[64,640]{1,0:T(8,128)S(1)}, f32[64,640]{1,0:T(8,128)S(1)}, u32[]{:S(2)}, u32[]{:S(2)}) collective-permute-start(f32[64,640]{1,0:T(8,128)S(1)} %slice_bitcast_fusion), channel_id=1, source_target_pairs={{0,4},{2,6},{4,0},{6,2},{8,12},{10,14},{12,8},{14,10},{16,20},{18,... | collective-permute-start | bytes 491528 | tf_op jit(solution)/shard_map/ppermute | solution.py:420
  112.4 5.6 %collective-permute-start.22 = (f32[64,640]{1,0:T(8,128)S(1)}, f32[64,640]{1,0:T(8,128)S(1)}, u32[]{:S(2)}, u32[]{:S(2)}) collective-permute-start(f32[64,640]{1,0:T(8,128)S(1)} %fusion.1), channel_id=1, source_target_pairs={{0,8},{2,10},{4,12},{6,14},{8,0},{10,2},{12,4},{14,6},{16,24},{18,... | collective-permute-start | bytes 491528 | tf_op jit(solution)/shard_map/ppermute | solution.py:420
  118.1 9.1 %collective-permute-start.23 = (f32[64,640]{1,0:T(8,128)S(1)}, f32[64,640]{1,0:T(8,128)S(1)}, u32[]{:S(2)}, u32[]{:S(2)}) collective-permute-start(f32[64,640]{1,0:T(8,128)S(1)} %add.47), channel_id=1, source_target_pairs={{0,16},{2,18},{4,20},{6,22},{8,24},{10,26},{12,28},{14,30},{16,0},... | collective-permute-start | bytes 491528 | tf_op jit(solution)/shard_map/ppermute | solution.py:420
  127.2 5.4 %collective-permute-start.24 = (f32[64,640]{1,0:T(8,128)S(1)}, f32[64,640]{1,0:T(8,128)S(1)}, u32[]{:S(2)}, u32[]{:S(2)}) collective-permute-start(f32[64,640]{1,0:T(8,128)S(1)} %add.48), channel_id=1, source_target_pairs={{0,4},{2,6},{4,0},{6,2},{8,12},{10,14},{12,8},{14,10},{16,20},{18,... | collective-permute-start | bytes 491528 | tf_op jit(solution)/shard_map/ppermute | solution.py:420
  132.7 1.7 %collective-permute-start.25 = (f32[2,64,640]{2,1,0:T(8,128)S(1)}, f32[2,64,640]{2,1,0:T(8,128)S(1)}, u32[]{:S(2)}, u32[]{:S(2)}) collective-permute-start(f32[2,64,640]{2,1,0:T(8,128)S(1)} %pad_maximum_fusion.near_ref), channel_id=1, source_target_pairs={{0,2},{2,0},{4,6},{6,4},{8,10},{10,8},{12,14},{14,12},{16,18},{18,... | collective-permute-start | bytes 983048 | tf_op jit(solution)/shard_map/ppermute | solution.py:420
  135.8 3.7 %collective-permute-start.26 = (f32[16,128]{1,0:T(8,128)S(1)}, f32[16,128]{1,0:T(8,128)S(1)}, u32[]{:S(2)}, u32[]{:S(2)}) collective-permute-start(f32[16,128]{1,0:T(8,128)S(1)} %get-tuple-element.39.rest_2_), channel_id=1, source_target_pairs={{0,1},{1,0},{2,3},{3,2},{4,5},{5,4},{6,7},{7,6},{8,9},{9,8},{10,11... | collective-permute-start | bytes 24584 | tf_op jit(solution)/shard_map/ppermute | solution.py:424
